TPU v7x, 32 devices: a whole 2x2x4 slice. The times are simulated.
32 devices in a mesh: fsdp: 8 (over z, x), seq: 4 (over y, core).
Axes of the slice: x: 2, y: 2, z: 4, core: 2. Of those that a mesh axis runs over, the one named last changes fastest.
Arguments:
- tokens: bfloat16 [8, 1024, 1024], P('fsdp', 'seq'), may hold values from -6 to 6, as said below
- lengths: int32 [8], P('fsdp'), may hold values from 769 to 1024, as said below
- cotangent: bfloat16 [8, 1024, 1024], P('fsdp', 'seq'), may hold values from -6 to 6
- ln1_gain: bfloat16 [2, 1024], P(None, 'fsdp'), may hold values from 0.099609375 to 1.8984375
- ln1_bias: bfloat16 [2, 1024], P(None, 'fsdp'), may hold values from -1.75 to 1.75
- qkv_weight: bfloat16 [2, 1024, 3072], P(None, 'fsdp'), may hold values from -0.1875 to 0.1875
- query_bias: bfloat16 [2, 1024], P(None, 'fsdp'), may hold values from -3 to 3
- value_bias: bfloat16 [2, 1024], P(None, 'fsdp'), may hold values from -3 to 3
- out_weight: bfloat16 [2, 1024, 1024], P(None, 'fsdp'), may hold values from -0.375 to 0.375
- out_bias: bfloat16 [2, 1024], P(None, 'fsdp'), may hold values from -1.75 to 1.75
- ln2_gain: bfloat16 [2, 1024], P(None, 'fsdp'), may hold values from 0.099609375 to 1.8984375
- ln2_bias: bfloat16 [2, 1024], P(None, 'fsdp'), may hold values from -1.75 to 1.75
- up_weight: bfloat16 [2, 1024, 4096], P(None, 'fsdp'), may hold values from -0.1875 to 0.1875
- up_bias: bfloat16 [2, 4096], P(None, 'fsdp'), may hold values from -3 to 3
- down_weight: bfloat16 [2, 4096, 1024], P(None, 'fsdp'), may hold values from -0.09375 to 0.09375
- down_bias: bfloat16 [2, 1024], P(None, 'fsdp'), may hold values from -1.75 to 1.75
Outputs:
- output: bfloat16 [8, 1024, 1024], P('fsdp', 'seq')
- input_grad: float32 [8, 1024, 1024], P('fsdp', 'seq')
- ln1_gain_grad: float32 [2, 1024], P(None, 'fsdp')
- ln1_bias_grad: float32 [2, 1024], P(None, 'fsdp')
- qkv_weight_grad: float32 [2, 1024, 3072], P(None, 'fsdp')
- query_bias_grad: float32 [2, 1024], P(None, 'fsdp')
- value_bias_grad: float32 [2, 1024], P(None, 'fsdp')
- out_weight_grad: float32 [2, 1024, 1024], P(None, 'fsdp')
- out_bias_grad: float32 [2, 1024], P(None, 'fsdp')
- ln2_gain_grad: float32 [2, 1024], P(None, 'fsdp')
- ln2_bias_grad: float32 [2, 1024], P(None, 'fsdp')
- up_weight_grad: float32 [2, 1024, 4096], P(None, 'fsdp')
- up_bias_grad: float32 [2, 4096], P(None, 'fsdp')
- down_weight_grad: float32 [2, 4096, 1024], P(None, 'fsdp')
- down_bias_grad: float32 [2, 1024], P(None, 'fsdp')
Inputs may be any that keep to these rules, and one draw needn't show every extreme that they name: `lengths`: keys at or after a sequence's length are hidden from every query. Every length exceeds three quarters of 1024; in every draw some sequence has exactly 1024. `tokens`: input activations of order one.
All inputs are finite; a program needn't handle non-finite values.
Results may differ from a plain program's by a relative error of at most 0.03.
Values may be sent and summed in bfloat16 or wider, within the bound.
No kernel may reach another device: no remote copies, remote signals or barrier semaphores. Data moves between devices by JAX's collectives and lax.ppermute only.
A program may use at most 320 MiB of HBM per device.

v0:
```python
import jax
import jax.numpy as jnp
from jax import lax
from jax.sharding import PartitionSpec as P

HEADS = 16
HEAD_DIM = 64
LAYERS = 2
BLOCK = 256


EPS = 1e-05
NEG = -1e30


def normalize(inputs, scale_vec, shift_vec):
    center = inputs - jnp.mean(inputs, axis=-1, keepdims=True)
    spread = jnp.mean(center * center, axis=-1, keepdims=True)
    return center * lax.rsqrt(spread + EPS) * scale_vec + shift_vec


def smooth_gelu(values_in):
    inner = 0.7978845608028654 * (values_in + 0.044715 * values_in * values_in * values_in)
    return 0.5 * values_in * (1.0 + jnp.tanh(inner))


def head_slopes():
    return jnp.exp2(-8.0 * (jnp.arange(HEADS, dtype=jnp.float32) + 1.0) / HEADS)


def score_block(queries, query_pos, key_piece, key_pos, seq_length):
    raw_scores = jnp.einsum(
        "qhd,khd->hqk", queries, key_piece, preferred_element_type=jnp.float32
    ) * HEAD_DIM ** (-0.5)
    distance = jnp.abs(query_pos[:, None] - key_pos[None, :]).astype(jnp.float32)
    raw_scores = raw_scores - head_slopes()[:, None, None] * distance[None]
    visible = (key_pos[None, :] // BLOCK <= query_pos[:, None] // BLOCK) & (
        key_pos[None, :] < seq_length
    )
    return (raw_scores, visible[None])


def attend(queries, keys, values, positions, seq_length):
    row_count = queries.shape[0]

    def absorb(carried, pieces, first_key):
        running_max, running_sum, weighted = carried
        key_piece = pieces[0].reshape(-1, HEADS, HEAD_DIM)
        value_piece = pieces[1].reshape(-1, HEADS, HEAD_DIM)
        key_pos = jnp.arange(key_piece.shape[0], dtype=jnp.int32)
        raw_scores, visible = score_block(queries, positions, key_piece, key_pos, seq_length)
        new_max = jnp.maximum(running_max, jnp.max(jnp.where(visible, raw_scores, NEG), axis=-1))
        exp_scores = jnp.where(visible, jnp.exp(raw_scores - new_max[..., None]), 0.0)
        running_sum = jnp.sum(exp_scores, axis=-1)
        weighted = jnp.einsum(
            "hqk,khd->hqd",
            exp_scores.astype(jnp.bfloat16),
            value_piece,
            preferred_element_type=jnp.float32,
        )
        return (new_max, running_sum, weighted)

    start_state = (
        jnp.full((HEADS, row_count), NEG, jnp.float32),
        jnp.zeros((HEADS, row_count), jnp.float32),
        jnp.zeros((HEADS, row_count, HEAD_DIM), jnp.float32),
    )
    running_max, running_sum, weighted = absorb(
        start_state,
        (
            lax.all_gather(keys, "seq", axis=0, tiled=True),
            lax.all_gather(values, "seq", axis=0, tiled=True),
        ),
        jnp.int32(0),
    )
    attended = jnp.transpose(weighted / running_sum[..., None], (1, 0, 2)).reshape(
        row_count, HEADS * HEAD_DIM
    )
    return (attended, running_max + jnp.log(running_sum))


def attend_back(queries, keys, values, grad_att_low, attended, log_total, positions, seq_length):
    row_count = queries.shape[0]
    model_width = HEADS * HEAD_DIM
    seq_total = row_count * lax.axis_size("seq")
    grad_heads = grad_att_low.reshape(row_count, HEADS, HEAD_DIM)
    offset_term = jnp.sum(
        grad_heads.astype(jnp.float32) * attended.reshape(row_count, HEADS, HEAD_DIM), axis=-1
    ).T
    scale_factor = HEAD_DIM ** (-0.5)

    def absorb(carried, pieces, first_key):
        key_piece = pieces[0].reshape(-1, HEADS, HEAD_DIM)
        value_piece = pieces[1].reshape(-1, HEADS, HEAD_DIM)
        piece_rows = key_piece.shape[0]
        key_pos = jnp.arange(piece_rows, dtype=jnp.int32)
        raw_scores, visible = score_block(queries, positions, key_piece, key_pos, seq_length)
        probabilities = jnp.where(visible, jnp.exp(raw_scores - log_total[..., None]), 0.0)
        grad_probs = jnp.einsum(
            "qhd,khd->hqk", grad_heads, value_piece, preferred_element_type=jnp.float32
        )
        grad_scores = (probabilities * (grad_probs - offset_term[..., None])).astype(jnp.bfloat16)
        grad_query = (
            jnp.einsum("hqk,khd->qhd", grad_scores, key_piece, preferred_element_type=jnp.float32)
            * scale_factor
        )
        grad_key_piece = (
            jnp.einsum("hqk,qhd->khd", grad_scores, queries, preferred_element_type=jnp.float32)
            * scale_factor
        )
        grad_value_piece = jnp.einsum(
            "hqk,qhd->khd",
            probabilities.astype(jnp.bfloat16),
            grad_heads,
            preferred_element_type=jnp.float32,
        )
        grad_key_all = grad_key_piece.reshape(piece_rows, model_width)
        grad_value_all = grad_value_piece.reshape(piece_rows, model_width)
        return (grad_query, grad_key_all, grad_value_all)

    start_state = (
        jnp.zeros((row_count, HEADS, HEAD_DIM), jnp.float32),
        jnp.zeros((seq_total, model_width), jnp.float32),
        jnp.zeros((seq_total, model_width), jnp.float32),
    )
    grad_query, grad_key_all, grad_value_all = absorb(
        start_state,
        (
            lax.all_gather(keys, "seq", axis=0, tiled=True),
            lax.all_gather(values, "seq", axis=0, tiled=True),
        ),
        jnp.int32(0),
    )
    grad_keys, grad_values = (
        lax.psum_scatter(
            grad_key_all.astype(jnp.bfloat16), "seq", scatter_dimension=0, tiled=True
        ).astype(jnp.float32),
        lax.psum_scatter(
            grad_value_all.astype(jnp.bfloat16), "seq", scatter_dimension=0, tiled=True
        ).astype(jnp.float32),
    )
    return (grad_query.reshape(row_count, model_width), grad_keys, grad_values)


def as_working(weight_set):
    return tuple((item if item.ndim == 2 else item.astype(jnp.float32) for item in weight_set))


def project(stream, gain_one, shift_one, w_qkv, bias_query, bias_value):
    normed_one = normalize(stream, gain_one, shift_one)
    packed = jnp.dot(normed_one.astype(jnp.bfloat16), w_qkv, preferred_element_type=jnp.float32)
    packed = packed + jnp.concatenate([bias_query, jnp.zeros_like(bias_query), bias_value])
    return (normed_one, packed.astype(jnp.bfloat16))


def layer_forward(stream, weight_set, positions, seq_length):
    (
        gain_one,
        shift_one,
        w_qkv,
        bias_query,
        bias_value,
        w_out,
        bias_out,
        gain_two,
        shift_two,
        w_up,
        bias_up,
        w_down,
        bias_down,
    ) = as_working(weight_set)
    model_width = HEADS * HEAD_DIM
    normed_one, packed_low = project(stream, gain_one, shift_one, w_qkv, bias_query, bias_value)
    queries = packed_low[:, :model_width].reshape(-1, HEADS, HEAD_DIM)
    attended, log_total = attend(
        queries,
        packed_low[:, model_width : 2 * model_width],
        packed_low[:, 2 * model_width :],
        positions,
        seq_length,
    )
    middle = stream + (
        jnp.dot(attended.astype(jnp.bfloat16), w_out, preferred_element_type=jnp.float32) + bias_out
    )
    normed_two = normalize(middle, gain_two, shift_two)
    hidden_pre = (
        jnp.dot(normed_two.astype(jnp.bfloat16), w_up, preferred_element_type=jnp.float32) + bias_up
    )
    hidden_act = smooth_gelu(hidden_pre).astype(jnp.bfloat16)
    result = middle + (jnp.dot(hidden_act, w_down, preferred_element_type=jnp.float32) + bias_down)
    return (result, (stream, attended, log_total))


def layer_backward(grad_out, weight_set, saved, positions, seq_length):
    (
        gain_one,
        shift_one,
        w_qkv,
        bias_query,
        bias_value,
        w_out,
        bias_out,
        gain_two,
        shift_two,
        w_up,
        bias_up,
        w_down,
        bias_down,
    ) = as_working(weight_set)
    stream, attended, log_total = saved
    model_width = HEADS * HEAD_DIM
    normed_one, norm_one_pull = jax.vjp(normalize, stream, gain_one, shift_one)
    packed = jnp.dot(normed_one.astype(jnp.bfloat16), w_qkv, preferred_element_type=jnp.float32)
    packed_low = (
        packed + jnp.concatenate([bias_query, jnp.zeros_like(bias_query), bias_value])
    ).astype(jnp.bfloat16)
    queries = packed_low[:, :model_width].reshape(-1, HEADS, HEAD_DIM)
    attended_low = attended.astype(jnp.bfloat16)
    middle = stream + (jnp.dot(attended_low, w_out, preferred_element_type=jnp.float32) + bias_out)
    normed_two, norm_two_pull = jax.vjp(normalize, middle, gain_two, shift_two)
    normed_two_low = normed_two.astype(jnp.bfloat16)
    hidden_pre = jnp.dot(normed_two_low, w_up, preferred_element_type=jnp.float32) + bias_up
    hidden_act, gelu_pull = jax.vjp(smooth_gelu, hidden_pre)
    hidden_low = hidden_act.astype(jnp.bfloat16)
    grad_down_low = grad_out.astype(jnp.bfloat16)
    grad_down_w = jnp.einsum(
        "tf,td->fd", hidden_low, grad_down_low, preferred_element_type=jnp.float32
    )
    grad_down_b = jnp.sum(grad_down_low, axis=0, dtype=jnp.float32)
    grad_hidden = jnp.einsum("td,fd->tf", grad_down_low, w_down, preferred_element_type=jnp.float32)
    grad_pre_low = gelu_pull(grad_hidden)[0].astype(jnp.bfloat16)
    grad_up_w = jnp.einsum(
        "td,tf->df", normed_two_low, grad_pre_low, preferred_element_type=jnp.float32
    )
    grad_up_b = jnp.sum(grad_pre_low, axis=0, dtype=jnp.float32)
    grad_normed_two = jnp.einsum(
        "tf,df->td", grad_pre_low, w_up, preferred_element_type=jnp.float32
    )
    grad_middle_part, grad_gain_two, grad_shift_two = norm_two_pull(grad_normed_two)
    grad_middle = grad_out + grad_middle_part
    grad_branch_low = grad_middle.astype(jnp.bfloat16)
    grad_out_w = jnp.einsum(
        "td,te->de", attended_low, grad_branch_low, preferred_element_type=jnp.float32
    )
    grad_out_b = jnp.sum(grad_branch_low, axis=0, dtype=jnp.float32)
    grad_att_low = jnp.einsum(
        "te,de->td", grad_branch_low, w_out, preferred_element_type=jnp.float32
    ).astype(jnp.bfloat16)
    grad_query, grad_keys, grad_values = attend_back(
        queries,
        packed_low[:, model_width : 2 * model_width],
        packed_low[:, 2 * model_width :],
        grad_att_low,
        attended,
        log_total,
        positions,
        seq_length,
    )
    grad_packed = jnp.concatenate([grad_query, grad_keys, grad_values], axis=1).astype(jnp.bfloat16)
    normed_one_low = normed_one.astype(jnp.bfloat16)
    grad_qkv_w = jnp.einsum(
        "td,te->de", normed_one_low, grad_packed, preferred_element_type=jnp.float32
    )
    grad_bias_query = jnp.sum(grad_packed[:, :model_width], axis=0, dtype=jnp.float32)
    grad_bias_value = jnp.sum(grad_packed[:, 2 * model_width :], axis=0, dtype=jnp.float32)
    grad_normed_one = jnp.einsum(
        "te,de->td", grad_packed, w_qkv, preferred_element_type=jnp.float32
    )
    grad_stream_part, grad_gain_one, grad_shift_one = norm_one_pull(grad_normed_one)
    grad_stream = grad_middle + grad_stream_part
    local_grads = (
        grad_gain_one,
        grad_shift_one,
        grad_qkv_w,
        grad_bias_query,
        grad_bias_value,
        grad_out_w,
        grad_out_b,
        grad_gain_two,
        grad_shift_two,
        grad_up_w,
        grad_up_b,
        grad_down_w,
        grad_down_b,
    )
    return (grad_stream, local_grads)


def shards(
    tokens,
    lengths,
    cotangent,
    ln1_gain,
    ln1_bias,
    qkv_weight,
    query_bias,
    value_bias,
    out_weight,
    out_bias,
    ln2_gain,
    ln2_bias,
    up_weight,
    up_bias,
    down_weight,
    down_bias,
):
    shard_sets = (
        ln1_gain,
        ln1_bias,
        qkv_weight,
        query_bias,
        value_bias,
        out_weight,
        out_bias,
        ln2_gain,
        ln2_bias,
        up_weight,
        up_bias,
        down_weight,
        down_bias,
    )
    stream = tokens[0].astype(jnp.float32)
    seq_length = lengths[0]
    row_count = stream.shape[0]
    positions = lax.axis_index("seq") * row_count + jnp.arange(row_count, dtype=jnp.int32)
    saved_layers = []
    gathered_layers = []
    for layer_index in range(LAYERS):
        own_shards = tuple((item[layer_index] for item in shard_sets))
        gathered = (
            lax.all_gather(own_shards[0], "fsdp", axis=0, tiled=True),
            lax.all_gather(own_shards[1], "fsdp", axis=0, tiled=True),
            lax.all_gather(own_shards[2], "fsdp", axis=0, tiled=True),
            lax.all_gather(own_shards[3], "fsdp", axis=0, tiled=True),
            lax.all_gather(own_shards[4], "fsdp", axis=0, tiled=True),
            lax.all_gather(own_shards[5], "fsdp", axis=0, tiled=True),
            lax.all_gather(own_shards[6], "fsdp", axis=0, tiled=True),
            lax.all_gather(own_shards[7], "fsdp", axis=0, tiled=True),
            lax.all_gather(own_shards[8], "fsdp", axis=0, tiled=True),
            lax.all_gather(own_shards[9], "fsdp", axis=0, tiled=True),
            lax.all_gather(own_shards[10], "fsdp", axis=0, tiled=True),
            lax.all_gather(own_shards[11], "fsdp", axis=0, tiled=True),
            lax.all_gather(own_shards[12], "fsdp", axis=0, tiled=True),
        )
        gathered_layers.append(gathered)
        stream, saved = layer_forward(stream, gathered, positions, seq_length)
        saved_layers.append(saved)
    result = stream.astype(jnp.bfloat16)[None]
    grad_stream = cotangent[0].astype(jnp.float32)
    layer_grads = [None] * LAYERS
    for layer_index in reversed(range(LAYERS)):
        own_shards = tuple((item[layer_index] for item in shard_sets))
        gathered = (
            lax.all_gather(own_shards[0], "fsdp", axis=0, tiled=True),
            lax.all_gather(own_shards[1], "fsdp", axis=0, tiled=True),
            lax.all_gather(own_shards[2], "fsdp", axis=0, tiled=True),
            lax.all_gather(own_shards[3], "fsdp", axis=0, tiled=True),
            lax.all_gather(own_shards[4], "fsdp", axis=0, tiled=True),
            lax.all_gather(own_shards[5], "fsdp", axis=0, tiled=True),
            lax.all_gather(own_shards[6], "fsdp", axis=0, tiled=True),
            lax.all_gather(own_shards[7], "fsdp", axis=0, tiled=True),
            lax.all_gather(own_shards[8], "fsdp", axis=0, tiled=True),
            lax.all_gather(own_shards[9], "fsdp", axis=0, tiled=True),
            lax.all_gather(own_shards[10], "fsdp", axis=0, tiled=True),
            lax.all_gather(own_shards[11], "fsdp", axis=0, tiled=True),
            lax.all_gather(own_shards[12], "fsdp", axis=0, tiled=True),
        )
        grad_stream, local_grads = layer_backward(
            grad_stream, gathered, saved_layers[layer_index], positions, seq_length
        )
        slices = (
            lax.psum_scatter(
                local_grads[0].astype(jnp.bfloat16), "fsdp", scatter_dimension=0, tiled=True
            ).astype(jnp.float32),
            lax.psum_scatter(
                local_grads[1].astype(jnp.bfloat16), "fsdp", scatter_dimension=0, tiled=True
            ).astype(jnp.float32),
            lax.psum_scatter(
                local_grads[2].astype(jnp.bfloat16), "fsdp", scatter_dimension=0, tiled=True
            ).astype(jnp.float32),
            lax.psum_scatter(
                local_grads[3].astype(jnp.bfloat16), "fsdp", scatter_dimension=0, tiled=True
            ).astype(jnp.float32),
            lax.psum_scatter(
                local_grads[4].astype(jnp.bfloat16), "fsdp", scatter_dimension=0, tiled=True
            ).astype(jnp.float32),
            lax.psum_scatter(
                local_grads[5].astype(jnp.bfloat16), "fsdp", scatter_dimension=0, tiled=True
            ).astype(jnp.float32),
            lax.psum_scatter(
                local_grads[6].astype(jnp.bfloat16), "fsdp", scatter_dimension=0, tiled=True
            ).astype(jnp.float32),
            lax.psum_scatter(
                local_grads[7].astype(jnp.bfloat16), "fsdp", scatter_dimension=0, tiled=True
            ).astype(jnp.float32),
            lax.psum_scatter(
                local_grads[8].astype(jnp.bfloat16), "fsdp", scatter_dimension=0, tiled=True
            ).astype(jnp.float32),
            lax.psum_scatter(
                local_grads[9].astype(jnp.bfloat16), "fsdp", scatter_dimension=0, tiled=True
            ).astype(jnp.float32),
            lax.psum_scatter(
                local_grads[10].astype(jnp.bfloat16), "fsdp", scatter_dimension=0, tiled=True
            ).astype(jnp.float32),
            lax.psum_scatter(
                local_grads[11].astype(jnp.bfloat16), "fsdp", scatter_dimension=0, tiled=True
            ).astype(jnp.float32),
            lax.psum_scatter(
                local_grads[12].astype(jnp.bfloat16), "fsdp", scatter_dimension=0, tiled=True
            ).astype(jnp.float32),
        )
        summed = (
            lax.psum(slices[0].astype(jnp.bfloat16), "seq").astype(jnp.float32),
            lax.psum(slices[1].astype(jnp.bfloat16), "seq").astype(jnp.float32),
            lax.psum(slices[2].astype(jnp.bfloat16), "seq").astype(jnp.float32),
            lax.psum(slices[3].astype(jnp.bfloat16), "seq").astype(jnp.float32),
            lax.psum(slices[4].astype(jnp.bfloat16), "seq").astype(jnp.float32),
            lax.psum(slices[5].astype(jnp.bfloat16), "seq").astype(jnp.float32),
            lax.psum(slices[6].astype(jnp.bfloat16), "seq").astype(jnp.float32),
            lax.psum(slices[7].astype(jnp.bfloat16), "seq").astype(jnp.float32),
            lax.psum(slices[8].astype(jnp.bfloat16), "seq").astype(jnp.float32),
            lax.psum(slices[9].astype(jnp.bfloat16), "seq").astype(jnp.float32),
            lax.psum(slices[10].astype(jnp.bfloat16), "seq").astype(jnp.float32),
            lax.psum(slices[11].astype(jnp.bfloat16), "seq").astype(jnp.float32),
            lax.psum(slices[12].astype(jnp.bfloat16), "seq").astype(jnp.float32),
        )
        layer_grads[layer_index] = summed
    stacked = tuple(
        (
            jnp.stack([layer_grads[layer_index][member] for layer_index in range(LAYERS)])
            for member in range(13)
        )
    )
    return (
        result,
        grad_stream[None],
        stacked[0],
        stacked[1],
        stacked[2],
        stacked[3],
        stacked[4],
        stacked[5],
        stacked[6],
        stacked[7],
        stacked[8],
        stacked[9],
        stacked[10],
        stacked[11],
        stacked[12],
    )


def solution(mesh):
    in_specs = (
        P("fsdp", "seq", None),
        P("fsdp"),
        P("fsdp", "seq", None),
        P(None, "fsdp"),
        P(None, "fsdp"),
        P(None, "fsdp", None),
        P(None, "fsdp"),
        P(None, "fsdp"),
        P(None, "fsdp", None),
        P(None, "fsdp"),
        P(None, "fsdp"),
        P(None, "fsdp"),
        P(None, "fsdp", None),
        P(None, "fsdp"),
        P(None, "fsdp", None),
        P(None, "fsdp"),
    )
    out_specs = (
        P("fsdp", "seq", None),
        P("fsdp", "seq", None),
        P(None, "fsdp"),
        P(None, "fsdp"),
        P(None, "fsdp", None),
        P(None, "fsdp"),
        P(None, "fsdp"),
        P(None, "fsdp", None),
        P(None, "fsdp"),
        P(None, "fsdp"),
        P(None, "fsdp"),
        P(None, "fsdp", None),
        P(None, "fsdp"),
        P(None, "fsdp", None),
        P(None, "fsdp"),
    )
    return jax.shard_map(shards, mesh=mesh, in_specs=in_specs, out_specs=out_specs, check_vma=False)
```

profile of v0, /device:TPU:0, one launch (start us, length us, event | category | flops | bytes accessed | tf_op | source)
XLA Modules:
  0.0 2253.8 jit_solution(17627585776963668294)
XLA Ops:
  10.7 22.2 all-gather.17
  33.7 16.4 all-gather.16
  50.1 18.4 all-gather.4
  68.5 16.5 all-gather.3
  85.7 18.2 all-gather.1
  137.4 18.0 all-gather.14
  172.3 18.0 all-gather.12
  190.3 16.4 all-gather.8
  206.7 18.1 all-gather.7
  224.9 16.3 all-gather.6
  241.2 26.7 %all-gather.10 = bf16[1,4096]{1,0:T(2,128)(2,1)S(1)} all-gather(bf16[1,512]{1,0:T(2,128)(2,1)S(1)} %get-tuple-element.101), channel_id=12, replica_groups=mesh['fsdp'=8,'seq'=4] {'fsdp'}, dimensions={1}, use_global_device_ids=true | all-gather | bytes 9216 | tf_op jit(solution)/shard_map/all_gather | solution.py:341
  297.3 54.3 %all-gather.51.cloned.1.call-done = bf16[1,1024,4096]{2,1,0:T(8,128)(2,1)} async-done(((bf16[1,128,4096]{2,1,0:T(8,128)(2,1)}), bf16[1,1024,4096]{2,1,0:T(8,128)(2,1)}) %all-gather.51.cloned.1.call-update) | async-done | bytes 8388624 | tf_op jit(solution)/shard_map/all_gather | solution.py:340
  359.4 117.9 %all-gather.53.cloned.1.call-done = bf16[1,4096,1024]{2,1,0:T(8,128)(2,1)} async-done(((bf16[1,512,1024]{2,1,0:T(8,128)(2,1)}), bf16[1,4096,1024]{2,1,0:T(8,128)(2,1)}) %all-gather.53.cloned.1.call-update) | async-done | bytes 8388624 | tf_op jit(solution)/shard_map/all_gather | solution.py:342
  485.1 91.7 %all-gather.55.cloned.1.call-done = bf16[1,1024,3072]{2,1,0:T(8,128)(2,1)} async-done(((bf16[1,128,3072]{2,1,0:T(8,128)(2,1)}), bf16[1,1024,3072]{2,1,0:T(8,128)(2,1)}) %all-gather.55.cloned.1.call-update) | async-done | bytes 6291472 | tf_op jit(solution)/shard_map/all_gather | solution.py:333
  585.2 17.6 all-gather.21
  602.8 16.7 all-gather.20
  619.5 17.6 all-gather.19
  637.1 26.2 %all-gather.23 = bf16[1,4096]{1,0:T(2,128)(2,1)S(1)} all-gather(bf16[1,512]{1,0:T(2,128)(2,1)S(1)} %get-tuple-element.100), channel_id=25, replica_groups=mesh['fsdp'=8,'seq'=4] {'fsdp'}, dimensions={1}, use_global_device_ids=true | all-gather | bytes 9216 | tf_op jit(solution)/shard_map/all_gather | solution.py:341
  692.2 113.1 %all-gather.59.cloned.1.call-done = bf16[1,1024,4096]{2,1,0:T(8,128)(2,1)} async-done(((bf16[1,128,4096]{2,1,0:T(8,128)(2,1)}), bf16[1,1024,4096]{2,1,0:T(8,128)(2,1)}) %all-gather.59.cloned.1.call-update) | async-done | bytes 8388624 | tf_op jit(solution)/shard_map/all_gather | solution.py:340
  813.2 117.9 %all-gather.61.cloned.1.call-done = bf16[1,4096,1024]{2,1,0:T(8,128)(2,1)} async-done(((bf16[1,512,1024]{2,1,0:T(8,128)(2,1)}), bf16[1,4096,1024]{2,1,0:T(8,128)(2,1)}) %all-gather.61.cloned.1.call-update) | async-done | bytes 8388624 | tf_op jit(solution)/shard_map/all_gather | solution.py:342
  988.7 34.0 %reduce-scatter.13.cloned.1.call-done = bf16[256,1024]{0,1:T(8,128)(2,1)} async-done(((bf16[1024,1024]{0,1:T(8,128)(2,1)}), bf16[256,1024]{0,1:T(8,128)(2,1)}) %reduce-scatter.13.cloned.1.call-update) | async-done | bytes 524304 | tf_op jit(solution)/shard_map/reduce_scatter | solution.py:135
  1140.1 20.4 all-gather.25
  1169.2 25.4 %reduce-scatter.27.cloned.1.call-done = bf16[128,1024]{1,0:T(8,128)(2,1)} async-done(((bf16[1024,1024]{1,0:T(8,128)(2,1)}), bf16[128,1024]{1,0:T(8,128)(2,1)}) %reduce-scatter.27.cloned.1.call-update) | async-done | bytes 262160 | tf_op jit(solution)/shard_map/reduce_scatter | solution.py:387
  1194.6 70.0 %reduce-scatter.25.cloned.1.call-done = bf16[128,1024]{1,0:T(8,128)(2,1)} async-done(((bf16[1024,1024]{1,0:T(8,128)(2,1)}), bf16[128,1024]{1,0:T(8,128)(2,1)}) %reduce-scatter.25.cloned.1.call-update) | async-done | bytes 262160 | tf_op jit(solution)/shard_map/reduce_scatter | solution.py:387
  1264.6 120.5 %reduce-scatter.23.cloned.1.call-done = bf16[128,3072]{1,0:T(8,128)(2,1)} async-done(((bf16[1024,3072]{1,0:T(8,128)(2,1)}), bf16[128,3072]{1,0:T(8,128)(2,1)}) %reduce-scatter.23.cloned.1.call-update) | async-done | bytes 786448 | tf_op jit(solution)/shard_map/reduce_scatter | solution.py:378
  1385.1 151.7 %reduce-scatter.35.cloned.1.call-done = bf16[512,1024]{1,0:T(8,128)(2,1)} async-done(((bf16[4096,1024]{1,0:T(8,128)(2,1)}), bf16[512,1024]{1,0:T(8,128)(2,1)}) %reduce-scatter.35.cloned.1.call-update) | async-done | bytes 1048592 | tf_op jit(solution)/shard_map/reduce_scatter | solution.py:405
  1536.8 152.1 %reduce-scatter.31.cloned.1.call-done = bf16[128,4096]{1,0:T(8,128)(2,1)} async-done(((bf16[1024,4096]{1,0:T(8,128)(2,1)}), bf16[128,4096]{1,0:T(8,128)(2,1)}) %reduce-scatter.31.cloned.1.call-update) | async-done | bytes 1048592 | tf_op jit(solution)/shard_map/reduce_scatter | solution.py:399
  1688.9 151.7 %reduce-scatter.33.cloned.1.call-done = bf16[512,1024]{1,0:T(8,128)(2,1)} async-done(((bf16[4096,1024]{1,0:T(8,128)(2,1)}), bf16[512,1024]{1,0:T(8,128)(2,1)}) %reduce-scatter.33.cloned.1.call-update) | async-done | bytes 1048592 | tf_op jit(solution)/shard_map/reduce_scatter | solution.py:405
  1840.6 121.0 %reduce-scatter.21.cloned.1.call-done = bf16[128,3072]{1,0:T(8,128)(2,1)} async-done(((bf16[1024,3072]{1,0:T(8,128)(2,1)}), bf16[128,3072]{1,0:T(8,128)(2,1)}) %reduce-scatter.21.cloned.1.call-update) | async-done | bytes 786448 | tf_op jit(solution)/shard_map/reduce_scatter | solution.py:378
  1961.6 152.1 %reduce-scatter.29.cloned.1.call-done = bf16[128,4096]{1,0:T(8,128)(2,1)} async-done(((bf16[1024,4096]{1,0:T(8,128)(2,1)}), bf16[128,4096]{1,0:T(8,128)(2,1)}) %reduce-scatter.29.cloned.1.call-update) | async-done | bytes 1048592 | tf_op jit(solution)/shard_map/reduce_scatter | solution.py:399
  2123.2 35.5 %all-reduce.18 = (bf16[1024]{0:T(1024)(128)(2,1)S(1)}, bf16[1024]{0:T(1024)(128)(2,1)S(1)}, bf16[1024]{0:T(1024)(128)(2,1)S(1)}, bf16[1024]{0:T(1024)(128)(2,1)S...) all-reduce(bf16[1024]{0:T(1024)(128)(2,1)S(1)} %get-tuple-element.1, ...), channel_id=33, replica_groups=mesh['fsdp'=8,'seq'=4] {'fsdp'}, use_global_device_ids=true, to_apply=%region_30.31.clone | all-reduce | flops 24576 | bytes 98304
  2179.2 57.5 %all-reduce.23.cloned.1.call-done = (bf16[1,128,3072]{2,1,0:T(8,128)(2,1)}, bf16[1,128,3072]{2,1,0:T(8,128)(2,1)}, bf16[1,128,1024]{2,1,0:T(8,128)(2,1)}, bf16[1...) async-done(((bf16[1,128,3072]{2,1,0:T(8,128)(2,1)}, ...) | async-done | bytes 6291472 | tf_op jit(solution)/shard_map/psum | solution.py:415
  (354 shorter events, 366.1 us)
Async XLA Ops:
  7.2 113.8 %copy-start.4 = (bf16[1,256,1024]{2,1,0:T(8,128)(2,1)S(1)}, bf16[1,256,1024]{2,1,0:T(8,128)(2,1)}, u32[]{:S(2)}) copy-start(bf16[1,256,1024]{2,1,0:T(8,128)(2,1)} %param.16) | copy-start | bytes 1572868
  7.2 114.3 %all-gather.47.cloned.1.call-start = ((), (), s32[]{:S(2)}) async-start(), calls=%async_computation.28 | async-start | bytes 7077888 | tf_op jit(solution)/shard_map/all_gather | solution.py:333
  9.9 258.8 %all-gather.39.cloned.1.call-start = ((), (), s32[]{:S(2)}) async-start(), calls=%async_computation.12 | async-start | bytes 2621440 | tf_op jit(solution)/shard_map/all_gather | solution.py:71
  127.9 145.1 %all-gather.41.cloned.1.call-start = ((), (), s32[]{:S(2)}) async-start(), calls=%async_computation.13 | async-start | bytes 2621440 | tf_op jit(solution)/shard_map/all_gather | solution.py:72
  128.6 165.8 %all-gather.49.cloned.1.call-start = ((), (), s32[]{:S(2)}) async-start(), calls=%async_computation.29 | async-start | bytes 2359296 | tf_op jit(solution)/shard_map/all_gather | solution.py:336
  129.6 222.0 %all-gather.51.cloned.1.call-start = ((), (), s32[]{:S(2)}) async-start(), calls=%async_computation.30 | async-start | bytes 9437184 | tf_op jit(solution)/shard_map/all_gather | solution.py:340
  132.7 74.0 %copy-start.58 = (bf16[2,128]{1,0:T(2,128)(2,1)S(1)}, bf16[2,128]{1,0:T(2,128)(2,1)}, u32[]{:S(2)}) copy-start(bf16[2,128]{1,0:T(2,128)(2,1)} %param.26) | copy-start | bytes 1540
  132.7 92.2 %copy-start.59 = (bf16[2,128]{1,0:T(2,128)(2,1)S(1)}, bf16[2,128]{1,0:T(2,128)(2,1)}, u32[]{:S(2)}) copy-start(bf16[2,128]{1,0:T(2,128)(2,1)} %param.25) | copy-start | bytes 1540
  132.7 108.5 %copy-start.53 = (bf16[2,512]{1,0:T(2,128)(2,1)S(1)}, bf16[2,512]{1,0:T(2,128)(2,1)}, u32[]{:S(2)}) copy-start(bf16[2,512]{1,0:T(2,128)(2,1)} %param.29) | copy-start | bytes 6148
  132.7 344.6 %all-gather.53.cloned.1.call-start = ((), (), s32[]{:S(2)}) async-start(), calls=%async_computation.31 | async-start | bytes 9437184 | tf_op jit(solution)/shard_map/all_gather | solution.py:342
  136.0 440.8 %all-gather.55.cloned.1.call-start = ((), (), s32[]{:S(2)}) async-start(), calls=%async_computation.32 | async-start | bytes 7077888 | tf_op jit(solution)/shard_map/all_gather | solution.py:333
  136.7 526.9 %all-gather.43.cloned.1.call-start = ((), (), s32[]{:S(2)}) async-start(), calls=%async_computation.14 | async-start | bytes 2621440 | tf_op jit(solution)/shard_map/all_gather | solution.py:71
  206.7 144.9 %copy-start.39 = (f32[1,1024]{1,0:T(1,128)}, f32[1,1024]{1,0:T(1,128)S(1)}, u32[]{:S(2)}) copy-start(f32[1,1024]{1,0:T(1,128)S(1)} %convert_element_type.458) | copy-start | bytes 12292
  485.0 96.4 %copy-start.47 = (f32[256]{0:T(256)}, f32[256]{0:T(256)S(1)}, u32[]{:S(2)}) copy-start(f32[256]{0:T(256)S(1)} %multiply_reduce_fusion.9) | copy-start | bytes 3076
  582.5 85.2 %all-gather.45.cloned.1.call-start = ((), (), s32[]{:S(2)}) async-start(), calls=%async_computation.15 | async-start | bytes 2621440 | tf_op jit(solution)/shard_map/all_gather | solution.py:72
  583.3 105.4 %all-gather.57.cloned.1.call-start = ((), (), s32[]{:S(2)}) async-start(), calls=%async_computation.33 | async-start | bytes 2359296 | tf_op jit(solution)/shard_map/all_gather | solution.py:336
  583.9 221.5 %all-gather.59.cloned.1.call-start = ((), (), s32[]{:S(2)}) async-start(), calls=%async_computation.34 | async-start | bytes 9437184 | tf_op jit(solution)/shard_map/all_gather | solution.py:340
  584.6 346.4 %all-gather.61.cloned.1.call-start = ((), (), s32[]{:S(2)}) async-start(), calls=%async_computation.35 | async-start | bytes 9437184 | tf_op jit(solution)/shard_map/all_gather | solution.py:342
  585.2 403.6 %reduce-scatter.15.cloned.1.call-start = ((), (), s32[]{:S(2)}) async-start(), calls=%async_computation.17 | async-start | bytes 2621440 | tf_op jit(solution)/shard_map/reduce_scatter | solution.py:138
  959.0 63.8 %reduce-scatter.13.cloned.1.call-start = ((), (), s32[]{:S(2)}) async-start(), calls=%async_computation.16 | async-start | bytes 2621440 | tf_op jit(solution)/shard_map/reduce_scatter | solution.py:135
  975.1 145.9 %reduce-scatter.19.cloned.1.call-start = ((), (), s32[]{:S(2)}) async-start(), calls=%async_computation.19 | async-start | bytes 2621440 | tf_op jit(solution)/shard_map/reduce_scatter | solution.py:138
  1058.0 65.6 %reduce-scatter.17.cloned.1.call-start = ((), (), s32[]{:S(2)}) async-start(), calls=%async_computation.18 | async-start | bytes 2621440 | tf_op jit(solution)/shard_map/reduce_scatter | solution.py:135
  1073.9 120.6 %reduce-scatter.27.cloned.1.call-start = ((), (), s32[]{:S(2)}) async-start(), calls=%async_computation.23 | async-start | bytes 2359296 | tf_op jit(solution)/shard_map/reduce_scatter | solution.py:387
  1077.3 187.3 %reduce-scatter.25.cloned.1.call-start = ((), (), s32[]{:S(2)}) async-start(), calls=%async_computation.22 | async-start | bytes 2359296 | tf_op jit(solution)/shard_map/reduce_scatter | solution.py:387
  1080.7 304.4 %reduce-scatter.23.cloned.1.call-start = ((), (), s32[]{:S(2)}) async-start(), calls=%async_computation.21 | async-start | bytes 7077888 | tf_op jit(solution)/shard_map/reduce_scatter | solution.py:378
  1086.9 449.9 %reduce-scatter.35.cloned.1.call-start = ((), (), s32[]{:S(2)}) async-start(), calls=%async_computation.27 | async-start | bytes 9437184 | tf_op jit(solution)/shard_map/reduce_scatter | solution.py:405
  1096.4 592.5 %reduce-scatter.31.cloned.1.call-start = ((), (), s32[]{:S(2)}) async-start(), calls=%async_computation.25 | async-start | bytes 9437184 | tf_op jit(solution)/shard_map/reduce_scatter | solution.py:399
  1104.3 736.3 %reduce-scatter.33.cloned.1.call-start = ((), (), s32[]{:S(2)}) async-start(), calls=%async_computation.26 | async-start | bytes 9437184 | tf_op jit(solution)/shard_map/reduce_scatter | solution.py:405
  1114.0 847.6 %reduce-scatter.21.cloned.1.call-start = ((), (), s32[]{:S(2)}) async-start(), calls=%async_computation.20 | async-start | bytes 7077888 | tf_op jit(solution)/shard_map/reduce_scatter | solution.py:378
  1129.5 984.2 %reduce-scatter.29.cloned.1.call-start = ((), (), s32[]{:S(2)}) async-start(), calls=%async_computation.24 | async-start | bytes 9437184 | tf_op jit(solution)/shard_map/reduce_scatter | solution.py:399
  1137.5 1099.2 %all-reduce.23.cloned.1.call-start = ((), (), s32[]{:S(2)}) async-start(), calls=%async_computation.36 | async-start | bytes 12582912 | tf_op jit(solution)/shard_map/psum | solution.py:415
  1168.9 944.9 %copy-start.37 = (bf16[16,64,256]{2,1,0:T(8,128)(2,1)S(1)}, bf16[16,64,256]{2,1,0:T(8,128)(2,1)}, u32[]{:S(2)}) copy-start(bf16[16,64,256]{2,1,0:T(8,128)(2,1)} %copy-done.36) | copy-start | bytes 1572868
  (61 other events, 583.6 us)
Sparse Core Ops, SparseCore 0:
  10.8 101.9 all-gather.46
  128.0 21.1 all-gather.38
  151.3 22.5 all-gather.40
  175.9 49.3 all-gather.48
  227.9 123.6 all-gather.50
  354.2 123.1 all-gather.52
  479.5 97.1 all-gather.54
  582.6 20.7 all-gather.42
  605.6 22.5 all-gather.44
  630.2 49.4 all-gather.56
  681.9 123.4 all-gather.58
  807.9 123.1 all-gather.60
  959.1 29.6 reduce-scatter.14
  991.3 31.4 reduce-scatter.12
  1058.1 31.4 reduce-scatter.18
  1092.1 31.3 reduce-scatter.16
  1126.9 67.6 reduce-scatter.26
  1198.0 66.5 reduce-scatter.24
  1268.2 116.9 reduce-scatter.22
  1388.6 148.1 reduce-scatter.34
  1540.9 147.9 reduce-scatter.30
  1692.5 148.0 reduce-scatter.32
  1844.6 116.9 reduce-scatter.20
  1965.5 148.1 reduce-scatter.28
  2116.6 120.1 all-reduce.22
where the time goes:
time: 2260 us; the launch traced here: 2250 us
  waiting for transfers between devices  1540 us (68%)
  blocking collectives  384 us (17%)
  matrix products  218 us (10%)
  local copies, waits for them, and re-layouts  52.3 us (2%)
  other arithmetic  36.9 us (2%)
    reduce_scatter x2, waiting for transfers between devices, shards(): lax.psum_scatter(local_grads[9].astype(jnp.bfloat16), 'fsdp', scatter_dim...  304 us
    reduce_scatter x2, waiting for transfers between devices, shards(): lax.psum_scatter(local_grads[11].astype(jnp.bfloat16), 'fsdp', scatter_di...  303 us
    reduce_scatter x2, waiting for transfers between devices, shards(): lax.psum_scatter(local_grads[2].astype(jnp.bfloat16), 'fsdp', scatter_dim...  242 us
    all_gather x2, waiting for transfers between devices, shards(): lax.all_gather(own_shards[11], 'fsdp', axis=0, tiled=True)  236 us
    all_gather x2, waiting for transfers between devices, shards(): lax.all_gather(own_shards[9], 'fsdp', axis=0, tiled=True)  167 us
    reduce_scatter x2, waiting for transfers between devices, shards(): lax.psum_scatter(local_grads[5].astype(jnp.bfloat16), 'fsdp', scatter_dim...  95.4 us
    all_gather x2, waiting for transfers between devices, shards(): lax.all_gather(own_shards[2], 'fsdp', axis=0, tiled=True)  91.7 us
    psum x1, waiting for transfers between devices, shards(): lax.psum(slices[2].astype(jnp.bfloat16), 'seq').astype(jnp.float32)  57.5 us
  transfers between devices with their start and end apart: 25, of which 17 were waited for; matrix products, arithmetic and copies ran while one was open for 9% of the time, Pallas kernels for 0%

commit v1 on v0

v1 whole, which is shorter than its diff:
```python
import jax
import jax.numpy as jnp
from jax import lax
from jax.sharding import PartitionSpec as P

HEADS = 16
HEAD_DIM = 64
LAYERS = 2
BLOCK = 256
EPS = 1e-05
NEG = -1e30
BF = jnp.bfloat16
F32 = jnp.float32


def normalize(inputs, scale_vec, shift_vec):
    center = inputs - jnp.mean(inputs, axis=-1, keepdims=True)
    spread = jnp.mean(center * center, axis=-1, keepdims=True)
    return center * lax.rsqrt(spread + EPS) * scale_vec + shift_vec


def smooth_gelu(values_in):
    inner = 0.7978845608028654 * (values_in + 0.044715 * values_in * values_in * values_in)
    return 0.5 * values_in * (1.0 + jnp.tanh(inner))


def head_slopes():
    return jnp.exp2(-8.0 * (jnp.arange(HEADS, dtype=F32) + 1.0) / HEADS)


def cube_masks(size):
    if size == 8:
        return (1, 2, 6)
    if size == 32:
        return (1, 3, 4, 12, 16)
    return tuple(1 << bit for bit in range(size.bit_length() - 1))


def rotated(masks, by):
    by = by % len(masks)
    return masks[by:] + masks[:by]


def hop(value, axis, mask):
    size = lax.axis_size(axis)
    return lax.ppermute(value, axis, [(i, i ^ mask) for i in range(size)])


def core_swap(value):
    return hop(value, "seq", 1)


def y_swap(value):
    return hop(value, "seq", 2)


def slot_table(order):
    rel = [0]
    for mask in order:
        rel = rel + [item ^ mask for item in rel]
    return rel


def take_slot(stacked, index):
    return lax.dynamic_index_in_dim(stacked, index, 0, keepdims=False)


def gather_shards(shard, order):
    current = shard[None]
    for mask in order:
        current = jnp.concatenate([current, hop(current, "fsdp", mask)])
    rel = slot_table(order)
    slot_of = [0] * len(rel)
    for slot, item in enumerate(rel):
        slot_of[item] = slot
    slot_of = jnp.array(slot_of, jnp.int32)
    me = lax.axis_index("fsdp")
    return jnp.concatenate(
        [take_slot(current, slot_of[me ^ owner])[None] for owner in range(len(rel))]
    )


def scatter_shards(full, order, kind=BF):
    me = lax.axis_index("fsdp")
    rel = slot_table(order[::-1])
    current = jnp.concatenate([take_slot(full, me ^ item)[None] for item in rel])
    for mask in order:
        half = current.shape[0] // 2
        other = hop(current[half:], "fsdp", mask)
        current = (current[:half].astype(F32) + other.astype(F32)).astype(kind)
    return current[0]


def attention_scores(queries, keys, q_pos, k_pos, slopes, seq_length):
    raw = jnp.einsum("qhd,khd->hqk", queries, keys, preferred_element_type=F32) * HEAD_DIM**-0.5
    distance = jnp.abs(q_pos[:, None] - k_pos[None, :]).astype(F32)
    raw = raw - slopes[:, None, None] * distance[None]
    visible = (k_pos[None, :] // BLOCK <= q_pos[:, None] // BLOCK) & (k_pos[None, :] < seq_length)
    return raw, visible[None]


def attend(queries, keys, values, q_pos, k_pos, slopes, seq_length):
    raw, visible = attention_scores(queries, keys, q_pos, k_pos, slopes, seq_length)
    top = jnp.max(jnp.where(visible, raw, NEG), axis=-1)
    weights = jnp.where(visible, jnp.exp(raw - top[..., None]), 0.0)
    total = jnp.sum(weights, axis=-1)
    summed = jnp.einsum("hqk,khd->hqd", weights.astype(BF), values, preferred_element_type=F32)
    attended = jnp.transpose(summed / total[..., None], (1, 0, 2)).reshape(queries.shape[0], -1)
    return attended, top + jnp.log(total)


def attend_back(queries, keys, values, grad_att, attended, lse, q_pos, k_pos, slopes, seq_length):
    rows, heads, _ = queries.shape
    grad_heads = grad_att.reshape(rows, heads, HEAD_DIM)
    delta = jnp.sum(
        grad_heads.astype(F32) * attended.reshape(rows, heads, HEAD_DIM), axis=-1
    ).T
    raw, visible = attention_scores(queries, keys, q_pos, k_pos, slopes, seq_length)
    probs = jnp.where(visible, jnp.exp(raw - lse[..., None]), 0.0)
    grad_probs = jnp.einsum("qhd,khd->hqk", grad_heads, values, preferred_element_type=F32)
    grad_scores = (probs * (grad_probs - delta[..., None])).astype(BF)
    scale = HEAD_DIM**-0.5
    grad_q = jnp.einsum("hqk,khd->qhd", grad_scores, keys, preferred_element_type=F32) * scale
    grad_k = jnp.einsum("hqk,qhd->khd", grad_scores, queries, preferred_element_type=F32) * scale
    grad_v = jnp.einsum("hqk,qhd->khd", probs.astype(BF), grad_heads, preferred_element_type=F32)
    return (
        grad_q.reshape(rows, -1),
        grad_k.reshape(keys.shape[0], -1),
        grad_v.reshape(keys.shape[0], -1),
    )


def dot(left, right):
    return jnp.dot(left, right, preferred_element_type=F32)


def dot_t(left, right):
    return jnp.einsum("tf,df->td", left, right, preferred_element_type=F32)


def t_dot(left, right):
    return jnp.einsum("td,tf->df", left, right, preferred_element_type=F32)


def pair(own):
    return jnp.concatenate([own, core_swap(own)])


def pair_sum(partial, rows):
    return partial[:rows] + core_swap(partial[rows:].astype(BF)).astype(F32)


def shards(
    tokens,
    lengths,
    cotangent,
    ln1_gain,
    ln1_bias,
    qkv_weight,
    query_bias,
    value_bias,
    out_weight,
    out_bias,
    ln2_gain,
    ln2_bias,
    up_weight,
    up_bias,
    down_weight,
    down_bias,
):
    fsdp = lax.axis_size("fsdp")
    masks = cube_masks(fsdp)
    run = lax.axis_index("seq")
    core = run % 2
    stream = tokens[0].astype(F32)
    rows, width = stream.shape
    half = width // 2
    seq_length = lengths[0]
    hidden = up_weight.shape[2]
    piece = hidden // fsdp // 2
    heads = HEADS // 2

    own_pos = jnp.arange(rows, dtype=jnp.int32)
    blocks = [(run ^ j) * rows + own_pos for j in range(4)]
    q_pos = jnp.concatenate(blocks[:2])
    k_pos = jnp.concatenate(blocks)
    slopes = lax.dynamic_slice_in_dim(head_slopes(), core * heads, heads)

    def core_part(value, axis):
        size = value.shape[axis] // 2
        return lax.dynamic_slice_in_dim(value, core * size, size, axis)

    vectors = (ln1_gain, ln1_bias, query_bias, value_bias, out_bias, ln2_gain, ln2_bias, down_bias)
    small = jnp.concatenate([jnp.stack(vectors, 1).reshape(LAYERS, -1), up_bias], axis=1)
    small = gather_shards(small, rotated(masks, 0)).astype(F32)
    part = width // fsdp

    def small_of(layer, member):
        return small[:, layer, member * part : (member + 1) * part].reshape(-1)

    def gathered(layer):
        qkv = qkv_weight[layer].reshape(-1, 3, width)
        qkv = core_part(qkv, 2).reshape(-1, 3 * half)
        w_qkv = gather_shards(qkv, rotated(masks, 0)).reshape(width, 3 * half)
        out_half = gather_shards(core_part(out_weight[layer], 1), rotated(masks, 0))
        out_half = out_half.reshape(width, half)
        out_other = core_swap(out_half)
        w_out = jnp.where(
            core == 0,
            jnp.concatenate([out_half, out_other], axis=1),
            jnp.concatenate([out_other, out_half], axis=1),
        )
        up = up_weight[layer].reshape(part, fsdp, 2, piece)
        up = lax.dynamic_index_in_dim(up, core, 2, keepdims=False).reshape(part, -1)
        w_up = gather_shards(up, rotated(masks, 1)).reshape(width, hidden // 2)
        w_down = gather_shards(core_part(down_weight[layer], 0), rotated(masks, 2))
        w_down = w_down.reshape(hidden // 2, width)
        bias_up = small[:, layer, 8 * part :].reshape(fsdp, 2, piece)
        bias_up = lax.dynamic_index_in_dim(bias_up, core, 1, keepdims=False).reshape(-1)
        bias_qkv = jnp.concatenate(
            [
                core_part(small_of(layer, 2), 0),
                jnp.zeros((half,), F32),
                core_part(small_of(layer, 3), 0),
            ]
        )
        return w_qkv, bias_qkv, w_out, w_up, bias_up, w_down

    weights = [gathered(layer) for layer in range(LAYERS)]
    saved = []
    for layer in range(LAYERS):
        w_qkv, bias_qkv, w_out, w_up, bias_up, w_down = weights[layer]
        normed = normalize(stream, small_of(layer, 0), small_of(layer, 1))
        h1 = pair(normed.astype(BF))
        packed = (dot(h1, w_qkv) + bias_qkv).astype(BF)
        kv = packed[:, half:]
        kv = jnp.concatenate([kv, y_swap(kv)])
        queries = packed[:, :half].reshape(-1, heads, HEAD_DIM)
        keys = kv[:, :half].reshape(-1, heads, HEAD_DIM)
        values = kv[:, half:].reshape(-1, heads, HEAD_DIM)
        attended, lse = attend(queries, keys, values, q_pos, k_pos, slopes, seq_length)
        att_low = attended.astype(BF)
        att_other = core_swap(att_low[rows:])
        att_own = jnp.where(
            core == 0,
            jnp.concatenate([att_low[:rows], att_other], axis=1),
            jnp.concatenate([att_other, att_low[:rows]], axis=1),
        )
        middle = stream + (dot(att_own, w_out) + small_of(layer, 4))
        normed = normalize(middle, small_of(layer, 5), small_of(layer, 6))
        h2 = pair(normed.astype(BF))
        pre = dot(h2, w_up) + bias_up
        act = smooth_gelu(pre).astype(BF)
        saved.append(
            (stream, h1, queries, keys, values, attended, lse, att_own, middle, h2, pre, act)
        )
        stream = middle + (pair_sum(dot(act, w_down), rows) + small_of(layer, 7))
    result = stream.astype(BF)[None]

    grad = cotangent[0].astype(F32)
    layer_grads = [None] * LAYERS
    for layer in reversed(range(LAYERS)):
        w_qkv, bias_qkv, w_out, w_up, bias_up, w_down = weights[layer]
        stream, h1, queries, keys, values, attended, lse, att_own, middle, h2, pre, act = saved[
            layer
        ]

        def owner_sum(full, by):
            shard = scatter_shards(full, rotated(masks, by)[::-1]).astype(F32)
            shard = shard + y_swap(shard.astype(BF)).astype(F32)
            return shard

        g_own = grad.astype(BF)
        g_down = pair(g_own)
        grad_down_w = owner_sum(t_dot(act, g_down).astype(BF).reshape(fsdp, piece, width), 2)
        grad_act = dot_t(g_down, w_down)
        _, gelu_pull = jax.vjp(smooth_gelu, pre)
        g_pre = gelu_pull(grad_act)[0].astype(BF)
        grad_up_w = owner_sum(t_dot(h2, g_pre).astype(BF).reshape(fsdp, part, -1), 1)
        grad_h2 = pair_sum(dot_t(g_pre, w_up), rows)
        _, norm_pull = jax.vjp(normalize, middle, small_of(layer, 5), small_of(layer, 6))
        grad_middle, grad_gain_two, grad_shift_two = norm_pull(grad_h2)
        grad_middle = grad + grad_middle
        g_branch = grad_middle.astype(BF)
        grad_out = t_dot(att_own, g_branch).astype(BF)
        kept = core_part(grad_out, 1)
        sent = lax.dynamic_slice_in_dim(grad_out, (1 - core) * half, half, 1)
        grad_out = (kept.astype(F32) + core_swap(sent).astype(F32)).astype(BF)
        grad_out_w = owner_sum(grad_out.reshape(fsdp, part, half), 0)
        g_att = dot_t(g_branch, w_out).astype(BF)
        g_att_kept = core_part(g_att, 1)
        g_att_sent = lax.dynamic_slice_in_dim(g_att, (1 - core) * half, half, 1)
        g_att = jnp.concatenate([g_att_kept, core_swap(g_att_sent)])
        grad_q, grad_k, grad_v = attend_back(
            queries, keys, values, g_att, attended, lse, q_pos, k_pos, slopes, seq_length
        )
        grad_kv = jnp.concatenate([grad_k, grad_v], axis=1)
        local = 2 * rows
        grad_kv = grad_kv[:local].astype(BF).astype(F32) + y_swap(grad_kv[local:].astype(BF)).astype(F32)
        g_packed = jnp.concatenate([grad_q, grad_kv], axis=1).astype(BF)
        grad_qkv_w = owner_sum(t_dot(h1, g_packed).astype(BF).reshape(fsdp, part, -1), 0)
        grad_h1 = pair_sum(dot_t(g_packed, w_qkv), rows)
        _, norm_pull = jax.vjp(normalize, stream, small_of(layer, 0), small_of(layer, 1))
        grad_stream, grad_gain_one, grad_shift_one = norm_pull(grad_h1)
        grad = grad_middle + grad_stream

        def spread(value):
            return lax.dynamic_update_slice_in_dim(
                jnp.zeros((2 * value.shape[0],), F32), value, core * value.shape[0], 0
            )

        packed_sum = jnp.sum(g_packed, axis=0, dtype=F32)
        up_sum = jnp.sum(g_pre, axis=0, dtype=F32).reshape(fsdp, 1, piece)
        up_sum = lax.dynamic_update_slice_in_dim(
            jnp.zeros((fsdp, 2, piece), F32), up_sum, core, 1
        ).reshape(fsdp, 2 * piece)
        members = [
            grad_gain_one,
            grad_shift_one,
            spread(packed_sum[:half]),
            spread(packed_sum[2 * half :]),
            jnp.sum(g_branch, axis=0, dtype=F32),
            grad_gain_two,
            grad_shift_two,
            jnp.sum(g_own, axis=0, dtype=F32),
        ]
        vector = jnp.concatenate([item.reshape(fsdp, part) for item in members] + [up_sum], axis=1)
        vector = scatter_shards(vector, rotated(masks, 0), F32)
        vector = vector + y_swap(vector)
        vector = vector + core_swap(vector)
        small_grads = [vector[i * part : (i + 1) * part] for i in range(8)] + [vector[8 * part :]]

        def both(own, axis):
            other = core_swap(own)
            return jnp.where(
                core == 0,
                jnp.concatenate([own, other], axis=axis),
                jnp.concatenate([other, own], axis=axis),
            )

        grad_qkv_w = both(grad_qkv_w.reshape(part, 3, half), 2).reshape(part, 3 * width)
        grad_out_w = both(grad_out_w, 1)
        grad_up_w = both(grad_up_w.reshape(part, fsdp, 1, piece), 2).reshape(part, hidden)
        grad_down_w = both(grad_down_w, 0)
        layer_grads[layer] = (
            small_grads[0],
            small_grads[1],
            grad_qkv_w,
            small_grads[2],
            small_grads[3],
            grad_out_w,
            small_grads[4],
            small_grads[5],
            small_grads[6],
            grad_up_w,
            small_grads[8],
            grad_down_w,
            small_grads[7],
        )
    stacked = tuple(
        jnp.stack([layer_grads[layer][member] for layer in range(LAYERS)]) for member in range(13)
    )
    return (result, grad[None]) + stacked


def solution(mesh):
    vector = P(None, "fsdp")
    matrix = P(None, "fsdp", None)
    data = P("fsdp", "seq", None)
    weight_specs = (
        vector,
        vector,
        matrix,
        vector,
        vector,
        matrix,
        vector,
        vector,
        vector,
        matrix,
        vector,
        matrix,
        vector,
    )
    in_specs = (data, P("fsdp"), data) + weight_specs
    out_specs = (data, data) + weight_specs
    return jax.shard_map(shards, mesh=mesh, in_specs=in_specs, out_specs=out_specs, check_vma=False)
```

time: 2260 us -> 1350 us (0.60)
  waiting for transfers between devices: 1540 us -> 422 us
  blocking collectives: 384 us -> 0 us
  starting transfers between devices: 1.89 us -> 355 us
  local copies, waits for them, and re-layouts: 52.3 us -> 200 us
  other arithmetic: 36.9 us -> 152 us
  matrix products: 218 us -> 158 us
  between operations: 17.5 us -> 50.9 us
    reduce_scatter x12 -> x0, waiting for transfers between devices: 987 us -> none  [the longest x2 304 us: shards(): lax.psum_scatter(local_grads[9].astype(jnp.bfloat16), 'fsdp', scatter_dim...]
    all_gather x12 -> x0, waiting for transfers between devices: 495 us -> none  [the longest x2 236 us: shards(): lax.all_gather(own_shards[11], 'fsdp', axis=0, tiled=True)]
    ppermute x0 -> x101, waiting for transfers between devices: none -> 422 us  [hop(): return lax.ppermute(value, axis, [(i, i ^ mask) for i in range(size)])]
    ppermute x0 -> x101, starting transfers between devices: none -> 355 us  [hop(): return lax.ppermute(value, axis, [(i, i ^ mask) for i in range(size)])]
    all_gather x18 -> x0, blocking collectives: 336 us -> none  [the longest x2 52.9 us: shards(): lax.all_gather(own_shards[10], 'fsdp', axis=0, tiled=True)]
    unnamed x139 -> x449, local copies, waits for them, and re-layouts: 15.3 us -> 93.5 us
    dot_general x36, matrix products: 218 us -> 158 us  [the longest x8 33.4 us: dot_t(): return jnp.einsum('tf,df->td', left, right, preferred_element_type=F32)]
    psum x1 -> x0, waiting for transfers between devices: 57.5 us -> none  [shards(): lax.psum(slices[2].astype(jnp.bfloat16), 'seq').astype(jnp.float32)]
  transfers between devices with their start and end apart: 25 -> 101, of which waited for: 17 -> 34; matrix products, arithmetic and copies ran while one was open for 9% -> 33% of each run, Pallas kernels for 0% -> 0%
where the time goes in v1:
time: 1350 us; the launch traced here: 1340 us
  waiting for transfers between devices  422 us (31%)
  starting transfers between devices  355 us (26%)
  local copies, waits for them, and re-layouts  200 us (15%)
  matrix products  158 us (12%)
  other arithmetic  152 us (11%)
  between operations  50.9 us (4%)
    ppermute x101, waiting for transfers between devices, hop(): return lax.ppermute(value, axis, [(i, i ^ mask) for i in range(size)])  422 us
    ppermute x101, starting transfers between devices, hop(): return lax.ppermute(value, axis, [(i, i ^ mask) for i in range(size)])  355 us
    unnamed x449, local copies, waits for them, and re-layouts  93.5 us
    concatenate x27, other arithmetic, gather_shards(): current = jnp.concatenate([current, hop(current, 'fsdp', mask)])  34.5 us
    dot_general x8, matrix products, dot_t(): return jnp.einsum('tf,df->td', left, right, preferred_element_type=F32)  33.4 us
    concatenate x13, local copies, waits for them, and re-layouts, gather_shards(): jnp.concatenate([take_slot(current, slot_of[me ^ owner])[None] for owner...  30.5 us
    dot_general x8, matrix products, dot(): return jnp.dot(left, right, preferred_element_type=F32)  28.4 us
    dot_general x8, matrix products, t_dot(): return jnp.einsum('td,tf->df', left, right, preferred_element_type=F32)  27.1 us
  transfers between devices with their start and end apart: 101, of which 34 were waited for; matrix products, arithmetic and copies ran while one was open for 33% of the time, Pallas kernels for 0%

profile of v1, /device:TPU:0, one launch (start us, length us, event | category | flops | bytes accessed | tf_op | source)
XLA Modules:
  0.0 1337.9 jit_solution(9727880250602798446)
XLA Ops:
  129.1 14.9 %collective-permute-done.35 = bf16[1,256,1024]{2,1,0:T(8,128)(2,1)S(1)} collective-permute-done((bf16[1,256,1024]{2,1,0:T(8,128)(2,1)S(1)}, bf16[1,256,1024]{2,1,0:T(8,128)(2,1)S(1)}, u32[]{:S(2)}, u32[]{:S(2)}) %collective-permute-start.35) | collective-permute-done | bytes 524320 | tf_op jit(solution)/shard_map/ppermute | solution.py:46
  147.6 7.6 collective-permute-done.17
  155.2 38.8 %collective-permute-start.5 = (bf16[2,128,1536]{1,2,0:T(8,128)(2,1)S(1)}, bf16[2,128,1536]{1,2,0:T(8,128)(2,1)S(1)}, u32[]{:S(2)}, u32[]{:S(2)}) collective-permute-start(bf16[2,128,1536]{1,2,0:T(8,128)(2,1)S(1)} %pad_maximum_fusion.38), channel_id=1, source_target_pairs={{0,8},{4,12},{8,0},{12,4},{16,24},{20,28},{24,16},{28,20},{1,9},{5... | collective-permute-start | bytes 2359304 | tf_op jit(solution)/shard_map/ppermute | solution.py:46
  204.7 7.3 collective-permute-done.5
  215.6 13.2 collective-permute-done.23
  237.2 15.7 %collective-permute-done.33 = bf16[2,128,2048]{1,2,0:T(8,128)(2,1)S(1)} collective-permute-done((bf16[2,128,2048]{1,2,0:T(8,128)(2,1)S(1)}, bf16[2,128,2048]{1,2,0:T(8,128)(2,1)S(1)}, u32[]{:S(2)}, u32[]{:S(2)}) %collective-permute-start.33) | collective-permute-done | bytes 1048608 | tf_op jit(solution)/shard_map/ppermute | solution.py:46
  255.9 48.5 %collective-permute-done.15 = bf16[2,128,2048]{1,2,0:T(8,128)(2,1)S(1)} collective-permute-done((bf16[2,128,2048]{1,2,0:T(8,128)(2,1)S(1)}, bf16[2,128,2048]{1,2,0:T(8,128)(2,1)S(1)}, u32[]{:S(2)}, u32[]{:S(2)}) %collective-permute-start.15) | collective-permute-done | bytes 1048608 | tf_op jit(solution)/shard_map/ppermute | solution.py:46
  308.6 97.6 %collective-permute-start.19 = (bf16[4,256,1024]{2,1,0:T(8,128)(2,1)}, bf16[4,256,1024]{2,1,0:T(8,128)(2,1)}, u32[]{:S(2)}, u32[]{:S(2)}) collective-permute-start(bf16[4,256,1024]{2,1,0:T(8,128)(2,1)} %pad_maximum_fusion.10), channel_id=1, source_target_pairs={{0,8},{4,12},{8,0},{12,4},{16,24},{20,28},{24,16},{28,20},{1,9},{5... | collective-permute-start | bytes 6291464 | tf_op jit(solution)/shard_map/ppermute | solution.py:46
  439.6 46.1 %collective-permute-done.37 = bf16[4,256,1024]{2,1,0:T(8,128)(2,1)} collective-permute-done((bf16[4,256,1024]{2,1,0:T(8,128)(2,1)}, bf16[4,256,1024]{2,1,0:T(8,128)(2,1)}, u32[]{:S(2)}, u32[]{:S(2)}) %collective-permute-start.37) | collective-permute-done | bytes 2097184 | tf_op jit(solution)/shard_map/ppermute | solution.py:46
  503.0 15.6 %collective-permute-done.7 = bf16[512,1024]{1,0:T(8,128)(2,1)S(1)} collective-permute-done((bf16[512,1024]{1,0:T(8,128)(2,1)S(1)}, bf16[512,1024]{1,0:T(8,128)(2,1)S(1)}, u32[]{:S(2)}, u32[]{:S(2)}) %collective-permute-start.7) | collective-permute-done | bytes 1048608 | tf_op jit(solution)/shard_map/ppermute | solution.py:46
  565.2 6.5 fusion.140
  588.2 17.7 %collective-permute-done.25 = bf16[512,1024]{1,0:T(8,128)(2,1)} collective-permute-done((bf16[512,1024]{1,0:T(8,128)(2,1)S(1)}, bf16[512,1024]{1,0:T(8,128)(2,1)}, u32[]{:S(2)}, u32[]{:S(2)}) %collective-permute-start.25) | collective-permute-done | bytes 1048608 | tf_op jit(solution)/shard_map/ppermute | solution.py:46
  631.6 6.7 copy.106
  655.8 8.0 convert_reduce_fusion
  667.0 6.5 convolution_convert_fusion
  687.3 9.0 fusion.8
  696.3 9.2 multiply_convert_fusion.1
  717.5 6.5 fusion.53
  726.9 10.1 collective-permute-done.42
  750.0 8.8 convert_reduce_fusion.1
  798.6 7.6 fusion.6
  806.2 9.2 multiply_convert_fusion
  827.3 15.7 %collective-permute-done.47 = bf16[512,1024]{0,1:T(8,128)(2,1)S(1)} collective-permute-done((bf16[512,1024]{0,1:T(8,128)(2,1)S(1)}, bf16[512,1024]{0,1:T(8,128)(2,1)S(1)}, u32[]{:S(2)}, u32[]{:S(2)}) %collective-permute-start.47) | collective-permute-done | bytes 1048608 | tf_op jit(solution)/shard_map/ppermute | solution.py:46
  923.8 35.7 %collective-permute-done.49 = f32[4,1536]{1,0:T(4,128)S(1)} collective-permute-done((f32[4,1536]{1,0:T(4,128)S(1)}, f32[4,1536]{1,0:T(4,128)S(1)}, u32[]{:S(2)}, u32[]{:S(2)}) %collective-permute-start.49) | collective-permute-done | bytes 24608 | tf_op jit(solution)/shard_map/ppermute | solution.py:46
  1017.5 83.4 %collective-permute-done.82 = bf16[2,128,2048]{2,1,0:T(8,128)(2,1)S(1)} collective-permute-done((bf16[2,128,2048]{2,1,0:T(8,128)(2,1)S(1)}, bf16[2,128,2048]{2,1,0:T(8,128)(2,1)S(1)}, u32[]{:S(2)}, u32[]{:S(2)}) %collective-permute-start.82) | collective-permute-done | bytes 1048608 | tf_op jit(solution)/shard_map/ppermute | solution.py:46
  1100.9 108.5 %collective-permute-start.88 = (bf16[1,128,2048]{2,1,0:T(8,128)(2,1)S(1)}, bf16[1,128,2048]{2,1,0:T(8,128)(2,1)S(1)}, u32[]{:S(2)}, u32[]{:S(2)}) collective-permute-start(bf16[1,128,2048]{2,1,0:T(8,128)(2,1)S(1)} %slice.631), channel_id=1, source_target_pairs={{0,8},{4,12},{8,0},{12,4},{16,24},{20,28},{24,16},{28,20},{1,9},{5... | collective-permute-start | bytes 1572872 | tf_op jit(solution)/shard_map/ppermute | solution.py:46
  1213.1 7.6 collective-permute-start.65
  1224.1 9.4 collective-permute-done.83
  1236.1 14.2 %collective-permute-done.60 = bf16[2,128,1536]{1,2,0:T(8,128)(2,1)S(1)} collective-permute-done((bf16[2,128,1536]{1,2,0:T(8,128)(2,1)S(1)}, bf16[2,128,1536]{1,2,0:T(8,128)(2,1)S(1)}, u32[]{:S(2)}, u32[]{:S(2)}) %collective-permute-start.60) | collective-permute-done | bytes 786464 | tf_op jit(solution)/shard_map/ppermute | solution.py:46
  1252.3 13.5 %collective-permute-done.65 = bf16[2,128,1536]{1,2,0:T(8,128)(2,1)S(1)} collective-permute-done((bf16[2,128,1536]{1,2,0:T(8,128)(2,1)S(1)}, bf16[2,128,1536]{1,2,0:T(8,128)(2,1)S(1)}, u32[]{:S(2)}, u32[]{:S(2)}) %collective-permute-start.65) | collective-permute-done | bytes 786464 | tf_op jit(solution)/shard_map/ppermute | solution.py:46
  1287.0 7.4 collective-permute-done.62
  1297.1 6.7 collective-permute-done.67
  (938 shorter events, 573.7 us)
Async XLA Ops:
  10.7 97.6 %collective-permute-start.9 = (bf16[1,128,512]{2,1,0:T(8,128)(2,1)S(1)}, bf16[1,128,512]{2,1,0:T(8,128)(2,1)}, u32[]{:S(2)}, u32[]{:S(2)}) collective-permute-start(bf16[1,128,512]{2,1,0:T(8,128)(2,1)S(1)} %constant_dynamic-slice_fusion.86), channel_id=1, source_target_pairs={{0,4},{4,0},{8,12},{12,8},{16,20},{20,16},{24,28},{28,24},{1,5},{5... | collective-permute-start | bytes 393224 | tf_op jit(solution)/shard_map/ppermute | solution.py:46
  11.4 93.8 %collective-permute-start.27 = (bf16[1,128,512]{2,1,0:T(8,128)(2,1)}, bf16[1,128,512]{2,1,0:T(8,128)(2,1)}, u32[]{:S(2)}, u32[]{:S(2)}) collective-permute-start(bf16[1,128,512]{2,1,0:T(8,128)(2,1)} %constant_dynamic-slice_fusion.65), channel_id=1, source_target_pairs={{0,4},{4,0},{8,12},{12,8},{16,20},{20,16},{24,28},{28,24},{1,5},{5... | collective-permute-start | bytes 393224 | tf_op jit(solution)/shard_map/ppermute | solution.py:46
  17.1 105.9 %collective-permute-start.22 = (bf16[1,128,1536]{1,2,0:T(8,128)(2,1)S(1)}, bf16[1,128,1536]{1,2,0:T(8,128)(2,1)}, u32[]{:S(2)}, u32[]{:S(2)}) collective-permute-start(bf16[1,128,1536]{1,2,0:T(8,128)(2,1)S(1)} %bitcast.326), channel_id=1, source_target_pairs={{0,4},{4,0},{8,12},{12,8},{16,20},{20,16},{24,28},{28,24},{1,5},{5... | collective-permute-start | bytes 1179656 | tf_op jit(solution)/shard_map/ppermute | solution.py:46
  17.6 109.5 %collective-permute-start.4 = (bf16[1,128,1536]{1,2,0:T(8,128)(2,1)S(1)}, bf16[1,128,1536]{1,2,0:T(8,128)(2,1)}, u32[]{:S(2)}, u32[]{:S(2)}) collective-permute-start(bf16[1,128,1536]{1,2,0:T(8,128)(2,1)S(1)} %bitcast.330), channel_id=1, source_target_pairs={{0,4},{4,0},{8,12},{12,8},{16,20},{20,16},{24,28},{28,24},{1,5},{5... | collective-permute-start | bytes 1179656 | tf_op jit(solution)/shard_map/ppermute | solution.py:46
  96.9 97.2 %collective-permute-start.32 = (bf16[1,128,2048]{1,2,0:T(8,128)(2,1)S(1)}, bf16[1,128,2048]{1,2,0:T(8,128)(2,1)}, u32[]{:S(2)}, u32[]{:S(2)}) collective-permute-start(bf16[1,128,2048]{1,2,0:T(8,128)(2,1)S(1)} %bitcast.316), channel_id=1, source_target_pairs={{0,8},{4,12},{8,0},{12,4},{16,24},{20,28},{24,16},{28,20},{1,9},{5... | collective-permute-start | bytes 1572872 | tf_op jit(solution)/shard_map/ppermute | solution.py:46
  115.5 79.8 %collective-permute-start.14 = (bf16[1,128,2048]{1,2,0:T(8,128)(2,1)S(1)}, bf16[1,128,2048]{1,2,0:T(8,128)(2,1)S(1)}, u32[]{:S(2)}, u32[]{:S(2)}) collective-permute-start(bf16[1,128,2048]{1,2,0:T(8,128)(2,1)S(1)} %bitcast.320), channel_id=1, source_target_pairs={{0,8},{4,12},{8,0},{12,4},{16,24},{20,28},{24,16},{28,20},{1,9},{5... | collective-permute-start | bytes 1572872 | tf_op jit(solution)/shard_map/ppermute | solution.py:46
  127.1 72.4 %collective-permute-start.11 = (bf16[4,128,512]{2,1,0:T(8,128)(2,1)S(1)}, bf16[4,128,512]{2,1,0:T(8,128)(2,1)S(1)}, u32[]{:S(2)}, u32[]{:S(2)}) collective-permute-start(bf16[4,128,512]{2,1,0:T(8,128)(2,1)S(1)} %pad_maximum_fusion.56), channel_id=1, source_target_pairs={{0,24},{4,28},{8,16},{12,20},{16,8},{20,12},{24,0},{28,4},{1,25},{... | collective-permute-start | bytes 1572872 | tf_op jit(solution)/shard_map/ppermute | solution.py:46
  213.2 95.5 %collective-permute-start.6 = (bf16[4,128,1536]{1,2,0:T(8,128)(2,1)S(1)}, bf16[4,128,1536]{1,2,0:T(8,128)(2,1)S(1)}, u32[]{:S(2)}, u32[]{:S(2)}) collective-permute-start(bf16[4,128,1536]{1,2,0:T(8,128)(2,1)S(1)} %pad_maximum_fusion.17), channel_id=1, source_target_pairs={{0,24},{4,28},{8,16},{12,20},{16,8},{20,12},{24,0},{28,4},{1,25},{... | collective-permute-start | bytes 4718600 | tf_op jit(solution)/shard_map/ppermute | solution.py:46
  228.9 75.5 %collective-permute-start.15 = (bf16[2,128,2048]{1,2,0:T(8,128)(2,1)S(1)}, bf16[2,128,2048]{1,2,0:T(8,128)(2,1)S(1)}, u32[]{:S(2)}, u32[]{:S(2)}) collective-permute-start(bf16[2,128,2048]{1,2,0:T(8,128)(2,1)S(1)} %pad_maximum_fusion.28), channel_id=1, source_target_pairs={{0,24},{4,28},{8,16},{12,20},{16,8},{20,12},{24,0},{28,4},{1,25},{... | collective-permute-start | bytes 3145736 | tf_op jit(solution)/shard_map/ppermute | solution.py:46
  233.6 422.3 %collective-permute-start.39 = (bf16[256,1024]{1,0:T(8,128)(2,1)}, bf16[256,1024]{1,0:T(8,128)(2,1)}, u32[]{:S(2)}, u32[]{:S(2)}) collective-permute-start(bf16[256,1024]{1,0:T(8,128)(2,1)} %bitcast.85), channel_id=1, source_target_pairs={{0,1},{1,0},{2,3},{3,2},{4,5},{5,4},{6,7},{7,6},{8,9},{9,8},{10,11... | collective-permute-start | bytes 1572872 | tf_op jit(solution)/shard_map/ppermute | solution.py:46
  235.2 183.1 %collective-permute-start.3 = (bf16[256,1024]{1,0:T(8,128)(2,1)}, bf16[256,1024]{1,0:T(8,128)(2,1)}, u32[]{:S(2)}, u32[]{:S(2)}) collective-permute-start(bf16[256,1024]{1,0:T(8,128)(2,1)} %fusion.58), channel_id=1, source_target_pairs={{0,1},{1,0},{2,3},{3,2},{4,5},{5,4},{6,7},{7,6},{8,9},{9,8},{10,11... | collective-permute-start | bytes 1572872 | tf_op jit(solution)/shard_map/ppermute | solution.py:46
  253.0 291.9 %collective-permute-start.12 = (bf16[1024,512]{1,0:T(8,128)(2,1)}, bf16[1024,512]{1,0:T(8,128)(2,1)}, u32[]{:S(2)}, u32[]{:S(2)}) collective-permute-start(bf16[1024,512]{1,0:T(8,128)(2,1)} %bitcast.34), channel_id=1, source_target_pairs={{0,1},{1,0},{2,3},{3,2},{4,5},{5,4},{6,7},{7,6},{8,9},{9,8},{10,11... | collective-permute-start | bytes 3145736 | tf_op jit(solution)/shard_map/ppermute | solution.py:46
  304.3 120.0 %collective-permute-start.24 = (bf16[4,128,1536]{1,2,0:T(8,128)(2,1)}, bf16[4,128,1536]{1,2,0:T(8,128)(2,1)}, u32[]{:S(2)}, u32[]{:S(2)}) collective-permute-start(bf16[4,128,1536]{1,2,0:T(8,128)(2,1)} %pad_maximum_fusion.18), channel_id=1, source_target_pairs={{0,24},{4,28},{8,16},{12,20},{16,8},{20,12},{24,0},{28,4},{1,25},{... | collective-permute-start | bytes 4718600 | tf_op jit(solution)/shard_map/ppermute | solution.py:46
  308.6 180.2 %collective-permute-start.19 = (bf16[4,256,1024]{2,1,0:T(8,128)(2,1)}, bf16[4,256,1024]{2,1,0:T(8,128)(2,1)}, u32[]{:S(2)}, u32[]{:S(2)}) collective-permute-start(bf16[4,256,1024]{2,1,0:T(8,128)(2,1)} %pad_maximum_fusion.10), channel_id=1, source_target_pairs={{0,8},{4,12},{8,0},{12,4},{16,24},{20,28},{24,16},{28,20},{1,9},{5... | collective-permute-start | bytes 6291464 | tf_op jit(solution)/shard_map/ppermute | solution.py:46
  418.4 67.3 %collective-permute-start.37 = (bf16[4,256,1024]{2,1,0:T(8,128)(2,1)}, bf16[4,256,1024]{2,1,0:T(8,128)(2,1)}, u32[]{:S(2)}, u32[]{:S(2)}) collective-permute-start(bf16[4,256,1024]{2,1,0:T(8,128)(2,1)} %pad_maximum_fusion.12), channel_id=1, source_target_pairs={{0,8},{4,12},{8,0},{12,4},{16,24},{20,28},{24,16},{28,20},{1,9},{5... | collective-permute-start | bytes 6291464 | tf_op jit(solution)/shard_map/ppermute | solution.py:46
  424.4 69.1 %collective-permute-start.16 = (bf16[4,128,2048]{1,2,0:T(8,128)(2,1)}, bf16[4,128,2048]{1,2,0:T(8,128)(2,1)}, u32[]{:S(2)}, u32[]{:S(2)}) collective-permute-start(bf16[4,128,2048]{1,2,0:T(8,128)(2,1)} %pad_maximum_fusion.9), channel_id=1, source_target_pairs={{0,4},{4,0},{8,12},{12,8},{16,20},{20,16},{24,28},{28,24},{1,5},{5... | collective-permute-start | bytes 6291464 | tf_op jit(solution)/shard_map/ppermute | solution.py:46
  485.7 156.4 %collective-permute-start.30 = (bf16[1024,512]{1,0:T(8,128)(2,1)}, bf16[1024,512]{1,0:T(8,128)(2,1)}, u32[]{:S(2)}, u32[]{:S(2)}) collective-permute-start(bf16[1024,512]{1,0:T(8,128)(2,1)} %bitcast.414), channel_id=1, source_target_pairs={{0,1},{1,0},{2,3},{3,2},{4,5},{5,4},{6,7},{7,6},{8,9},{9,8},{10,11... | collective-permute-start | bytes 3145736 | tf_op jit(solution)/shard_map/ppermute | solution.py:46
  488.8 70.7 %collective-permute-start.34 = (bf16[4,128,2048]{1,2,0:T(8,128)(2,1)}, bf16[4,128,2048]{1,2,0:T(8,128)(2,1)}, u32[]{:S(2)}, u32[]{:S(2)}) collective-permute-start(bf16[4,128,2048]{1,2,0:T(8,128)(2,1)} %pad_maximum_fusion.11), channel_id=1, source_target_pairs={{0,4},{4,0},{8,12},{12,8},{16,20},{20,16},{24,28},{28,24},{1,5},{5... | collective-permute-start | bytes 6291464 | tf_op jit(solution)/shard_map/ppermute | solution.py:46
  774.2 126.1 %collective-permute-start.96 = (bf16[4,256,1024]{2,1,0:T(8,128)(2,1)}, bf16[4,256,1024]{2,1,0:T(8,128)(2,1)}, u32[]{:S(2)}, u32[]{:S(2)}) collective-permute-start(bf16[4,256,1024]{2,1,0:T(8,128)(2,1)} %pad_maximum_fusion.16), channel_id=1, source_target_pairs={{0,8},{4,12},{8,0},{12,4},{16,24},{20,28},{24,16},{28,20},{1,9},{5... | collective-permute-start | bytes 6291464 | tf_op jit(solution)/shard_map/ppermute | solution.py:46
  777.6 130.5 %collective-permute-start.91 = (bf16[4,256,1024]{2,1,0:T(8,128)(2,1)}, bf16[4,256,1024]{2,1,0:T(8,128)(2,1)}, u32[]{:S(2)}, u32[]{:S(2)}) collective-permute-start(bf16[4,256,1024]{2,1,0:T(8,128)(2,1)} %pad_maximum_fusion.15), channel_id=1, source_target_pairs={{0,8},{4,12},{8,0},{12,4},{16,24},{20,28},{24,16},{28,20},{1,9},{5... | collective-permute-start | bytes 6291464 | tf_op jit(solution)/shard_map/ppermute | solution.py:46
  784.5 126.6 %collective-permute-start.86 = (bf16[4,128,2048]{2,1,0:T(8,128)(2,1)}, bf16[4,128,2048]{2,1,0:T(8,128)(2,1)}, u32[]{:S(2)}, u32[]{:S(2)}) collective-permute-start(bf16[4,128,2048]{2,1,0:T(8,128)(2,1)} %pad_maximum_fusion.14), channel_id=1, source_target_pairs={{0,4},{4,0},{8,12},{12,8},{16,20},{20,16},{24,28},{28,24},{1,5},{5... | collective-permute-start | bytes 6291464 | tf_op jit(solution)/shard_map/ppermute | solution.py:46
  821.7 93.1 %collective-permute-start.81 = (bf16[4,128,2048]{2,1,0:T(8,128)(2,1)}, bf16[4,128,2048]{2,1,0:T(8,128)(2,1)}, u32[]{:S(2)}, u32[]{:S(2)}) collective-permute-start(bf16[4,128,2048]{2,1,0:T(8,128)(2,1)} %pad_maximum_fusion.13), channel_id=1, source_target_pairs={{0,4},{4,0},{8,12},{12,8},{16,20},{20,16},{24,28},{28,24},{1,5},{5... | collective-permute-start | bytes 6291464 | tf_op jit(solution)/shard_map/ppermute | solution.py:46
  908.1 78.8 %collective-permute-start.71 = (bf16[2,128,512]{2,1,0:T(8,128)(2,1)S(1)}, bf16[2,128,512]{2,1,0:T(8,128)(2,1)S(1)}, u32[]{:S(2)}, u32[]{:S(2)}) collective-permute-start(bf16[2,128,512]{2,1,0:T(8,128)(2,1)S(1)} %slice.611), channel_id=1, source_target_pairs={{0,8},{4,12},{8,0},{12,4},{16,24},{20,28},{24,16},{28,20},{1,9},{5... | collective-permute-start | bytes 786440 | tf_op jit(solution)/shard_map/ppermute | solution.py:46
  911.1 99.6 %collective-permute-start.97 = (bf16[2,256,1024]{2,1,0:T(8,128)(2,1)S(1)}, bf16[2,256,1024]{2,1,0:T(8,128)(2,1)S(1)}, u32[]{:S(2)}, u32[]{:S(2)}) collective-permute-start(bf16[2,256,1024]{2,1,0:T(8,128)(2,1)S(1)} %slice.639), channel_id=1, source_target_pairs={{0,4},{4,0},{8,12},{12,8},{16,20},{20,16},{24,28},{28,24},{1,5},{5... | collective-permute-start | bytes 3145736 | tf_op jit(solution)/shard_map/ppermute | solution.py:46
  914.8 97.9 %collective-permute-start.92 = (bf16[2,256,1024]{2,1,0:T(8,128)(2,1)S(1)}, bf16[2,256,1024]{2,1,0:T(8,128)(2,1)S(1)}, u32[]{:S(2)}, u32[]{:S(2)}) collective-permute-start(bf16[2,256,1024]{2,1,0:T(8,128)(2,1)S(1)} %slice.635), channel_id=1, source_target_pairs={{0,4},{4,0},{8,12},{12,8},{16,20},{20,16},{24,28},{28,24},{1,5},{5... | collective-permute-start | bytes 3145736 | tf_op jit(solution)/shard_map/ppermute | solution.py:46
  918.7 96.8 %collective-permute-start.87 = (bf16[2,128,2048]{2,1,0:T(8,128)(2,1)S(1)}, bf16[2,128,2048]{2,1,0:T(8,128)(2,1)S(1)}, u32[]{:S(2)}, u32[]{:S(2)}) collective-permute-start(bf16[2,128,2048]{2,1,0:T(8,128)(2,1)S(1)} %slice.629), channel_id=1, source_target_pairs={{0,24},{4,28},{8,16},{12,20},{16,8},{20,12},{24,0},{28,4},{1,25},{... | collective-permute-start | bytes 3145736 | tf_op jit(solution)/shard_map/ppermute | solution.py:46
  1005.6 204.3 %collective-permute-start.59 = (bf16[4,128,1536]{1,2,0:T(8,128)(2,1)S(1)}, bf16[4,128,1536]{1,2,0:T(8,128)(2,1)S(1)}, u32[]{:S(2)}, u32[]{:S(2)}) collective-permute-start(bf16[4,128,1536]{1,2,0:T(8,128)(2,1)S(1)} %copy-done.81), channel_id=1, source_target_pairs={{0,24},{4,28},{8,16},{12,20},{16,8},{20,12},{24,0},{28,4},{1,25},{... | collective-permute-start | bytes 4718600 | tf_op jit(solution)/shard_map/ppermute | solution.py:46
  1007.2 203.4 %collective-permute-start.64 = (bf16[4,128,1536]{1,2,0:T(8,128)(2,1)S(1)}, bf16[4,128,1536]{1,2,0:T(8,128)(2,1)S(1)}, u32[]{:S(2)}, u32[]{:S(2)}) collective-permute-start(bf16[4,128,1536]{1,2,0:T(8,128)(2,1)S(1)} %copy-done.80), channel_id=1, source_target_pairs={{0,24},{4,28},{8,16},{12,20},{16,8},{20,12},{24,0},{28,4},{1,25},{... | collective-permute-start | bytes 4718600 | tf_op jit(solution)/shard_map/ppermute | solution.py:46
  1010.7 90.2 %collective-permute-start.82 = (bf16[2,128,2048]{2,1,0:T(8,128)(2,1)S(1)}, bf16[2,128,2048]{2,1,0:T(8,128)(2,1)S(1)}, u32[]{:S(2)}, u32[]{:S(2)}) collective-permute-start(bf16[2,128,2048]{2,1,0:T(8,128)(2,1)S(1)} %slice.625), channel_id=1, source_target_pairs={{0,24},{4,28},{8,16},{12,20},{16,8},{20,12},{24,0},{28,4},{1,25},{... | collective-permute-start | bytes 3145736 | tf_op jit(solution)/shard_map/ppermute | solution.py:46
  1012.7 200.4 %collective-permute-start.98 = (bf16[1,256,1024]{2,1,0:T(8,128)(2,1)S(1)}, bf16[1,256,1024]{2,1,0:T(8,128)(2,1)S(1)}, u32[]{:S(2)}, u32[]{:S(2)}) collective-permute-start(bf16[1,256,1024]{2,1,0:T(8,128)(2,1)S(1)} %slice.641), channel_id=1, source_target_pairs={{0,24},{4,28},{8,16},{12,20},{16,8},{20,12},{24,0},{28,4},{1,25},{... | collective-permute-start | bytes 1572872 | tf_op jit(solution)/shard_map/ppermute | solution.py:46
  1015.5 205.7 %collective-permute-start.93 = (bf16[1,256,1024]{2,1,0:T(8,128)(2,1)S(1)}, bf16[1,256,1024]{2,1,0:T(8,128)(2,1)S(1)}, u32[]{:S(2)}, u32[]{:S(2)}) collective-permute-start(bf16[1,256,1024]{2,1,0:T(8,128)(2,1)S(1)} %slice.637), channel_id=1, source_target_pairs={{0,24},{4,28},{8,16},{12,20},{16,8},{20,12},{24,0},{28,4},{1,25},{... | collective-permute-start | bytes 1572872 | tf_op jit(solution)/shard_map/ppermute | solution.py:46
  1100.9 122.3 %collective-permute-start.88 = (bf16[1,128,2048]{2,1,0:T(8,128)(2,1)S(1)}, bf16[1,128,2048]{2,1,0:T(8,128)(2,1)S(1)}, u32[]{:S(2)}, u32[]{:S(2)}) collective-permute-start(bf16[1,128,2048]{2,1,0:T(8,128)(2,1)S(1)} %slice.631), channel_id=1, source_target_pairs={{0,8},{4,12},{8,0},{12,4},{16,24},{20,28},{24,16},{28,20},{1,9},{5... | collective-permute-start | bytes 1572872 | tf_op jit(solution)/shard_map/ppermute | solution.py:46
  (239 other events, 4127.0 us)

commit v2 on v1

v2 whole, which is shorter than its diff:
```python
import functools

import jax
import jax.numpy as jnp
from jax import lax
from jax.experimental import pallas as pl
from jax.experimental.pallas import tpu as pltpu
from jax.sharding import PartitionSpec as P

HEADS = 16
HEAD_DIM = 64
LAYERS = 2
BLOCK = 256
EPS = 1e-05
NEG = -1e30
BF = jnp.bfloat16
F32 = jnp.float32


def normalize(inputs, scale_vec, shift_vec):
    center = inputs - jnp.mean(inputs, axis=-1, keepdims=True)
    spread = jnp.mean(center * center, axis=-1, keepdims=True)
    return center * lax.rsqrt(spread + EPS) * scale_vec + shift_vec


def smooth_gelu(values_in):
    inner = 0.7978845608028654 * (values_in + 0.044715 * values_in * values_in * values_in)
    return 0.5 * values_in * (1.0 + jnp.tanh(inner))


def head_slopes():
    return jnp.exp2(-8.0 * (jnp.arange(HEADS, dtype=F32) + 1.0) / HEADS)


def cube_masks(size):
    return tuple(1 << bit for bit in range(size.bit_length() - 1))


def hop(value, axis, mask):
    size = lax.axis_size(axis)
    return lax.ppermute(value, axis, [(i, i ^ mask) for i in range(size)])


def core_swap(value):
    return hop(value, "seq", 1)


def y_swap(value):
    return hop(value, "seq", 2)


def natural(parts):
    run = lax.axis_index("seq")
    stacked = jnp.stack(parts)
    return [lax.dynamic_index_in_dim(stacked, run ^ j, 0, keepdims=False) for j in range(4)]


def relative(value, axis):
    run = lax.axis_index("seq")
    size = value.shape[axis] // 4
    return [lax.dynamic_slice_in_dim(value, (run ^ j) * size, size, axis) for j in range(4)]


def seq_gather(own):
    across = y_swap(own)
    return jnp.concatenate([own, core_swap(own), across, core_swap(across)])


def seq_scatter(parts):
    far = parts[2] + core_swap(parts[3].astype(BF)).astype(F32)
    near = parts[0] + core_swap(parts[1].astype(BF)).astype(F32)
    return near + y_swap(far.astype(BF)).astype(F32)


def heads_to_rows(parts):
    across = y_swap(jnp.stack(parts[2:]))
    beside = core_swap(jnp.stack([parts[1], across[1]]))
    return jnp.concatenate(natural([parts[0], beside[0], across[0], beside[1]]), axis=1)


def rows_to_heads(value):
    parts = relative(value, 1)
    beside = core_swap(jnp.stack([parts[1], parts[3]]))
    across = y_swap(jnp.stack([parts[2], beside[1]]))
    return jnp.concatenate([parts[0], beside[0], across[0], across[1]])


def gather_small(shard):
    size = lax.axis_size("fsdp")
    current = shard[None]
    for mask in cube_masks(size):
        current = jnp.concatenate([current, hop(current, "fsdp", mask)])
    me = lax.axis_index("fsdp")
    return jnp.take(current, me ^ jnp.arange(size), axis=0)


def sum_small(full):
    size = lax.axis_size("fsdp")
    me = lax.axis_index("fsdp")
    current = jnp.take(full, me ^ jnp.arange(size), axis=0)
    for mask in cube_masks(size)[::-1]:
        half = current.shape[0] // 2
        current = current[:half] + hop(current[half:], "fsdp", mask)
    current = current[0]
    current = current + y_swap(current)
    return current + core_swap(current)


def assemble_kernel(widths, me_ref, *refs):
    count = len(widths)
    slots, outs, sems = refs[: -count - 1], refs[-count - 1 : -1], refs[-1]
    me = me_ref[0]
    rows = slots[0].shape[0]
    copies = []
    for r, slot in enumerate(slots):
        start = pl.multiple_of((me ^ r) * rows, rows)
        offset = 0
        for i, (out, size) in enumerate(zip(outs, widths)):
            source = slot.at[:, pl.ds(offset, size)]
            copies.append(
                pltpu.make_async_copy(source, out.at[pl.ds(start, rows), :], sems.at[r, i])
            )
            offset += size
    for copy in copies:
        copy.start()
    for copy in copies:
        copy.wait()


def assemble(slots, widths):
    rows = slots[0].shape[0]
    me = lax.axis_index("fsdp").astype(jnp.int32).reshape(1)
    hbm = pl.BlockSpec(memory_space=pl.ANY)
    return pl.pallas_call(
        functools.partial(assemble_kernel, widths),
        grid_spec=pltpu.PrefetchScalarGridSpec(
            num_scalar_prefetch=1,
            grid=(),
            in_specs=[hbm] * len(slots),
            out_specs=[hbm] * len(widths),
            scratch_shapes=[pltpu.SemaphoreType.DMA((len(slots), len(widths)))],
        ),
        out_shape=[jax.ShapeDtypeStruct((len(slots) * rows, size), BF) for size in widths],
        name="assemble",
    )(me, *slots)


def disperse_kernel(widths, slots, me_ref, *refs):
    count = len(widths)
    mats, even, odd, sems = refs[:count], refs[count], refs[count + 1], refs[-1]
    me = me_ref[0]
    rows = even.shape[1]
    copies = []
    for r in range(slots):
        start = pl.multiple_of((me ^ r) * rows, rows)
        target = (odd if r % 2 else even).at[r // 2]
        offset = 0
        for i, (mat, size) in enumerate(zip(mats, widths)):
            copies.append(
                pltpu.make_async_copy(
                    mat.at[pl.ds(start, rows), :],
                    target.at[:, pl.ds(offset, size)],
                    sems.at[r, i],
                )
            )
            offset += size
    for copy in copies:
        copy.start()
    for copy in copies:
        copy.wait()


def disperse(mats, slots):
    widths = [mat.shape[1] for mat in mats]
    rows = mats[0].shape[0] // slots
    me = lax.axis_index("fsdp").astype(jnp.int32).reshape(1)
    hbm = pl.BlockSpec(memory_space=pl.ANY)
    shape = jax.ShapeDtypeStruct((slots // 2, rows, sum(widths)), BF)
    return pl.pallas_call(
        functools.partial(disperse_kernel, widths, slots),
        grid_spec=pltpu.PrefetchScalarGridSpec(
            num_scalar_prefetch=1,
            grid=(),
            in_specs=[hbm] * len(mats),
            out_specs=[hbm] * 2,
            scratch_shapes=[pltpu.SemaphoreType.DMA((slots, len(widths)))],
        ),
        out_shape=[shape, shape],
        name="disperse",
    )(me, *mats)


def tied(value, after):
    return lax.optimization_barrier((value, after))[0]


def gather_bundle(own):
    size = lax.axis_size("fsdp")
    slots = [None] * size
    slots[0] = own
    for r in range(2, size, 2):
        slots[r] = hop(own, "fsdp", r)
    for r in range(0, size, 2):
        slots[r + 1] = hop(slots[r], "fsdp", 1)
    return slots


def scatter_bundle(mats, split=False):
    size = lax.axis_size("fsdp")
    even, odd = disperse(mats, size)
    if split:
        places = list(range(1, size // 2)) + [0]
        summed = [None] * (size // 2)
        for k in places:
            summed[k] = even[k].astype(F32) + hop(odd[k], "fsdp", 1).astype(F32)
    else:
        summed = even.astype(F32) + hop(odd, "fsdp", 1).astype(F32)
    total = summed[0]
    for k in range(1, size // 2):
        total = total + hop(summed[k].astype(BF), "fsdp", 2 * k).astype(F32)
    return total.astype(BF)


def attention_scores(queries, keys, q_pos, k_pos, slopes, seq_length):
    raw = jnp.einsum("qhd,khd->hqk", queries, keys, preferred_element_type=F32) * HEAD_DIM**-0.5
    distance = jnp.abs(q_pos[:, None] - k_pos[None, :]).astype(F32)
    raw = raw - slopes[:, None, None] * distance[None]
    visible = (k_pos[None, :] // BLOCK <= q_pos[:, None] // BLOCK) & (k_pos[None, :] < seq_length)
    return raw, visible[None]


def attend(queries, keys, values, q_pos, k_pos, slopes, seq_length):
    raw, visible = attention_scores(queries, keys, q_pos, k_pos, slopes, seq_length)
    top = jnp.max(jnp.where(visible, raw, NEG), axis=-1)
    weights = jnp.where(visible, jnp.exp(raw - top[..., None]), 0.0)
    total = jnp.sum(weights, axis=-1)
    summed = jnp.einsum("hqk,khd->hqd", weights.astype(BF), values, preferred_element_type=F32)
    attended = jnp.transpose(summed / total[..., None], (1, 0, 2)).reshape(queries.shape[0], -1)
    return attended, top + jnp.log(total)


def attend_back(queries, keys, values, grad_att, attended, lse, q_pos, k_pos, slopes, seq_length):
    rows, heads, _ = queries.shape
    grad_heads = grad_att.reshape(rows, heads, HEAD_DIM)
    delta = jnp.sum(
        grad_heads.astype(F32) * attended.reshape(rows, heads, HEAD_DIM), axis=-1
    ).T
    raw, visible = attention_scores(queries, keys, q_pos, k_pos, slopes, seq_length)
    probs = jnp.where(visible, jnp.exp(raw - lse[..., None]), 0.0)
    grad_probs = jnp.einsum("qhd,khd->hqk", grad_heads, values, preferred_element_type=F32)
    grad_scores = (probs * (grad_probs - delta[..., None])).astype(BF)
    scale = HEAD_DIM**-0.5
    grad_q = jnp.einsum("hqk,khd->qhd", grad_scores, keys, preferred_element_type=F32) * scale
    grad_k = jnp.einsum("hqk,qhd->khd", grad_scores, queries, preferred_element_type=F32) * scale
    grad_v = jnp.einsum("hqk,qhd->khd", probs.astype(BF), grad_heads, preferred_element_type=F32)
    return (
        grad_q.reshape(rows, -1),
        grad_k.reshape(keys.shape[0], -1),
        grad_v.reshape(keys.shape[0], -1),
    )


def dot(left, right):
    return jnp.dot(left, right, preferred_element_type=F32)


def dot_t(left, right):
    return jnp.einsum("tf,df->td", left, right, preferred_element_type=F32)


def t_dot(left, right):
    return jnp.einsum("td,tf->df", left, right, preferred_element_type=F32)


def shards(
    tokens,
    lengths,
    cotangent,
    ln1_gain,
    ln1_bias,
    qkv_weight,
    query_bias,
    value_bias,
    out_weight,
    out_bias,
    ln2_gain,
    ln2_bias,
    up_weight,
    up_bias,
    down_weight,
    down_bias,
):
    fsdp = lax.axis_size("fsdp")
    run = lax.axis_index("seq")
    stream = tokens[0].astype(F32)
    rows, width = stream.shape
    seq_length = lengths[0]
    hidden = up_weight.shape[2]
    heads = HEADS // 4
    mine = width // 4
    part = width // fsdp
    piece = hidden // fsdp // 4

    positions = jnp.concatenate(
        [(run ^ j) * rows + jnp.arange(rows, dtype=jnp.int32) for j in range(4)]
    )
    slopes = lax.dynamic_slice_in_dim(head_slopes(), run * heads, heads)

    def quarter(value, axis):
        size = value.shape[axis] // 4
        return lax.dynamic_slice_in_dim(value, run * size, size, axis)

    vectors = (ln1_gain, ln1_bias, query_bias, value_bias, out_bias, ln2_gain, ln2_bias, down_bias)
    small = jnp.concatenate([jnp.stack(vectors, 1).reshape(LAYERS, -1), up_bias], axis=1)
    small = gather_small(small).astype(F32)

    def small_of(layer, member):
        return small[:, layer, member * part : (member + 1) * part].reshape(-1)

    half = width // 2

    def core_half(value, axis):
        return lax.dynamic_slice_in_dim(value, (run % 2) * half, half, axis)

    def bundle(layer, members):
        parts = {
            "qkv": lambda: quarter(qkv_weight[layer].reshape(part, 3, width), 2),
            "out": lambda: core_half(out_weight[layer], 1),
            "up": lambda: quarter(up_weight[layer].reshape(part, fsdp, -1), 2),
            "down": lambda: quarter(down_weight[layer], 0),
        }
        return jnp.concatenate([parts[name]().reshape(part, -1) for name in members], axis=1)

    def both(own):
        other = core_swap(own)
        return jnp.where(
            run % 2 == 0,
            jnp.concatenate([own, other], axis=1),
            jnp.concatenate([other, own], axis=1),
        )

    first = gather_bundle(bundle(0, ["qkv"]))
    second = gather_bundle(tied(bundle(0, ["out", "up", "down"]), first[2::2]))
    third = gather_bundle(tied(bundle(1, ["qkv", "out", "up", "down"]), second[2::2]))
    sizes = [3 * mine, half, hidden // 4, width]
    weights = [assemble(first, sizes[:1]) + assemble(second, sizes[1:]), assemble(third, sizes)]
    weights = [(w_qkv, both(w_out), w_up, w_down) for w_qkv, w_out, w_up, w_down in weights]

    def biases(layer):
        bias_up = quarter(small[:, layer, 8 * part :], 1).reshape(-1)
        bias_qkv = jnp.concatenate(
            [quarter(small_of(layer, 2), 0), jnp.zeros((mine,), F32), quarter(small_of(layer, 3), 0)]
        )
        return bias_qkv, bias_up

    saved = []
    for layer in range(LAYERS):
        w_qkv, w_out, w_up, w_down = weights[layer]
        bias_qkv, bias_up = biases(layer)
        normed = normalize(stream, small_of(layer, 0), small_of(layer, 1))
        h1 = seq_gather(normed.astype(BF))
        packed = (dot(h1, w_qkv) + bias_qkv).astype(BF)
        queries, keys, values = (
            packed[:, i * mine : (i + 1) * mine].reshape(-1, heads, HEAD_DIM) for i in range(3)
        )
        attended, lse = attend(queries, keys, values, positions, positions, slopes, seq_length)
        att_low = attended.astype(BF)
        att_own = heads_to_rows([att_low[j * rows : (j + 1) * rows] for j in range(4)])
        middle = stream + (dot(att_own, w_out) + small_of(layer, 4))
        normed = normalize(middle, small_of(layer, 5), small_of(layer, 6))
        h2 = seq_gather(normed.astype(BF))
        pre = dot(h2, w_up) + bias_up
        act = smooth_gelu(pre).astype(BF)
        saved.append(
            (stream, h1, queries, keys, values, attended, lse, att_own, middle, h2, pre, act)
        )
        partial = dot(act, w_down)
        total = seq_scatter([partial[j * rows : (j + 1) * rows] for j in range(4)])
        stream = middle + (total + small_of(layer, 7))
    result = stream.astype(BF)[None]

    grad = cotangent[0].astype(F32)
    layer_grads = [None] * LAYERS
    for layer in reversed(range(LAYERS)):
        w_qkv, w_out, w_up, w_down = weights[layer]
        stream, h1, queries, keys, values, attended, lse, att_own, middle, h2, pre, act = saved[
            layer
        ]
        g_own = grad.astype(BF)
        g_down = seq_gather(g_own)
        grad_down_w = t_dot(act, g_down).astype(BF)
        _, gelu_pull = jax.vjp(smooth_gelu, pre)
        g_pre = gelu_pull(dot_t(g_down, w_down))[0].astype(BF)
        grad_up_w = t_dot(h2, g_pre).astype(BF)
        partial = dot_t(g_pre, w_up)
        grad_h2 = seq_scatter([partial[j * rows : (j + 1) * rows] for j in range(4)])
        _, norm_pull = jax.vjp(normalize, middle, small_of(layer, 5), small_of(layer, 6))
        grad_middle, grad_gain_two, grad_shift_two = norm_pull(grad_h2)
        grad_middle = grad + grad_middle
        g_branch = grad_middle.astype(BF)
        grad_out_w = t_dot(att_own, g_branch).astype(BF)
        grad_out_w = (
            core_half(grad_out_w, 1).astype(F32)
            + core_swap(
                lax.dynamic_slice_in_dim(grad_out_w, (1 - run % 2) * half, half, 1)
            ).astype(F32)
        ).astype(BF)
        g_att = rows_to_heads(dot_t(g_branch, w_out).astype(BF))
        grads = attend_back(
            queries, keys, values, g_att, attended, lse, positions, positions, slopes, seq_length
        )
        g_packed = jnp.concatenate(grads, axis=1).astype(BF)
        grad_qkv_w = t_dot(h1, g_packed).astype(BF)
        partial = dot_t(g_packed, w_qkv)
        grad_h1 = seq_scatter([partial[j * rows : (j + 1) * rows] for j in range(4)])
        _, norm_pull = jax.vjp(normalize, stream, small_of(layer, 0), small_of(layer, 1))
        grad_stream, grad_gain_one, grad_shift_one = norm_pull(grad_h1)
        grad = grad_middle + grad_stream

        def spread(value, axis=0):
            shape = list(value.shape)
            size = shape[axis]
            shape[axis] = 4 * size
            return lax.dynamic_update_slice_in_dim(jnp.zeros(shape, F32), value, run * size, axis)

        packed_sum = jnp.sum(g_packed, axis=0, dtype=F32)
        members = [
            grad_gain_one,
            grad_shift_one,
            spread(packed_sum[:mine]),
            spread(packed_sum[2 * mine :]),
            jnp.sum(g_branch, axis=0, dtype=F32),
            grad_gain_two,
            grad_shift_two,
            jnp.sum(g_own, axis=0, dtype=F32),
        ]
        up_sum = spread(jnp.sum(g_pre, axis=0, dtype=F32).reshape(fsdp, piece), 1)
        vector = jnp.concatenate([item.reshape(fsdp, part) for item in members] + [up_sum], axis=1)
        vector = sum_small(vector)
        small_grads = [vector[i * part : (i + 1) * part] for i in range(8)] + [vector[8 * part :]]

        if layer:
            total = scatter_bundle([grad_qkv_w, grad_out_w, grad_up_w, grad_down_w])
            totals = [total]
        else:
            totals = [
                scatter_bundle([grad_qkv_w], True),
                scatter_bundle([grad_out_w, grad_up_w, grad_down_w]),
            ]
        quarters = []
        for total in totals:
            across = y_swap(total)
            beside = core_swap(jnp.stack([total, across]))
            quarters.append([total, beside[0], across, beside[1]])
        quarters = [jnp.concatenate(pieces, axis=1) for pieces in zip(*quarters)]
        edges = [3 * mine, 3 * mine + half, 3 * mine + half + hidden // 4]
        quarters = [jnp.split(item, edges, axis=1) for item in quarters]
        by_name = list(zip(*quarters))

        def whole(parts, axis):
            return jnp.concatenate(natural(parts), axis=axis).astype(F32)

        outs = by_name[1]
        halves = [
            outs[0].astype(F32) + outs[2].astype(F32),
            outs[1].astype(F32) + outs[3].astype(F32),
        ]
        grad_out_w = jnp.where(
            run % 2 == 0,
            jnp.concatenate(halves, axis=1),
            jnp.concatenate(halves[::-1], axis=1),
        )
        layer_grads[layer] = (
            small_grads[0],
            small_grads[1],
            whole([item.reshape(part, 3, mine) for item in by_name[0]], 2).reshape(part, 3 * width),
            small_grads[2],
            small_grads[3],
            grad_out_w,
            small_grads[4],
            small_grads[5],
            small_grads[6],
            whole([item.reshape(part, fsdp, piece) for item in by_name[2]], 2).reshape(
                part, hidden
            ),
            small_grads[8],
            whole([item.reshape(piece, width) for item in by_name[3]], 0),
            small_grads[7],
        )
    stacked = tuple(
        jnp.stack([layer_grads[layer][member] for layer in range(LAYERS)]) for member in range(13)
    )
    return (result, grad[None]) + stacked


def solution(mesh):
    vector = P(None, "fsdp")
    matrix = P(None, "fsdp", None)
    data = P("fsdp", "seq", None)
    weight_specs = (
        vector,
        vector,
        matrix,
        vector,
        vector,
        matrix,
        vector,
        vector,
        vector,
        matrix,
        vector,
        matrix,
        vector,
    )
    in_specs = (data, P("fsdp"), data) + weight_specs
    out_specs = (data, data) + weight_specs
    return jax.shard_map(shards, mesh=mesh, in_specs=in_specs, out_specs=out_specs, check_vma=False)
```

time: 1350 us -> 1620 us (1.20)
  Pallas kernels: 0 us -> 834 us
  starting transfers between devices: 355 us -> 89.6 us
  local copies, waits for them, and re-layouts: 200 us -> 74.2 us
  waiting for transfers between devices: 422 us -> 324 us
  between operations: 50.9 us -> 4.84 us
  other arithmetic: 152 us -> 117 us
    pallas_call x0 -> x6, Pallas kernels: none -> 834 us  [the longest x3 417 us: assemble(): pl.pallas_call(functools.partial(assemble_kernel, widths), grid_spec=pltp...]
    ppermute x101 -> x103, starting transfers between devices: 355 us -> 89.6 us  [hop(): return lax.ppermute(value, axis, [(i, i ^ mask) for i in range(size)])]
    ppermute x101 -> x103, waiting for transfers between devices: 422 us -> 324 us  [hop(): return lax.ppermute(value, axis, [(i, i ^ mask) for i in range(size)])]
    unnamed x449 -> x382, local copies, waits for them, and re-layouts: 93.5 us -> 17.5 us
    concatenate x46 -> x14, other arithmetic: 56.1 us -> 8.18 us  [the longest x4 4.89 us: shards(): jnp.concatenate(halves, axis=1)]
    concatenate x15 -> x0, local copies, waits for them, and re-layouts: 33.8 us -> none  [the longest x13 30.5 us: gather_shards(): jnp.concatenate([take_slot(current, slot_of[me ^ owner])[None] for owner...]
    another operation x4 -> x19, other arithmetic: 2.35 us -> 21.8 us
    dynamic_slice x27 -> x21, local copies, waits for them, and re-layouts: 27 us -> 10.1 us  [the longest x10 4.92 us: quarter(): return lax.dynamic_slice_in_dim(value, run * size, size, axis)]
  transfers between devices with their start and end apart: 101 -> 103, of which waited for: 34 -> 43; matrix products, arithmetic and copies ran while one was open for 33% -> 17% of each run, Pallas kernels for 0% -> 52%
where the time goes in v2:
time: 1620 us; the launch traced here: 1610 us
  Pallas kernels  834 us (51%)
  waiting for transfers between devices  324 us (20%)
  matrix products  171 us (11%)
  other arithmetic  117 us (7%)
  starting transfers between devices  89.6 us (6%)
  local copies, waits for them, and re-layouts  74.2 us (5%)
    pallas_call x3, Pallas kernels, assemble(): pl.pallas_call(functools.partial(assemble_kernel, widths), grid_spec=pltp...  417 us
    pallas_call x3, Pallas kernels, disperse(): pl.pallas_call(functools.partial(disperse_kernel, widths, slots), grid_sp...  417 us
    ppermute x103, waiting for transfers between devices, hop(): return lax.ppermute(value, axis, [(i, i ^ mask) for i in range(size)])  324 us
    ppermute x103, starting transfers between devices, hop(): return lax.ppermute(value, axis, [(i, i ^ mask) for i in range(size)])  89.6 us
    dot_general x8, matrix products, t_dot(): return jnp.einsum('td,tf->df', left, right, preferred_element_type=F32)  33.6 us
  transfers between devices with their start and end apart: 103, of which 43 were waited for; matrix products, arithmetic and copies ran while one was open for 17% of the time, Pallas kernels for 52%

profile of v2, /device:TPU:0, one launch (start us, length us, event | category | flops | bytes accessed | tf_op | source)
XLA Modules:
  0.0 1614.8 jit_solution(1577728340233038994)
XLA Ops:
  55.1 48.8 %assemble.3 = bf16[1024,768]{1,0:T(8,128)(2,1)} custom-call(s32[1]{0:T(128)} %bitcast.15.me_ref, bf16[128,768]{1,0:T(8,128)(2,1)} %copy.48.refs_0_, bf16[128,768]{1,0:T(8,128)(2,1)} %collective-permute-done.6.refs_1_, bf16[128,768]{1,0:T(8,128)(2,1)} %collective-permute-done.7.refs_2_, bf16[128,768]{1,0:T(8,128)(2,1)} %copy-done.66, ...), custom_call_target="tpu_custom_call" | custom-call | tf_op jit(solution)/shard_map/assemble/pallas_call | solution.py:134
  112.9 9.0 select_reduce_fusion.1
  121.9 8.8 fusion
  130.7 10.0 fusion.191
  141.4 8.4 collective-permute-done.19.refs_5_
  149.8 13.1 collective-permute-done.21.refs_7_
  162.9 160.1 %assemble.4 = (bf16[1024,512]{1,0:T(8,128)(2,1)}, bf16[1024,1024]{1,0:T(8,128)(2,1)}, bf16[1024,1024]{1,0:T(8,128)(2,1)}) custom-call(s32[1]{0:T(128)} %bitcast.15.me_ref, bf16[128,2560]{1,0:T(8,128)(2,1)} %copy-done.16, bf16[128,2560]{1,0:T(8,128)(2,1)} %collective-permute-done.15.refs_1_, bf16[128,2560]{1,0:T(8,128)(2,1)} %collective-permute-done.16.refs_2_, ...), custom_call_target="tpu_custom_call" | custom-call | tf_op jit(solution)/shard_map/assemble/pallas_call | solution.py:134
  330.8 13.4 collective-permute-done.24
  373.8 22.2 %collective-permute-done.33.refs_2_ = bf16[128,3328]{1,0:T(8,128)(2,1)S(1)} collective-permute-done((bf16[128,3328]{1,0:T(8,128)(2,1)S(1)}, bf16[128,3328]{1,0:T(8,128)(2,1)S(1)}, u32[]{:S(2)}, u32[]{:S(2)}) %collective-permute-start.33) | collective-permute-done | bytes 852000 | tf_op jit(solution)/shard_map/ppermute | solution.py:41
  396.5 21.1 %collective-permute-done.35.refs_4_ = bf16[128,3328]{1,0:T(8,128)(2,1)S(1)} collective-permute-done((bf16[128,3328]{1,0:T(8,128)(2,1)S(1)}, bf16[128,3328]{1,0:T(8,128)(2,1)S(1)}, u32[]{:S(2)}, u32[]{:S(2)}) %collective-permute-start.35) | collective-permute-done | bytes 852000 | tf_op jit(solution)/shard_map/ppermute | solution.py:41
  421.1 18.4 %collective-permute-done.36.refs_5_ = bf16[128,3328]{1,0:T(8,128)(2,1)S(1)} collective-permute-done((bf16[128,3328]{1,0:T(8,128)(2,1)S(1)}, bf16[128,3328]{1,0:T(8,128)(2,1)S(1)}, u32[]{:S(2)}, u32[]{:S(2)}) %collective-permute-start.36) | collective-permute-done | bytes 852000 | tf_op jit(solution)/shard_map/ppermute | solution.py:41
  440.5 11.7 collective-permute-done.38.refs_7_
  452.2 207.9 %assemble.5 = (bf16[1024,768]{1,0:T(8,128)(2,1)}, bf16[1024,512]{1,0:T(8,128)(2,1)}, bf16[1024,1024]{1,0:T(8,128)(2,1)}, bf16[1024,1024]{1,0:T(8,128)(2,1)}) custom-call(s32[1]{0:T(128)} %bitcast.15.me_ref, bf16[128,3328]{1,0:T(8,128)(2,1)} %copy-done.13, bf16[128,3328]{1,0:T(8,128)(2,1)} %copy-done.42, bf16[128,3328]{1,0:T(8,128)(2,1)} %copy-done.43, ...), custom_call_target="tpu_custom_call" | custom-call | tf_op jit(solution)/shard_map/assemble/pallas_call | solution.py:134
  665.1 9.0 select_reduce_fusion
  674.1 8.8 fusion.2
  683.0 8.7 fusion.194
  705.7 11.9 collective-permute-done.43
  718.3 9.7 collective-permute-done.49
  735.2 8.3 convert_reduce_fusion
  766.3 9.6 collective-permute-done.47
  797.1 8.9 fusion.55
  806.2 9.3 multiply_convert_fusion.1
  833.4 207.9 %disperse.4 = (bf16[4,128,3328]{2,1,0:T(8,128)(2,1)}, bf16[4,128,3328]{2,1,0:T(8,128)(2,1)}) custom-call(s32[1]{0:T(128)} %bitcast.15.me_ref, bf16[1024,768]{1,0:T(8,128)(2,1)} %convolution_convert_fusion.6.refs_0_, bf16[1024,512]{1,0:T(8,128)(2,1)} %add_convert_fusion.3.refs_1_, bf16[1024,1024]{1,0:T(8,128)(2,1)} %convolution_convert_fusion.4.refs_2_, ...), custom_call_target="tpu_custom_call" | custom-call | tf_op jit(solution)/shard_map/disperse/pallas_call | solution.py:179
  1047.2 12.7 collective-permute-done.60
  1061.9 8.1 convert_reduce_fusion.1
  1119.2 9.4 multiply_convert_fusion
  1145.7 48.8 %disperse.3 = (bf16[4,128,768]{2,1,0:T(8,128)(2,1)}, bf16[4,128,768]{2,1,0:T(8,128)(2,1)}) custom-call(s32[1]{0:T(128)} %bitcast.15.me_ref, bf16[1024,768]{1,0:T(8,128)(2,1)} %convolution_convert_fusion.7.refs_0_), custom_call_target="tpu_custom_call" | custom-call | tf_op jit(solution)/shard_map/disperse/pallas_call | solution.py:179
  1244.9 160.1 %disperse.5 = (bf16[4,128,2560]{2,1,0:T(8,128)(2,1)}, bf16[4,128,2560]{2,1,0:T(8,128)(2,1)}) custom-call(s32[1]{0:T(128)} %bitcast.15.me_ref, bf16[1024,512]{1,0:T(8,128)(2,1)} %add_convert_fusion.2.refs_0_, bf16[1024,1024]{1,0:T(8,128)(2,1)} %convolution_convert_fusion.1.refs_1_, bf16[1024,1024]{1,0:T(8,128)(2,1)} %convolution_convert_fusion.refs_2_), custom_call_target="tpu_custom_call" | custom-call | tf_op jit(solution)/shard_map/disperse/pallas_call | solution.py:179
  1458.0 14.3 collective-permute-done.94
  1478.3 26.5 %collective-permute-done.97 = bf16[4,128,2560]{2,1,0:T(8,128)(2,1)} collective-permute-done((bf16[4,128,2560]{2,1,0:T(8,128)(2,1)}, bf16[4,128,2560]{2,1,0:T(8,128)(2,1)}, u32[]{:S(2)}, u32[]{:S(2)}) %collective-permute-start.97) | collective-permute-done | bytes 2621472 | tf_op jit(solution)/shard_map/ppermute | solution.py:41
  1521.0 10.8 collective-permute-done.100
  1531.8 39.9 %collective-permute-done.99 = bf16[128,2560]{1,0:T(8,128)(2,1)} collective-permute-done((bf16[128,2560]{1,0:T(8,128)(2,1)}, bf16[128,2560]{1,0:T(8,128)(2,1)}, u32[]{:S(2)}, u32[]{:S(2)}) %collective-permute-start.99) | collective-permute-done | bytes 655392 | tf_op jit(solution)/shard_map/ppermute | solution.py:41
  (847 shorter events, 434.3 us)
Async XLA Ops:
  36.8 68.6 %collective-permute-start.16 = (bf16[128,2560]{1,0:T(8,128)(2,1)S(1)}, bf16[128,2560]{1,0:T(8,128)(2,1)}, u32[]{:S(2)}, u32[]{:S(2)}) collective-permute-start(bf16[128,2560]{1,0:T(8,128)(2,1)S(1)} %pad_maximum_fusion.20.refs_0_), channel_id=1, source_target_pairs={{0,8},{4,12},{8,0},{12,4},{16,24},{20,28},{24,16},{28,20},{1,9},{5... | collective-permute-start | bytes 1966088 | tf_op jit(solution)/shard_map/ppermute | solution.py:41
  38.1 67.9 %collective-permute-start.18 = (bf16[128,2560]{1,0:T(8,128)(2,1)S(1)}, bf16[128,2560]{1,0:T(8,128)(2,1)}, u32[]{:S(2)}, u32[]{:S(2)}) collective-permute-start(bf16[128,2560]{1,0:T(8,128)(2,1)S(1)} %pad_maximum_fusion.20.refs_0_), channel_id=1, source_target_pairs={{0,16},{4,20},{8,24},{12,28},{16,0},{20,4},{24,8},{28,12},{1,17},{... | collective-permute-start | bytes 1966088 | tf_op jit(solution)/shard_map/ppermute | solution.py:41
  42.7 64.8 %collective-permute-start.20 = (bf16[128,2560]{1,0:T(8,128)(2,1)S(1)}, bf16[128,2560]{1,0:T(8,128)(2,1)}, u32[]{:S(2)}, u32[]{:S(2)}) collective-permute-start(bf16[128,2560]{1,0:T(8,128)(2,1)S(1)} %pad_maximum_fusion.20.refs_0_), channel_id=1, source_target_pairs={{0,24},{4,28},{8,16},{12,20},{16,8},{20,12},{24,0},{28,4},{1,25},{... | collective-permute-start | bytes 1966088 | tf_op jit(solution)/shard_map/ppermute | solution.py:41
  50.8 53.1 %collective-permute-start.3 = (bf16[256,1024]{1,0:T(8,128)(2,1)S(1)}, bf16[256,1024]{1,0:T(8,128)(2,1)}, u32[]{:S(2)}, u32[]{:S(2)}) collective-permute-start(bf16[256,1024]{1,0:T(8,128)(2,1)S(1)} %fusion.68), channel_id=1, source_target_pairs={{0,1},{1,0},{2,3},{3,2},{4,5},{5,4},{6,7},{7,6},{8,9},{9,8},{10,11... | collective-permute-start | bytes 1572872 | tf_op jit(solution)/shard_map/ppermute | solution.py:41
  50.8 57.3 %collective-permute-start.5 = (bf16[256,1024]{1,0:T(8,128)(2,1)}, bf16[256,1024]{1,0:T(8,128)(2,1)}, u32[]{:S(2)}, u32[]{:S(2)}) collective-permute-start(bf16[256,1024]{1,0:T(8,128)(2,1)} %collective-permute-done.4), channel_id=1, source_target_pairs={{0,1},{1,0},{2,3},{3,2},{4,5},{5,4},{6,7},{7,6},{8,9},{9,8},{10,11... | collective-permute-start | bytes 1572872 | tf_op jit(solution)/shard_map/ppermute | solution.py:41
  103.9 37.5 %collective-permute-start.15 = (bf16[128,2560]{1,0:T(8,128)(2,1)S(1)}, bf16[128,2560]{1,0:T(8,128)(2,1)}, u32[]{:S(2)}, u32[]{:S(2)}) collective-permute-start(bf16[128,2560]{1,0:T(8,128)(2,1)S(1)} %pad_maximum_fusion.20.refs_0_), channel_id=1, source_target_pairs={{0,4},{4,0},{8,12},{12,8},{16,20},{20,16},{24,28},{28,24},{1,5},{5... | collective-permute-start | bytes 1966088 | tf_op jit(solution)/shard_map/ppermute | solution.py:41
  105.5 35.9 %collective-permute-start.17 = (bf16[128,2560]{1,0:T(8,128)(2,1)}, bf16[128,2560]{1,0:T(8,128)(2,1)}, u32[]{:S(2)}, u32[]{:S(2)}) collective-permute-start(bf16[128,2560]{1,0:T(8,128)(2,1)} %collective-permute-done.16.refs_2_), channel_id=1, source_target_pairs={{0,4},{4,0},{8,12},{12,8},{16,20},{20,16},{24,28},{28,24},{1,5},{5... | collective-permute-start | bytes 1966088 | tf_op jit(solution)/shard_map/ppermute | solution.py:41
  106.0 43.8 %collective-permute-start.19 = (bf16[128,2560]{1,0:T(8,128)(2,1)}, bf16[128,2560]{1,0:T(8,128)(2,1)}, u32[]{:S(2)}, u32[]{:S(2)}) collective-permute-start(bf16[128,2560]{1,0:T(8,128)(2,1)} %collective-permute-done.18.refs_4_), channel_id=1, source_target_pairs={{0,4},{4,0},{8,12},{12,8},{16,20},{20,16},{24,28},{28,24},{1,5},{5... | collective-permute-start | bytes 1966088 | tf_op jit(solution)/shard_map/ppermute | solution.py:41
  107.5 55.4 %collective-permute-start.21 = (bf16[128,2560]{1,0:T(8,128)(2,1)}, bf16[128,2560]{1,0:T(8,128)(2,1)}, u32[]{:S(2)}, u32[]{:S(2)}) collective-permute-start(bf16[128,2560]{1,0:T(8,128)(2,1)} %collective-permute-done.20.refs_6_), channel_id=1, source_target_pairs={{0,4},{4,0},{8,12},{12,8},{16,20},{20,16},{24,28},{28,24},{1,5},{5... | collective-permute-start | bytes 1966088 | tf_op jit(solution)/shard_map/ppermute | solution.py:41
  140.8 182.3 %collective-permute-start.13 = (bf16[2,256,256]{1,2,0:T(8,128)(2,1)S(1)}, bf16[2,256,256]{1,2,0:T(8,128)(2,1)S(1)}, u32[]{:S(2)}, u32[]{:S(2)}) collective-permute-start(bf16[2,256,256]{1,2,0:T(8,128)(2,1)S(1)} %pad_maximum_fusion.44), channel_id=1, source_target_pairs={{0,2},{1,3},{2,0},{3,1},{4,6},{5,7},{6,4},{7,5},{8,10},{9,11},{10,... | collective-permute-start | bytes 786440 | tf_op jit(solution)/shard_map/ppermute | solution.py:41
  356.5 63.1 %collective-permute-start.32 = (bf16[128,3328]{1,0:T(8,128)(2,1)S(1)}, bf16[128,3328]{1,0:T(8,128)(2,1)S(1)}, u32[]{:S(2)}, u32[]{:S(2)}) collective-permute-start(bf16[128,3328]{1,0:T(8,128)(2,1)S(1)} %pad_maximum_fusion.15.refs_0_), channel_id=1, source_target_pairs={{0,4},{4,0},{8,12},{12,8},{16,20},{20,16},{24,28},{28,24},{1,5},{5... | collective-permute-start | bytes 2555912 | tf_op jit(solution)/shard_map/ppermute | solution.py:41
  358.0 37.9 %collective-permute-start.33 = (bf16[128,3328]{1,0:T(8,128)(2,1)S(1)}, bf16[128,3328]{1,0:T(8,128)(2,1)S(1)}, u32[]{:S(2)}, u32[]{:S(2)}) collective-permute-start(bf16[128,3328]{1,0:T(8,128)(2,1)S(1)} %pad_maximum_fusion.15.refs_0_), channel_id=1, source_target_pairs={{0,8},{4,12},{8,0},{12,4},{16,24},{20,28},{24,16},{28,20},{1,9},{5... | collective-permute-start | bytes 2555912 | tf_op jit(solution)/shard_map/ppermute | solution.py:41
  358.3 59.3 %collective-permute-start.35 = (bf16[128,3328]{1,0:T(8,128)(2,1)S(1)}, bf16[128,3328]{1,0:T(8,128)(2,1)S(1)}, u32[]{:S(2)}, u32[]{:S(2)}) collective-permute-start(bf16[128,3328]{1,0:T(8,128)(2,1)S(1)} %pad_maximum_fusion.15.refs_0_), channel_id=1, source_target_pairs={{0,16},{4,20},{8,24},{12,28},{16,0},{20,4},{24,8},{28,12},{1,17},{... | collective-permute-start | bytes 2555912 | tf_op jit(solution)/shard_map/ppermute | solution.py:41
  361.3 56.9 %collective-permute-start.37 = (bf16[128,3328]{1,0:T(8,128)(2,1)S(1)}, bf16[128,3328]{1,0:T(8,128)(2,1)S(1)}, u32[]{:S(2)}, u32[]{:S(2)}) collective-permute-start(bf16[128,3328]{1,0:T(8,128)(2,1)S(1)} %pad_maximum_fusion.15.refs_0_), channel_id=1, source_target_pairs={{0,24},{4,28},{8,16},{12,20},{16,8},{20,12},{24,0},{28,4},{1,25},{... | collective-permute-start | bytes 2555912 | tf_op jit(solution)/shard_map/ppermute | solution.py:41
  373.2 47.4 %collective-permute-start.30 = (bf16[256,1024]{1,0:T(8,128)(2,1)}, bf16[256,1024]{1,0:T(8,128)(2,1)}, u32[]{:S(2)}, u32[]{:S(2)}) collective-permute-start(bf16[256,1024]{1,0:T(8,128)(2,1)} %add_convert_fusion.5), channel_id=1, source_target_pairs={{0,2},{1,3},{2,0},{3,1},{4,6},{5,7},{6,4},{7,5},{8,10},{9,11},{10,... | collective-permute-start | bytes 1572872 | tf_op jit(solution)/shard_map/ppermute | solution.py:41
  420.6 239.4 %collective-permute-start.29 = (bf16[256,1024]{1,0:T(8,128)(2,1)}, bf16[256,1024]{1,0:T(8,128)(2,1)}, u32[]{:S(2)}, u32[]{:S(2)}) collective-permute-start(bf16[256,1024]{1,0:T(8,128)(2,1)} %add_convert_fusion.5), channel_id=1, source_target_pairs={{0,1},{1,0},{2,3},{3,2},{4,5},{5,4},{6,7},{7,6},{8,9},{9,8},{10,11... | collective-permute-start | bytes 1572872 | tf_op jit(solution)/shard_map/ppermute | solution.py:41
  420.6 239.4 %collective-permute-start.31 = (bf16[256,1024]{1,0:T(8,128)(2,1)}, bf16[256,1024]{1,0:T(8,128)(2,1)}, u32[]{:S(2)}, u32[]{:S(2)}) collective-permute-start(bf16[256,1024]{1,0:T(8,128)(2,1)} %collective-permute-done.30), channel_id=1, source_target_pairs={{0,1},{1,0},{2,3},{3,2},{4,5},{5,4},{6,7},{7,6},{8,9},{9,8},{10,11... | collective-permute-start | bytes 1572872 | tf_op jit(solution)/shard_map/ppermute | solution.py:41
  793.2 37.6 %collective-permute-start.89 = (bf16[1024,512]{1,0:T(8,128)(2,1)}, bf16[1024,512]{1,0:T(8,128)(2,1)}, u32[]{:S(2)}, u32[]{:S(2)}) collective-permute-start(bf16[1024,512]{1,0:T(8,128)(2,1)} %constant_dynamic-slice_fusion.9), channel_id=1, source_target_pairs={{0,1},{1,0},{2,3},{3,2},{4,5},{5,4},{6,7},{7,6},{8,9},{9,8},{10,11... | collective-permute-start | bytes 3145736 | tf_op jit(solution)/shard_map/ppermute | solution.py:41
  822.6 219.3 %collective-permute-start.56 = (bf16[256,1024]{1,0:T(8,128)(2,1)}, bf16[256,1024]{1,0:T(8,128)(2,1)}, u32[]{:S(2)}, u32[]{:S(2)}) collective-permute-start(bf16[256,1024]{1,0:T(8,128)(2,1)} %get-tuple-element.107), channel_id=1, source_target_pairs={{0,1},{1,0},{2,3},{3,2},{4,5},{5,4},{6,7},{7,6},{8,9},{9,8},{10,11... | collective-permute-start | bytes 1572872 | tf_op jit(solution)/shard_map/ppermute | solution.py:41
  829.1 212.8 %collective-permute-start.58 = (bf16[256,1024]{1,0:T(8,128)(2,1)}, bf16[256,1024]{1,0:T(8,128)(2,1)}, u32[]{:S(2)}, u32[]{:S(2)}) collective-permute-start(bf16[256,1024]{1,0:T(8,128)(2,1)} %fusion.76), channel_id=1, source_target_pairs={{0,2},{1,3},{2,0},{3,1},{4,6},{5,7},{6,4},{7,5},{8,10},{9,11},{10,... | collective-permute-start | bytes 1572872 | tf_op jit(solution)/shard_map/ppermute | solution.py:41
  1041.3 175.4 %collective-permute-start.90 = (bf16[4,128,3328]{2,1,0:T(8,128)(2,1)}, bf16[4,128,3328]{2,1,0:T(8,128)(2,1)}, u32[]{:S(2)}, u32[]{:S(2)}) collective-permute-start(bf16[4,128,3328]{2,1,0:T(8,128)(2,1)} %get-tuple-element.43), channel_id=1, source_target_pairs={{0,4},{4,0},{8,12},{12,8},{16,20},{20,16},{24,28},{28,24},{1,5},{5... | collective-permute-start | bytes 10223624 | tf_op jit(solution)/shard_map/ppermute | solution.py:41
  1107.3 134.5 %collective-permute-start.96 = (bf16[1024,512]{1,0:T(8,128)(2,1)}, bf16[1024,512]{1,0:T(8,128)(2,1)}, u32[]{:S(2)}, u32[]{:S(2)}) collective-permute-start(bf16[1024,512]{1,0:T(8,128)(2,1)} %constant_dynamic-slice_fusion.8), channel_id=1, source_target_pairs={{0,1},{1,0},{2,3},{3,2},{4,5},{5,4},{6,7},{7,6},{8,9},{9,8},{10,11... | collective-permute-start | bytes 3145736 | tf_op jit(solution)/shard_map/ppermute | solution.py:41
  1223.0 187.8 %collective-permute-start.67 = (bf16[256,1024]{1,0:T(8,128)(2,1)}, bf16[256,1024]{1,0:T(8,128)(2,1)}, u32[]{:S(2)}, u32[]{:S(2)}) collective-permute-start(bf16[256,1024]{1,0:T(8,128)(2,1)} %get-tuple-element.103), channel_id=1, source_target_pairs={{0,1},{1,0},{2,3},{3,2},{4,5},{5,4},{6,7},{7,6},{8,9},{9,8},{10,11... | collective-permute-start | bytes 1572872 | tf_op jit(solution)/shard_map/ppermute | solution.py:41
  1233.2 215.6 %collective-permute-start.93 = (bf16[128,3328]{1,0:T(8,128)(2,1)}, bf16[128,3328]{1,0:T(8,128)(2,1)S(1)}, u32[]{:S(2)}, u32[]{:S(2)}) collective-permute-start(bf16[128,3328]{1,0:T(8,128)(2,1)} %get-tuple-element.98), channel_id=1, source_target_pairs={{0,24},{4,28},{8,16},{12,20},{16,8},{20,12},{24,0},{28,4},{1,25},{... | collective-permute-start | bytes 2555912 | tf_op jit(solution)/shard_map/ppermute | solution.py:41
  1237.6 211.2 %collective-permute-start.92 = (bf16[128,3328]{1,0:T(8,128)(2,1)}, bf16[128,3328]{1,0:T(8,128)(2,1)}, u32[]{:S(2)}, u32[]{:S(2)}) collective-permute-start(bf16[128,3328]{1,0:T(8,128)(2,1)} %get-tuple-element.99), channel_id=1, source_target_pairs={{0,16},{4,20},{8,24},{12,28},{16,0},{20,4},{24,8},{28,12},{1,17},{... | collective-permute-start | bytes 2555912 | tf_op jit(solution)/shard_map/ppermute | solution.py:41
  1239.5 166.6 %collective-permute-start.88 = (bf16[2,128,768]{2,1,0:T(8,128)(2,1)}, bf16[2,128,768]{2,1,0:T(8,128)(2,1)}, u32[]{:S(2)}, u32[]{:S(2)}) collective-permute-start(bf16[2,128,768]{2,1,0:T(8,128)(2,1)} %pad_maximum_fusion.27), channel_id=1, source_target_pairs={{0,1},{1,0},{2,3},{3,2},{4,5},{5,4},{6,7},{7,6},{8,9},{9,8},{10,11... | collective-permute-start | bytes 1179656 | tf_op jit(solution)/shard_map/ppermute | solution.py:41
  1241.8 169.1 %collective-permute-start.69 = (bf16[256,1024]{1,0:T(8,128)(2,1)}, bf16[256,1024]{1,0:T(8,128)(2,1)}, u32[]{:S(2)}, u32[]{:S(2)}) collective-permute-start(bf16[256,1024]{1,0:T(8,128)(2,1)} %fusion.72), channel_id=1, source_target_pairs={{0,2},{1,3},{2,0},{3,1},{4,6},{5,7},{6,4},{7,5},{8,10},{9,11},{10,... | collective-permute-start | bytes 1572872 | tf_op jit(solution)/shard_map/ppermute | solution.py:41
  1406.1 42.7 %collective-permute-start.91 = (bf16[128,3328]{1,0:T(8,128)(2,1)}, bf16[128,3328]{1,0:T(8,128)(2,1)}, u32[]{:S(2)}, u32[]{:S(2)}) collective-permute-start(bf16[128,3328]{1,0:T(8,128)(2,1)} %get-tuple-element.97), channel_id=1, source_target_pairs={{0,8},{4,12},{8,0},{12,4},{16,24},{20,28},{24,16},{28,20},{1,9},{5... | collective-permute-start | bytes 2555912 | tf_op jit(solution)/shard_map/ppermute | solution.py:41
  1445.2 59.6 %collective-permute-start.97 = (bf16[4,128,2560]{2,1,0:T(8,128)(2,1)}, bf16[4,128,2560]{2,1,0:T(8,128)(2,1)}, u32[]{:S(2)}, u32[]{:S(2)}) collective-permute-start(bf16[4,128,2560]{2,1,0:T(8,128)(2,1)} %get-tuple-element.45), channel_id=1, source_target_pairs={{0,4},{4,0},{8,12},{12,8},{16,20},{20,16},{24,28},{28,24},{1,5},{5... | collective-permute-start | bytes 7864328 | tf_op jit(solution)/shard_map/ppermute | solution.py:41
  1473.6 42.7 %collective-permute-start.95 = (bf16[2,128,3328]{2,1,0:T(8,128)(2,1)}, bf16[2,128,3328]{2,1,0:T(8,128)(2,1)S(1)}, u32[]{:S(2)}, u32[]{:S(2)}) collective-permute-start(bf16[2,128,3328]{2,1,0:T(8,128)(2,1)} %pad_maximum_fusion.6), channel_id=1, source_target_pairs={{0,1},{1,0},{2,3},{3,2},{4,5},{5,4},{6,7},{7,6},{8,9},{9,8},{10,11... | collective-permute-start | bytes 5111816 | tf_op jit(solution)/shard_map/ppermute | solution.py:41
  1513.6 58.1 %collective-permute-start.99 = (bf16[128,2560]{1,0:T(8,128)(2,1)}, bf16[128,2560]{1,0:T(8,128)(2,1)}, u32[]{:S(2)}, u32[]{:S(2)}) collective-permute-start(bf16[128,2560]{1,0:T(8,128)(2,1)} %get-tuple-element.102), channel_id=1, source_target_pairs={{0,16},{4,20},{8,24},{12,28},{16,0},{20,4},{24,8},{28,12},{1,17},{... | collective-permute-start | bytes 1966088 | tf_op jit(solution)/shard_map/ppermute | solution.py:41
  1514.9 56.8 %collective-permute-start.98 = (bf16[128,2560]{1,0:T(8,128)(2,1)}, bf16[128,2560]{1,0:T(8,128)(2,1)}, u32[]{:S(2)}, u32[]{:S(2)}) collective-permute-start(bf16[128,2560]{1,0:T(8,128)(2,1)} %get-tuple-element.100), channel_id=1, source_target_pairs={{0,8},{4,12},{8,0},{12,4},{16,24},{20,28},{24,16},{28,20},{1,9},{5... | collective-permute-start | bytes 1966088 | tf_op jit(solution)/shard_map/ppermute | solution.py:41
  (240 other events, 4123.9 us)

commit v3 on v1

v3 whole, which is shorter than its diff:
```python
import functools

import jax
import jax.numpy as jnp
from jax import lax
from jax.experimental import pallas as pl
from jax.experimental.pallas import tpu as pltpu
from jax.sharding import PartitionSpec as P

HEADS = 16
HEAD_DIM = 64
LAYERS = 2
BLOCK = 256
EPS = 1e-05
NEG = -1e30
BF = jnp.bfloat16
F32 = jnp.float32
GELU = 0.7978845608028654
CUBIC = 0.044715
VMEM = pl.BlockSpec(memory_space=pltpu.VMEM)
SMEM = pl.BlockSpec(memory_space=pltpu.SMEM)


def head_slopes():
    return jnp.exp2(-8.0 * (jnp.arange(HEADS, dtype=F32) + 1.0) / HEADS)


def hop(value, axis, mask):
    size = lax.axis_size(axis)
    return lax.ppermute(value, axis, [(i, i ^ mask) for i in range(size)])


def core_swap(value):
    return hop(value, "seq", 1)


def y_swap(value):
    return hop(value, "seq", 2)


def sum_small(full):
    size = lax.axis_size("fsdp")
    me = lax.axis_index("fsdp")
    full = full + y_swap(full)
    full = full + core_swap(full)
    slots = jnp.take(full, me ^ jnp.arange(size), axis=0)
    slots = slots.reshape((size // 2, 2) + full.shape[1:])
    slots = slots[:, 0] + hop(slots[:, 1], "fsdp", 1)
    total = slots[0]
    for k in range(1, size // 2):
        total = total + hop(slots[k], "fsdp", 2 * k)
    return total


def assemble_kernel(column, stride, key_ref, same, other, out, held, sems):
    key = key_ref[0]
    pairs, rows, width = held.shape[0] // 2, held.shape[1], held.shape[2]
    loads, stores = [], []
    for r in range(2 * pairs):
        place = pl.ds(r // 2 * stride, rows)
        source = (other if r % 2 else same).at[place, pl.ds(column, width)]
        loads.append(pltpu.make_async_copy(source, held.at[r], sems.at[r, 0]))
        start = pl.multiple_of((r ^ key) * rows, rows)
        target = out.at[pl.ds(start, rows), :]
        stores.append(pltpu.make_async_copy(held.at[r], target, sems.at[r, 1]))
    for load in loads:
        load.start()
    for load, store in zip(loads, stores):
        load.wait()
        store.start()
    for store in stores:
        store.wait()


def assemble(halves, column, width, rows, key):
    slots = lax.axis_size("fsdp")
    stride = 2 * halves[0].shape[0] // slots
    key = key.astype(jnp.int32).reshape(1)
    hbm = pl.BlockSpec(memory_space=pl.ANY)
    return pl.pallas_call(
        functools.partial(assemble_kernel, column, stride),
        grid_spec=pltpu.PrefetchScalarGridSpec(
            num_scalar_prefetch=1,
            grid=(),
            in_specs=[hbm] * 2,
            out_specs=hbm,
            scratch_shapes=[
                pltpu.VMEM((slots, rows, width), BF),
                pltpu.SemaphoreType.DMA((slots, 2)),
            ],
        ),
        out_shape=jax.ShapeDtypeStruct((slots * rows, width), BF),
        compiler_params=pltpu.CompilerParams(vmem_limit_bytes=32 << 20),
        cost_estimate=pl.CostEstimate(flops=0, bytes_accessed=0, transcendentals=0),
        name="assemble",
    )(key, *halves)


def tied(value, after):
    return lax.optimization_barrier((value, after))[0]


def meet(*values):
    return lax.optimization_barrier(values)


def pack_kernel(names, layer, place, *refs):
    sources, (out, sems) = dict(zip(names, refs)), refs[len(names) :]
    run = place[0]
    copies = []
    column = 0

    def add(source, size, rows=None):
        rows = source.shape[0] if rows is None else rows
        target = out.at[pl.ds(0, rows), pl.ds(column, size)]
        copies.append(pltpu.make_async_copy(source, target, sems.at[len(copies)]))
        return column + size

    for name in names:
        source = sources[name]
        if name == "small":
            rows = source.shape[0]
            target = out.at[pl.ds(out.shape[0] - rows, rows), :]
            copies.append(pltpu.make_async_copy(source, target, sems.at[len(copies)]))
            continue
        source = source.at[layer]
        part, width = source.shape
        if name == "qkv":
            for third in range(3):
                start = pl.multiple_of((4 * third + run) * (width // 12), width // 12)
                column = add(source.at[:, pl.ds(start, width // 12)], width // 12)
        elif name == "out":
            start = pl.multiple_of(run % 2 * (width // 2), width // 2)
            column = add(source.at[:, pl.ds(start, width // 2)], width // 2)
        elif name == "up":
            piece = part
            for slot in range(width // (4 * piece)):
                start = pl.multiple_of((4 * slot + run) * piece, piece)
                column = add(source.at[:, pl.ds(start, piece)], piece)
        else:
            start = pl.multiple_of(run * (part // 4), part // 4)
            column = add(source.at[pl.ds(start, part // 4), :], width)
    for copy in copies:
        copy.start()
    for copy in copies:
        copy.wait()


def pack(names, arrays, layer, place, rows, columns):
    count = sum({"qkv": 3, "up": arrays[0].shape[-1]}.get(name, 1) for name in names)
    hbm = pl.BlockSpec(memory_space=pl.ANY)
    return pl.pallas_call(
        functools.partial(pack_kernel, names, layer),
        in_specs=[SMEM] + [hbm] * len(arrays),
        out_specs=VMEM,
        out_shape=jax.ShapeDtypeStruct((rows, columns), BF),
        scratch_shapes=[pltpu.SemaphoreType.DMA((min(count, 64),))],
        compiler_params=pltpu.CompilerParams(vmem_limit_bytes=32 << 20),
        cost_estimate=pl.CostEstimate(flops=0, bytes_accessed=0, transcendentals=0),
        name="pack",
    )(place, *arrays)


def z_groups():
    size = lax.axis_size("fsdp")
    return [[x + 2 * k for k in range(size // 2)] for x in range(2)]


def gather_z(own):
    return lax.all_gather(own, "fsdp", axis=0, tiled=True, axis_index_groups=z_groups())


def x_swap(value):
    return hop(value, "fsdp", 1)


def added(same, received):
    return (same.astype(F32) + received.astype(F32)).astype(BF)


def scatter_z(same):
    return lax.psum_scatter(
        same, "fsdp", scatter_dimension=0, tiled=True, axis_index_groups=z_groups()
    )


def four(total):
    across = y_swap(total)
    return total, core_swap(total), across, core_swap(across)


def staged(body, held, refs):
    count = len(held)
    inputs, rest = refs[:count], refs[count:]
    places = [i for i in range(count) if held[i]]
    sems, buffers, rest = rest[-1], rest[-1 - len(places) : -1], rest[: -1 - len(places)]
    copies = [
        pltpu.make_async_copy(inputs[i], buffer, sems.at[number])
        for number, (i, buffer) in enumerate(zip(places, buffers))
    ]
    for copy in copies:
        copy.start()
    for copy in copies:
        copy.wait()
    inputs = list(inputs)
    for i, buffer in zip(places, buffers):
        inputs[i] = buffer
    body(*inputs, *rest)


def kernel_call(body, name, inputs, outputs, scratch=(), in_specs=None):
    held = [spec is VMEM for spec in in_specs or [VMEM] * len(inputs)]
    buffers = [pltpu.VMEM(item.shape, item.dtype) for item, one in zip(inputs, held) if one]
    return pl.pallas_call(
        lambda *refs: staged(body, held, refs),
        in_specs=[pl.BlockSpec(memory_space=pl.ANY) if one else SMEM for one in held],
        out_specs=[VMEM] * len(outputs),
        out_shape=[jax.ShapeDtypeStruct(shape, kind) for shape, kind in outputs],
        scratch_shapes=[*scratch, *buffers, pltpu.SemaphoreType.DMA((max(len(buffers), 1),))],
        compiler_params=pltpu.CompilerParams(vmem_limit_bytes=48 << 20),
        cost_estimate=pl.CostEstimate(flops=0, bytes_accessed=0, transcendentals=0),
        name=name,
    )(*inputs)


def nn(left, right):
    return jnp.dot(left, right, preferred_element_type=F32)


def nt(left, right):
    return lax.dot_general(left, right, (((1,), (1,)), ((), ())), preferred_element_type=F32)


def tn(left, right):
    return lax.dot_general(left, right, (((0,), (0,)), ((), ())), preferred_element_type=F32)


def normalized(value):
    center = value - jnp.mean(value, axis=-1, keepdims=True)
    scale = lax.rsqrt(jnp.mean(center * center, axis=-1, keepdims=True) + EPS)
    return center * scale, scale


def norm_back(value, gain, grad):
    hat, scale = normalized(value)
    inner = grad * gain
    mean = jnp.mean(inner, axis=-1, keepdims=True)
    along = jnp.mean(inner * hat, axis=-1, keepdims=True)
    grad_gain = jnp.sum(grad * hat, axis=0, keepdims=True)
    return scale * (inner - mean - hat * along), grad_gain, jnp.sum(grad, axis=0, keepdims=True)


GAIN_ONE, SHIFT_ONE, BIAS_Q, BIAS_V, BIAS_OUT, GAIN_TWO, SHIFT_TWO, BIAS_DOWN = range(8)


def row(table, index):
    return table[index : index + 1, :]


def first_norm_kernel(a, b, c, d, table, *outs):
    for value, out in zip((a, b, c, d), outs):
        hat, _ = normalized(value[...].astype(F32))
        out[...] = (hat * row(table, GAIN_ONE) + row(table, SHIFT_ONE)).astype(BF)


def first_norm(blocks, table):
    outs = [(item.shape, BF) for item in blocks]
    return kernel_call(first_norm_kernel, "first_norm", (*blocks, table), outs)


def layer_end_kernel(middle, keep, beside, across, table, after, stream, normed):
    total = keep[...] + beside[...].astype(F32) + across[...].astype(F32)
    value = middle[...] + (total + row(table, BIAS_DOWN))
    stream[...] = value
    if after is None:
        normed[...] = value.astype(BF)
    else:
        hat, _ = normalized(value)
        normed[...] = (hat * row(after, GAIN_ONE) + row(after, SHIFT_ONE)).astype(BF)


def last_end_kernel(middle, keep, beside, across, table, stream, low):
    layer_end_kernel(middle, keep, beside, across, table, None, stream, low)


def layer_end(middle, sums, table, after):
    outs = [(middle.shape, F32), (middle.shape, BF)]
    if after is None:
        return kernel_call(last_end_kernel, "last_end", (middle, *sums, table), outs)
    return kernel_call(layer_end_kernel, "layer_end", (middle, *sums, table, after), outs)


def out_kernel(
    scalars, own, beside, across, w_own, w_other, stream, table, middle, normed, attended
):
    run = scalars[0]
    core = run % 2
    parts = [own[...], beside[0], across[0], beside[1]]
    size = parts[0].shape[1]
    starts = [pl.multiple_of((run ^ j) * size, size) for j in range(4)]
    for part, start in zip(parts, starts):
        attended[:, pl.ds(start, size)] = part
    half = w_own.shape[1]
    for weight, place in ((w_own, core), (w_other, 1 - core)):
        total = None
        for part, start in zip(parts, starts):
            term = nn(part, weight[pl.ds(start, size), :])
            total = term if total is None else total + term
        lanes = pl.ds(pl.multiple_of(place * half, half), half)
        bias = table[BIAS_OUT : BIAS_OUT + 1, lanes]
        middle[:, lanes] = stream[:, lanes] + (total + bias)
    hat, _ = normalized(middle[...])
    normed[...] = (hat * row(table, GAIN_TWO) + row(table, SHIFT_TWO)).astype(BF)


def out_step(scalars, own, beside, across, w_outs, stream, table):
    outs = [(stream.shape, F32), (stream.shape, BF), (stream.shape, BF)]
    inputs = (scalars, own, beside, across, *w_outs, stream, table)
    return kernel_call(out_kernel, "out_step", inputs, outs, in_specs=[SMEM] + [VMEM] * 7)


def ffn_kernel(a, b, w_up, bias, w_down, act, slope, keep, send, source):
    rows = a.shape[0]
    source[:rows, :] = a[...]
    source[rows:, :] = b[...]
    pre = nn(source[...], w_up[...]) + bias[...]
    square = pre * pre
    bent = jnp.tanh(GELU * pre * (1.0 + CUBIC * square))
    half = 0.5 + 0.5 * bent
    value = (pre * half).astype(BF)
    act[...] = value
    rise = half + (0.5 * GELU) * pre * (1.0 - bent * bent) * (1.0 + 3.0 * CUBIC * square)
    slope[...] = rise.astype(BF)
    total = nn(value, w_down[...])
    keep[...] = total[:rows, :]
    send[...] = total[rows:, :].astype(BF)


def ffn(a, b, w_up, bias, w_down):
    rows, width = a.shape
    hidden = w_up.shape[1]
    outs = [
        ((2 * rows, hidden), BF),
        ((2 * rows, hidden), BF),
        ((rows, width), F32),
        ((rows, width), BF),
    ]
    scratch = [pltpu.VMEM((2 * rows, width), BF)]
    return kernel_call(ffn_kernel, "ffn", (a, b, w_up, bias, w_down), outs, scratch)


def ffn_back_kernel(a, b, slope, w_up, w_down, grad_pre, keep, send, sums, source):
    rows = a.shape[0]
    source[:rows, :] = a[...]
    source[rows:, :] = b[...]
    grad_act = nt(source[...], w_down[...])
    value = (grad_act * slope[...].astype(F32)).astype(BF)
    grad_pre[...] = value
    sums[...] = jnp.sum(value.astype(F32), axis=0, keepdims=True)
    total = nt(value, w_up[...])
    keep[...] = total[:rows, :]
    send[...] = total[rows:, :].astype(BF)


def ffn_back(a, b, slope, w_up, w_down):
    rows, width = a.shape
    hidden = w_up.shape[1]
    outs = [
        ((2 * rows, hidden), BF),
        ((rows, width), F32),
        ((rows, width), BF),
        ((1, hidden), F32),
    ]
    scratch = [pltpu.VMEM((2 * rows, width), BF)]
    return kernel_call(ffn_back_kernel, "ffn_back", (a, b, slope, w_up, w_down), outs, scratch)


def weight_grad_kernel(count, parts, scalars, *refs):
    x = scalars[1]
    lefts, rights = refs[: parts[0]], refs[parts[0] : parts[0] + parts[1]]
    same, other, left, right, total = refs[parts[0] + parts[1] :]
    for sources, target in ((lefts, left), (rights, right)):
        start = 0
        for source in sources:
            target[start : start + source.shape[0], :] = source[...]
            start += source.shape[0]
    total[...] = tn(left[...], right[...]).astype(BF)
    rows = total.shape[0] // count
    for r in range(count):
        start = pl.multiple_of((r ^ x) * rows, rows)
        target = other if r % 2 else same
        target[r // 2 * rows : (r // 2 + 1) * rows, :] = total[pl.ds(start, rows), :]


def weight_grad(lefts, rights, place):
    count = lax.axis_size("fsdp")
    total = sum(item.shape[0] for item in lefts)
    tall, wide = lefts[0].shape[1], rights[0].shape[1]
    outs = [((tall // 2, wide), BF)] * 2
    scratch = [
        pltpu.VMEM((total, tall), BF),
        pltpu.VMEM((total, wide), BF),
        pltpu.VMEM((tall, wide), BF),
    ]
    inputs = (place, *lefts, *rights)
    body = functools.partial(weight_grad_kernel, count, (len(lefts), len(rights)))
    specs = [SMEM] + [VMEM] * (len(inputs) - 1)
    return kernel_call(body, "weight_grad", inputs, outs, scratch, specs)


def out_grad_kernel(count, place, left, right, keep, send, total):
    core, x = place[0] % 2, place[1]
    half = keep.shape[2]
    rows = total.shape[0] // count
    for target, number in ((keep, core), (send, 1 - core)):
        lanes = pl.ds(pl.multiple_of(number * half, half), half)
        total[...] = tn(left[...], right[:, lanes]).astype(BF)
        for r in range(count):
            start = pl.multiple_of((r ^ x) * rows, rows)
            target[r % 2, r // 2 * rows : (r // 2 + 1) * rows, :] = total[pl.ds(start, rows), :]


def out_grad(left, right, place):
    count = lax.axis_size("fsdp")
    tall, wide = left.shape[1], right.shape[1]
    outs = [((2, tall // 2, wide // 2), BF)] * 2
    scratch = [pltpu.VMEM((tall, wide // 2), BF)]
    body = functools.partial(out_grad_kernel, count)
    return kernel_call(
        body, "out_grad", (place, left, right), outs, scratch, [SMEM, VMEM, VMEM]
    )


def finish_kernel(layout, slots, aliased, place, *refs):
    run = place[0]
    groups = []
    for number in range(layout[-1]):
        groups.append(refs[4 * number : 4 * number + 4])
    refs = refs[4 * layout[-1] + aliased :]
    qkv, out, up, down = refs
    part, width = out.shape[1], out.shape[2]
    mine, half, size = width // 4, width // 2, up.shape[2] // 4
    piece = size // slots
    (q_group, q_start), (o_group, o_start), (u_group, u_start), (d_group, d_start) = layout[0]
    for j in range(4):
        owner = run ^ j
        for third in range(3):
            lanes = pl.ds(pl.multiple_of(third * width + owner * mine, mine), mine)
            start = q_start + third * mine
            qkv[0, :, lanes] = groups[q_group][j][:, start : start + mine].astype(F32)
        if piece % 128:
            lanes = pl.ds(pl.multiple_of(owner * size, size), size)
            up[0, :, lanes] = groups[u_group][j][:, u_start : u_start + size].astype(F32)
        else:
            for slot in range(slots):
                lanes = pl.ds(pl.multiple_of((4 * slot + owner) * piece, piece), piece)
                start = u_start + slot * piece
                up[0, :, lanes] = groups[u_group][j][:, start : start + piece].astype(F32)
        rows = pl.ds(pl.multiple_of(owner * part, part), part)
        down[0, rows, :] = groups[d_group][j][:, d_start : d_start + width].astype(F32)
    for j in range(2):
        lanes = pl.ds(pl.multiple_of((run ^ j) % 2 * half, half), half)
        columns = slice(o_start, o_start + half)
        first, second = groups[o_group][j][:, columns], groups[o_group][j + 2][:, columns]
        out[0, :, lanes] = first.astype(F32) + second.astype(F32)


def finish(layer, layers, groups, starts, place, before):
    slots = lax.axis_size("fsdp")
    part = groups[0][0].shape[0]
    width = part * slots
    shapes = [(part, 3 * width), (part, width), (part, 4 * width), (4 * part, width)]
    inputs = [place] + [item for group in groups for item in group]
    count = len(inputs)
    specs = [SMEM] + [VMEM] * (count - 1)
    aliases = {}
    if before is not None:
        inputs += before
        specs += [pl.BlockSpec(memory_space=pl.ANY)] * 4
        aliases = {count + i: i for i in range(4)}
    layout = (starts, len(groups))
    return pl.pallas_call(
        functools.partial(finish_kernel, layout, slots, len(aliases)),
        grid=(1,),
        in_specs=specs,
        out_specs=[pl.BlockSpec((1,) + shape, lambda i: (layer, 0, 0)) for shape in shapes],
        out_shape=[jax.ShapeDtypeStruct((layers,) + shape, F32) for shape in shapes],
        input_output_aliases=aliases,
        compiler_params=pltpu.CompilerParams(vmem_limit_bytes=48 << 20),
        cost_estimate=pl.CostEstimate(flops=0, bytes_accessed=0, transcendentals=0),
        name="finish",
    )(*inputs)


def out_back_kernel(
    scalars,
    keep,
    beside,
    across,
    middle,
    grad,
    table,
    w_own,
    w_other,
    grad_middle,
    branch,
    own,
    near,
    far,
    sums,
):
    run = scalars[0]
    core = run % 2
    total = keep[...] + beside[...].astype(F32) + across[...].astype(F32)
    value, grad_gain, grad_shift = norm_back(middle[...], row(table, GAIN_TWO), total)
    value = grad[...] + value
    grad_middle[...] = value
    low = value.astype(BF)
    branch[...] = low
    sums[...] = jnp.zeros_like(sums)
    sums[0:1, :] = grad_gain
    sums[1:2, :] = grad_shift
    sums[2:3, :] = jnp.sum(low.astype(F32), axis=0, keepdims=True)
    sums[3:4, :] = jnp.sum(grad[...].astype(BF).astype(F32), axis=0, keepdims=True)
    size = own.shape[1]
    half = w_own.shape[1]
    for j in range(4):
        rows = pl.ds(pl.multiple_of((run ^ j) * size, size), size)
        result = None
        for weight, place in ((w_own, core), (w_other, 1 - core)):
            lanes = pl.ds(pl.multiple_of(place * half, half), half)
            term = nt(branch[:, lanes], weight[rows, :])
            result = term if result is None else result + term
        result = result.astype(BF)
        if j == 0:
            own[...] = result
        elif j == 2:
            far[...] = result
        else:
            near[j // 2] = result


def out_back(scalars, sums, middle, grad, table, w_outs):
    rows, width = middle.shape
    mine = width // 4
    outs = [
        ((rows, width), F32),
        ((rows, width), BF),
        ((rows, mine), BF),
        ((2, rows, mine), BF),
        ((rows, mine), BF),
        ((8, width), F32),
    ]
    inputs = (scalars, *sums, middle, grad, table, *w_outs)
    return kernel_call(out_back_kernel, "out_back", inputs, outs, in_specs=[SMEM] + [VMEM] * 8)


def layer_begin_kernel(
    keep, beside, across, stream, grad_middle, table, grad, low, sums
):
    total = keep[...] + beside[...].astype(F32) + across[...].astype(F32)
    value, grad_gain, grad_shift = norm_back(stream[...], row(table, GAIN_ONE), total)
    value = grad_middle[...] + value
    grad[...] = value
    low[...] = value.astype(BF)
    sums[...] = jnp.zeros_like(sums)
    sums[0:1, :] = grad_gain
    sums[1:2, :] = grad_shift


def layer_begin(sums, stream, grad_middle, table):
    shape = stream.shape
    outs = [(shape, F32), (shape, BF), ((8, shape[1]), F32)]
    return kernel_call(
        layer_begin_kernel, "layer_begin", (*sums, stream, grad_middle, table), outs
    )


def halves(value, head):
    lane = lax.broadcasted_iota(jnp.int32, value.shape, 1)
    return jnp.where((lane >= HEAD_DIM) == (head == 1), value, jnp.zeros_like(value))


def masked_scores(keys, query, i, j, slope, offsets, length):
    scores = nt(keys, query)
    if i == j:
        scores = scores - slope * jnp.abs(offsets)
    else:
        scores = scores - (slope * offsets + slope * float((i - j) * BLOCK))
    if j == 0:
        return scores, None
    return scores, j * BLOCK + lax.broadcasted_iota(jnp.int32, scores.shape, 0) < length


def block(i):
    return slice(i * BLOCK, (i + 1) * BLOCK)


def distances(ref):
    shape = (BLOCK, BLOCK)
    offsets = lax.broadcasted_iota(jnp.int32, shape, 1) - lax.broadcasted_iota(jnp.int32, shape, 0)
    ref[...] = offsets.astype(F32)


def attend_kernel(
    scalars, slopes, a, b, c, d, w_qkv, bias, nat, att, own, near, far, lse, low, scores, offsets
):
    run, length = scalars[0], scalars[1]
    blocks = nat.shape[0] // BLOCK
    mine = nat.shape[1] // 3
    for j, rows in enumerate((a, b, c, d)):
        place = pl.ds(pl.multiple_of((run ^ j) * BLOCK, BLOCK), BLOCK)
        nat[place, :] = (nn(rows[...], w_qkv[...]) + bias[...]).astype(BF)
    distances(offsets)
    for i in range(blocks):
        for pair in range(mine // 128):
            lanes = slice(pair * 128, (pair + 1) * 128)
            out = jnp.zeros((128, BLOCK), F32)
            for head in range(2):
                slope = slopes[pair * 2 + head]
                query = halves(nat[block(i), lanes], head) * jnp.asarray(HEAD_DIM**-0.5, BF)
                top = None
                for j in range(i + 1):
                    keys = nat[block(j), mine + pair * 128 : mine + (pair + 1) * 128]
                    tile, seen = masked_scores(keys, query, i, j, slope, offsets[...], length)
                    if seen is not None:
                        tile = jnp.where(seen, tile, NEG)
                    scores[block(j), :] = tile
                    tile_top = jnp.max(tile, axis=0, keepdims=True)
                    top = tile_top if top is None else jnp.maximum(top, tile_top)
                total = jnp.zeros((1, BLOCK), F32)
                summed = jnp.zeros((128, BLOCK), F32)
                for j in range(i + 1):
                    weights = jnp.exp(scores[block(j), :] - top)
                    total = total + jnp.sum(weights, axis=0, keepdims=True)
                    values = nat[block(j), 2 * mine + pair * 128 : 2 * mine + (pair + 1) * 128]
                    summed = summed + tn(halves(values, head), weights.astype(BF))
                out = out + summed / total
                lse[pair * 2 + head : pair * 2 + head + 1, block(i)] = top + jnp.log(total)
            rows = jnp.transpose(out)
            att[block(i), lanes] = rows
            low[run ^ i, :, lanes] = rows.astype(BF)
    own[...] = low[0]
    near[...] = low[1]
    far[...] = low[2:4]


def attend_back_kernel(
    scalars,
    slopes,
    nat,
    own,
    beside,
    across,
    att,
    lse,
    w_qkv,
    out,
    near_keep,
    near_send,
    far_keep,
    far_send,
    sums,
    nat_grad,
    grad_q,
    grad_k,
    grad_v,
    offsets,
):
    run, length = scalars[0], scalars[1]
    blocks = nat.shape[0] // BLOCK
    mine = nat.shape[1] // 3
    for j, rows in enumerate((own[...], beside[0], across[0], across[1])):
        place = pl.ds(pl.multiple_of((run ^ j) * BLOCK, BLOCK), BLOCK)
        nat_grad[place, :] = rows
    distances(offsets)
    grad_k[...] = jnp.zeros_like(grad_k)
    grad_v[...] = jnp.zeros_like(grad_v)
    scale = jnp.asarray(HEAD_DIM**-0.5, BF)
    for pair in range(mine // 128):
        lanes = slice(pair * 128, (pair + 1) * 128)
        k_lanes = slice(mine + pair * 128, mine + (pair + 1) * 128)
        v_lanes = slice(2 * mine + pair * 128, 2 * mine + (pair + 1) * 128)
        for i in range(blocks):
            grad_rows = nat_grad[block(i), lanes]
            product = grad_rows.astype(F32) * att[block(i), lanes]
            ones = lax.broadcasted_iota(jnp.int32, (8, 128), 1) // HEAD_DIM
            ones = (ones == lax.broadcasted_iota(jnp.int32, (8, 128), 0)).astype(F32)
            delta = lax.dot_general(
                ones,
                product,
                (((1,), (1,)), ((), ())),
                precision=lax.Precision.HIGHEST,
                preferred_element_type=F32,
            )
            sum_q = jnp.zeros((128, BLOCK), F32)
            for head in range(2):
                number = pair * 2 + head
                slope = slopes[number]
                query = halves(nat[block(i), lanes], head) * scale
                grad_head = halves(grad_rows, head)
                row_lse = lse[number : number + 1, block(i)]
                row_delta = delta[head : head + 1, :]
                for j in range(i + 1):
                    keys = nat[block(j), k_lanes]
                    tile, seen = masked_scores(keys, query, i, j, slope, offsets[...], length)
                    probs = jnp.exp(tile - row_lse)
                    if seen is not None:
                        probs = jnp.where(seen, probs, 0.0)
                    grad_probs = nt(nat[block(j), v_lanes], grad_head)
                    grad_scores = (probs * (grad_probs - row_delta)).astype(BF)
                    grad_v[block(j), lanes] += nn(probs.astype(BF), grad_head)
                    grad_k[block(j), lanes] += nn(grad_scores, query)
                    sum_q = sum_q + tn(halves(keys, head), grad_scores)
            grad_q[block(i), lanes] = (jnp.transpose(sum_q) * HEAD_DIM**-0.5).astype(BF)
    sums[...] = jnp.zeros_like(sums)
    for j in range(4):
        place = pl.ds(pl.multiple_of((run ^ j) * BLOCK, BLOCK), BLOCK)
        out[block(j), :mine] = grad_q[place, :]
        out[block(j), mine : 2 * mine] = grad_k[place, :].astype(BF)
        out[block(j), 2 * mine :] = grad_v[place, :].astype(BF)
        rows = out[block(j), :]
        sums[0:1, :] += jnp.sum(rows.astype(F32), axis=0, keepdims=True)
        partial = nt(rows, w_qkv[...])
        if j == 0:
            near_keep[...] = partial
        elif j == 1:
            near_send[...] = partial.astype(BF)
        elif j == 2:
            far_keep[...] = partial
        else:
            far_send[...] = partial.astype(BF)


def attend(blocks, w_qkv, bias, scalars, slopes):
    rows, width = blocks[0].shape
    columns = w_qkv.shape[1]
    mine = columns // 3
    outs = [
        ((4 * rows, columns), BF),
        ((4 * rows, mine), F32),
        ((rows, mine), BF),
        ((rows, mine), BF),
        ((2, rows, mine), BF),
        ((8, 4 * rows), F32),
    ]
    scratch = [
        pltpu.VMEM((4, rows, mine), BF),
        pltpu.VMEM((4 * rows, BLOCK), F32),
        pltpu.VMEM((BLOCK, BLOCK), F32),
    ]
    inputs = (scalars, slopes, *blocks, w_qkv, bias)
    specs = [SMEM, SMEM] + [VMEM] * 6
    return kernel_call(attend_kernel, "attend", inputs, outs, scratch, specs)


def attend_back(nat, own, beside, across, att, lse, w_qkv, scalars, slopes):
    total, columns = nat.shape
    rows, mine = total // 4, columns // 3
    width = w_qkv.shape[0]
    outs = [
        ((total, columns), BF),
        ((rows, width), F32),
        ((rows, width), BF),
        ((rows, width), F32),
        ((rows, width), BF),
        ((8, columns), F32),
    ]
    scratch = [
        pltpu.VMEM((total, mine), BF),
        pltpu.VMEM((total, mine), BF),
        pltpu.VMEM((total, mine), F32),
        pltpu.VMEM((total, mine), F32),
        pltpu.VMEM((BLOCK, BLOCK), F32),
    ]
    inputs = (scalars, slopes, nat, own, beside, across, att, lse, w_qkv)
    specs = [SMEM, SMEM] + [VMEM] * 7
    return kernel_call(attend_back_kernel, "attend_back", inputs, outs, scratch, specs)


def shards(
    tokens,
    lengths,
    cotangent,
    ln1_gain,
    ln1_bias,
    qkv_weight,
    query_bias,
    value_bias,
    out_weight,
    out_bias,
    ln2_gain,
    ln2_bias,
    up_weight,
    up_bias,
    down_weight,
    down_bias,
):
    fsdp = lax.axis_size("fsdp")
    run = lax.axis_index("seq")
    rows, width = tokens.shape[1:]
    hidden = up_weight.shape[2]
    heads = HEADS // 4
    mine = width // 4
    half = width // 2
    ffn_size = hidden // 4
    part = width // fsdp
    piece = hidden // fsdp // 4
    me = lax.axis_index("fsdp")
    scalars = jnp.stack([run.astype(jnp.int32), lengths[0]])
    place = jnp.stack([run, me % 2]).astype(jnp.int32)
    slopes = lax.dynamic_slice_in_dim(head_slopes(), run * heads, heads)

    def quarter(value, axis):
        size = value.shape[axis] // 4
        return lax.dynamic_slice_in_dim(value, run * size, size, axis)

    def core_half(value, axis):
        return lax.dynamic_slice_in_dim(value, (run % 2) * half, half, axis)

    def qkv_of(layer):
        return quarter(qkv_weight[layer].reshape(part, 3, width), 2).reshape(part, 3 * mine)

    def out_of(layer):
        return core_half(out_weight[layer], 1)

    def up_of(layer):
        return quarter(up_weight[layer].reshape(part, fsdp, -1), 2).reshape(part, ffn_size)

    def down_of(layer):
        return quarter(down_weight[layer], 0)

    def seq_blocks(own):
        across = y_swap(own)
        return [own, core_swap(own), across, core_swap(across)]

    def summed(near, far):
        far = far_sum(far)
        return near[0], core_swap(near[1]), y_swap(far)

    def far_sum(far):
        return (far[0] + core_swap(far[1]).astype(F32)).astype(BF)

    vectors = (ln1_gain, ln1_bias, query_bias, value_bias, out_bias, ln2_gain, ln2_bias, down_bias)
    small = jnp.concatenate([jnp.stack(vectors, 1).reshape(LAYERS, -1), up_bias], axis=1)
    columns = 3 * mine
    extra = small.size // columns
    small = jnp.pad(small.reshape(extra, columns), ((0, -extra % 16), (0, 0)))
    stride = part + small.shape[0]
    own = pack(["qkv", "small"], [qkv_weight, small], 0, place, stride, columns)
    token_blocks = seq_blocks(tokens[0])
    even = [own] + [hop(own, "fsdp", 2 * k) for k in range(1, fsdp // 2)]
    first = jnp.concatenate(even)
    first = (first, x_swap(first))
    cot_blocks = seq_blocks(tied(cotangent[0], token_blocks[2]))
    token_blocks, cot_blocks, first = meet(token_blocks, cot_blocks, first)
    arrays = dict(qkv=qkv_weight, out=out_weight, up=up_weight, down=down_weight)
    sizes = dict(qkv=columns, out=half, up=ffn_size, down=width)

    def bundle(layer, names):
        if part % 128:
            parts = dict(qkv=qkv_of, out=out_of, up=up_of, down=down_of)
            return jnp.concatenate([parts[name](layer) for name in names], axis=1)
        total = sum(sizes[name] for name in names)
        return pack(names, [arrays[name] for name in names], layer, place, part, total)

    packs = [
        bundle(0, ["out", "up"]),
        bundle(0, ["down"]),
        bundle(1, ["qkv", "out"]),
        bundle(1, ["up", "down"]),
    ]
    token_blocks = tied(token_blocks, packs)
    early_one, late_one, early_two, late_two = (gather_z(item) for item in packs)

    def matrix(halves, column, size, key=me % 2):
        return assemble(halves, column, size, part, key)

    small = [item.reshape(fsdp // 2, stride, columns)[:, part : part + extra] for item in first]
    small = jnp.stack(small, 1).reshape(fsdp, LAYERS, -1)
    small = jnp.take(small, me ^ jnp.arange(fsdp), axis=0).astype(F32)
    tables, biases = [], []
    for layer in range(LAYERS):
        table = small[:, layer, : 8 * part].reshape(fsdp, 8, part)
        table = jnp.transpose(table, (1, 0, 2)).reshape(8, width)
        bias_q, bias_v = quarter(table[BIAS_Q], 0), quarter(table[BIAS_V], 0)
        bias_qkv = jnp.concatenate([bias_q, jnp.zeros_like(bias_q), bias_v])
        bias_up = quarter(small[:, layer, 8 * part :], 1)
        tables.append(table)
        biases.append((bias_qkv.reshape(1, -1), bias_up.reshape(1, -1)))

    stream = tokens[0].astype(F32)
    h1 = first_norm(token_blocks, tables[0])
    w_qkv = assemble(first, 0, columns, part, me)
    moved = x_swap(tied(early_one, first))
    saved, weights = [], []
    for layer in range(LAYERS):
        top = layer + 1 == LAYERS
        bias_qkv, bias_up = biases[layer]
        packed, attended, own, near, far, lse = attend(h1, w_qkv, bias_qkv, scalars, slopes)
        across = y_swap(far)
        if top:
            across, moved = meet(across, moved)
            late_two = (late_two, moved)
            w_out = matrix(early_two, columns, half)
            w_up, w_down = matrix(late_two, 0, ffn_size), matrix(late_two, ffn_size, width)
        else:
            across, moved, late_one = meet(across, moved, late_one)
            early_one = (early_one, moved)
            w_out, w_up = matrix(early_one, 0, half), matrix(early_one, half, ffn_size)
            moved = x_swap(late_one)
        beside = core_swap(jnp.stack([near, across[1]]))
        w_outs = (w_out, core_swap(w_out))
        middle, normed, att_own = out_step(
            scalars, own, beside, across, w_outs, stream, tables[layer]
        )
        h2 = seq_blocks(normed)
        if not top:
            h2[2], moved, early_two = meet(h2[2], moved, early_two)
            w_down = matrix((late_one, moved), 0, width)
            moved = x_swap(early_two)
            h2[3] = core_swap(h2[2])
        near = ffn(h2[0], h2[1], w_up, bias_up, w_down)
        if top:
            h2[2], near = meet(h2[2], near)
            h2[3] = core_swap(h2[2])
        far = ffn(h2[2], h2[3], w_up, bias_up, w_down)
        saved.append((stream, h1, packed, attended, lse, att_own, middle, h2, near[:2], far[:2]))
        weights.append((w_qkv, w_outs, w_up, w_down))
        if top:
            last_sums = near[2:], far[2:]
        else:
            sums, moved, late_two = meet(summed(near[2:], far[2:]), moved, late_two)
            early_two = (early_two, moved)
            w_qkv = matrix(early_two, 0, columns)
            moved = x_swap(late_two)
            stream, normed = layer_end(middle, sums, tables[layer], tables[layer + 1])
            h1 = seq_blocks(normed)

    grad = cotangent[0].astype(F32)
    g_down = cot_blocks
    vectors = [None] * LAYERS
    upper, lower = [], []
    waiting = None
    for layer in reversed(range(LAYERS)):
        top = layer + 1 == LAYERS
        totals = upper if top else lower
        w_qkv, w_outs, w_up, w_down = weights[layer]
        stream, h1, packed, attended, lse, att_own, middle, h2, act_near, act_far = saved[layer]
        near = ffn_back(g_down[0], g_down[1], act_near[1], w_up, w_down)
        if not top:
            g_down[2], near, waiting, reduced, upper[1] = meet(
                g_down[2], near, waiting, reduced, upper[1]
            )
            g_down[3] = core_swap(g_down[2])
            reduced = added(*waiting)
            upper.append(scatter_z(reduced))
        far = ffn_back(g_down[2], g_down[3], act_far[1], w_up, w_down)
        far_low = far_sum(far[1:3])
        acts, h2_late = tied(([act_near[0], act_far[0]], h2), far_low if not top else near)
        sent_down = weight_grad(acts, g_down, place)
        moved_down = x_swap(sent_down[1])
        sent_up = weight_grad(h2_late, [near[0], far[0]], place)
        sums = near[1], core_swap(near[2]), y_swap(far_low)
        if not top:
            sums = tied(sums, (reduced, upper[2]))
        sums, sent_up = meet(sums, sent_up)
        moved_up = x_swap(sent_up[1])
        grad_middle, g_branch, own, near_att, far_att, lines_two = out_back(
            scalars, sums, middle, grad, tables[layer], w_outs
        )
        beside = core_swap(near_att)
        across = jnp.stack([far_att, beside[1]])
        att_late, branch_late = tied((att_own, g_branch), across)
        across = y_swap(across)
        keep, send = out_grad(att_late, branch_late, place)
        sent_out = added(keep, core_swap(send))
        across, moved, sent_out = meet(across, moved_down, sent_out)
        reduced = added(sent_down[0], moved)
        totals.append(scatter_z(reduced))
        moved_out = x_swap(sent_out[1])
        if not top:
            across = tied(across, upper[3])
        g_packed, *parts, packed_sum = attend_back(
            packed, own, beside, across, attended, lse, w_qkv, scalars, slopes
        )
        if top:
            one, two = tied(last_sums, across)
            last_sums = summed(one, two)
            parts, moved, last_sums, reduced = meet(parts, moved_up, last_sums, reduced)
            result = layer_end(saved[layer][6], last_sums, tables[layer], None)[1]
        else:
            parts, moved, reduced = meet(parts, moved_up, reduced)
        reduced = added(sent_up[0], moved)
        totals.append(scatter_z(reduced))
        far_low = far_sum(parts[2:])
        sent_qkv = weight_grad(tied(h1, far_low), [g_packed], place)
        sums = parts[0], core_swap(parts[1]), y_swap(far_low)
        sums = tied(sums, (sent_qkv, reduced, totals[0]))
        sums, moved = meet(sums, moved_out)
        reduced = added(sent_out[0], moved)
        totals.append(scatter_z(reduced))
        waiting = sent_qkv[0], x_swap(sent_qkv[1])
        if not top:
            totals.append(scatter_z(added(*waiting)))
        up_sum = near[3] + far[3]
        grad, normed, lines_one = layer_begin(sums, stream, grad_middle, tables[layer])
        if layer:
            g_down = seq_blocks(normed)

        vectors[layer] = (lines_two, lines_two, packed_sum, lines_one, up_sum)

    def spread(value, axis=0):
        shape = list(value.shape)
        size = shape[axis]
        shape[axis] = 4 * size
        return lax.dynamic_update_slice_in_dim(jnp.zeros(shape, F32), value, run * size, axis)

    small_sums = []
    for _, lines_two, packed_sum, lines_one, up_sum in tied(vectors, grad):
        members = [
            lines_one[0],
            lines_one[1],
            spread(packed_sum[0, :mine]),
            spread(packed_sum[0, 2 * mine :]),
            lines_two[2],
            lines_two[0],
            lines_two[1],
            lines_two[3],
        ]
        small_sums.append(
            jnp.concatenate(
                [item.reshape(fsdp, part) for item in members]
                + [spread(up_sum.reshape(fsdp, piece), 1)],
                axis=1,
            )
        )

    upper = [four(item) for item in tied(upper, grad)]
    starts = ((3, 0), (2, 0), (1, 0), (0, 0))
    matrices = finish(1, LAYERS, upper, starts, place, None)
    lower[3] = tied(lower[3], matrices)
    lower = [four(item) for item in lower]
    matrices = finish(0, LAYERS, lower, starts, place, matrices)
    grad_qkv_w, grad_out_w, grad_up_w, grad_down_w = matrices
    if piece % 128:
        grad_up_w = grad_up_w.reshape(LAYERS, part, 4, fsdp, piece)
        grad_up_w = jnp.swapaxes(grad_up_w, 2, 3).reshape(LAYERS, part, hidden)
    vector = sum_small(jnp.stack(small_sums, axis=1))
    lines = [vector[:, i * part : (i + 1) * part] for i in range(8)]
    gain_one, shift_one, bias_q, bias_v, bias_o, gain_two, shift_two, bias_down = lines
    return (
        result[None],
        grad[None],
        gain_one,
        shift_one,
        grad_qkv_w,
        bias_q,
        bias_v,
        grad_out_w,
        bias_o,
        gain_two,
        shift_two,
        grad_up_w,
        vector[:, 8 * part :],
        grad_down_w,
        bias_down,
    )


def solution(mesh):
    vector = P(None, "fsdp")
    matrix = P(None, "fsdp", None)
    data = P("fsdp", "seq", None)
    weight_specs = (
        vector,
        vector,
        matrix,
        vector,
        vector,
        matrix,
        vector,
        vector,
        vector,
        matrix,
        vector,
        matrix,
        vector,
    )
    in_specs = (data, P("fsdp"), data) + weight_specs
    out_specs = (data, data) + weight_specs
    return jax.shard_map(shards, mesh=mesh, in_specs=in_specs, out_specs=out_specs, check_vma=False)
```

time: 1350 us -> 628 us (0.47)
  starting transfers between devices: 355 us -> 56.6 us
  waiting for transfers between devices: 422 us -> 218 us
  Pallas kernels: 0 us -> 183 us
  matrix products: 158 us -> 0 us
  other arithmetic: 152 us -> 34.7 us
  local copies, waits for them, and re-layouts: 200 us -> 107 us
  between operations: 50.9 us -> 17.2 us
    ppermute x101 -> x94, starting transfers between devices: 355 us -> 55.9 us  [hop(): return lax.ppermute(value, axis, [(i, i ^ mask) for i in range(size)])]
    ppermute x101 -> x94, waiting for transfers between devices: 422 us -> 178 us  [hop(): return lax.ppermute(value, axis, [(i, i ^ mask) for i in range(size)])]
    pallas_call x0 -> x44, Pallas kernels: none -> 183 us  [the longest x29 154 us: kernel_call(): pl.pallas_call(lambda *refs: staged(body, held, refs), in_specs=[pl.Block...]
    dot_general x36 -> x0, matrix products: 158 us -> none  [the longest x8 33.4 us: dot_t(): return jnp.einsum('tf,df->td', left, right, preferred_element_type=F32)]
    concatenate x46 -> x3, other arithmetic: 56.1 us -> 0.99 us  [the longest x1 0.97 us: shards(): first = jnp.concatenate(even)]
    concatenate x17 -> x2, local copies, waits for them, and re-layouts: 33.8 us -> 0.01 us  [shards(): jnp.concatenate([item.reshape(fsdp, part) for item in members] + [spread(...]
    all_gather x0 -> x4, waiting for transfers between devices: none -> 27.2 us  [gather_z(): lax.all_gather(own, 'fsdp', axis=0, tiled=True, axis_index_groups=z_group...]
    dynamic_slice x27 -> x5, local copies, waits for them, and re-layouts: 27 us -> 0.38 us  [the longest x4 0.31 us: quarter(): return lax.dynamic_slice_in_dim(value, run * size, size, axis)]
  transfers between devices with their start and end apart: 101 -> 106, of which waited for: 34 -> 47; matrix products, arithmetic and copies ran while one was open for 33% -> 7% of each run, Pallas kernels for 0% -> 24%
where the time goes in v3:
time: 628 us; the launch traced here: 616 us
  waiting for transfers between devices  218 us (35%)
  Pallas kernels  183 us (29%)
  local copies, waits for them, and re-layouts  107 us (17%)
  starting transfers between devices  56.6 us (9%)
  other arithmetic  34.7 us (6%)
  between operations  17.2 us (3%)
    ppermute x94, waiting for transfers between devices, hop(): return lax.ppermute(value, axis, [(i, i ^ mask) for i in range(size)])  178 us
    pallas_call x29, Pallas kernels, kernel_call(): pl.pallas_call(lambda *refs: staged(body, held, refs), in_specs=[pl.Block...  154 us
    unnamed x391, local copies, waits for them, and re-layouts  93.8 us
    ppermute x94, starting transfers between devices, hop(): return lax.ppermute(value, axis, [(i, i ^ mask) for i in range(size)])  55.9 us
    all_gather x4, waiting for transfers between devices, gather_z(): lax.all_gather(own, 'fsdp', axis=0, tiled=True, axis_index_groups=z_group...  27.2 us
    convert_element_type x10, other arithmetic, added(): return (same.astype(F32) + received.astype(F32)).astype(BF)  19.4 us
    reduce_scatter x8, waiting for transfers between devices, scatter_z(): lax.psum_scatter(same, 'fsdp', scatter_dimension=0, tiled=True, axis_inde...  13.2 us
    pallas_call x8, Pallas kernels, assemble(): pl.pallas_call(functools.partial(assemble_kernel, column, stride), grid_s...  13 us
  transfers between devices with their start and end apart: 106, of which 47 were waited for; matrix products, arithmetic and copies ran while one was open for 7% of the time, Pallas kernels for 24%

profile of v3, /device:TPU:0, one launch (start us, length us, event | category | flops | bytes accessed | tf_op | source)
XLA Modules:
  0.0 616.2 jit_solution(16540994173902958776)
XLA Ops:
  29.0 6.2 collective-permute-done.6
  35.1 12.1 %collective-permute-done.7 = bf16[144,768]{1,0:T(8,128)(2,1)S(1)} collective-permute-done((bf16[144,768]{1,0:T(8,128)(2,1)S(1)}, bf16[144,768]{1,0:T(8,128)(2,1)S(1)}, u32[]{:S(2)}, u32[]{:S(2)}) %collective-permute-start.7) | collective-permute-done | bytes 221216 | tf_op jit(solution)/shard_map/ppermute | solution.py:30
  62.9 4.6 collective-permute-done.9.other
  79.1 10.9 %attend.2 = (bf16[1024,768]{1,0:T(8,128)(2,1)S(1)}, f32[1024,256]{1,0:T(8,128)S(1)}, bf16[256,256]{1,0:T(8,128)(2,1)S(1)}, bf16[256,256]{1,0:T(8,128)(2,1)S(1)},...) custom-call(s32[2]{0:T(128)S(1)} %pad_add_fusion.refs_0_, f32[4]{0:T(128)S(1)} %dynamic_slice.21.refs_1_, ...), custom_call_target="tpu_custom_call" | custom-call | tf_op jit(solution)/shard_map/attend/pallas_call | solution.py:214
  120.1 11.4 %all-gather.9.cloned.1.call-done.same = bf16[512,1280]{1,0:T(8,128)(2,1)} async-done(((bf16[128,1280]{1,0:T(8,128)(2,1)}), bf16[512,1280]{1,0:T(8,128)(2,1)}) %all-gather.9.cloned.1.call-update) | async-done | bytes 1310736 | tf_op jit(solution)/shard_map/all_gather | solution.py:170
  131.6 4.8 collective-permute-done.16.other
  146.2 5.6 ffn.5
  155.3 6.2 ffn.4
  165.0 12.9 %all-gather.11.cloned.1.call-done.same = bf16[512,2048]{1,0:T(8,128)(2,1)} async-done(((bf16[128,2048]{1,0:T(8,128)(2,1)}), bf16[512,2048]{1,0:T(8,128)(2,1)}) %all-gather.11.cloned.1.call-update) | async-done | bytes 2097168 | tf_op jit(solution)/shard_map/all_gather | solution.py:170
  177.9 7.1 %collective-permute-done.21.other = bf16[512,1280]{1,0:T(8,128)(2,1)} collective-permute-done((bf16[512,1280]{1,0:T(8,128)(2,1)S(1)}, bf16[512,1280]{1,0:T(8,128)(2,1)}, u32[]{:S(2)}, u32[]{:S(2)}) %collective-permute-start.21) | collective-permute-done | bytes 1310752 | tf_op jit(solution)/shard_map/ppermute | solution.py:30
  191.4 12.7 %collective-permute-done.23.refs_4_.refs_3_ = bf16[256,1024]{1,0:T(8,128)(2,1)S(1)} collective-permute-done((bf16[256,1024]{1,0:T(8,128)(2,1)S(1)}, bf16[256,1024]{1,0:T(8,128)(2,1)S(1)}, u32[]{:S(2)}, u32[]{:S(2)}) %collective-permute-start.23) | collective-permute-done | bytes 524320 | tf_op jit(solution)/shard_map/ppermute | solution.py:30
  210.9 11.3 %attend.3 = (bf16[1024,768]{1,0:T(8,128)(2,1)S(1)}, f32[1024,256]{1,0:T(8,128)S(1)}, bf16[256,256]{1,0:T(8,128)(2,1)S(1)}, bf16[256,256]{1,0:T(8,128)(2,1)S(1)},...) custom-call(s32[2]{0:T(128)S(1)} %pad_add_fusion.refs_0_, f32[4]{0:T(128)S(1)} %dynamic_slice.21.refs_1_, ...), custom_call_target="tpu_custom_call" | custom-call | tf_op jit(solution)/shard_map/attend/pallas_call | solution.py:214
  225.1 7.9 %collective-permute-done.25.refs_3_ = bf16[2,256,256]{2,1,0:T(8,128)(2,1)S(1)} collective-permute-done((bf16[2,256,256]{2,1,0:T(8,128)(2,1)S(1)}, bf16[2,256,256]{2,1,0:T(8,128)(2,1)S(1)}, u32[]{:S(2)}, u32[]{:S(2)}) %collective-permute-start.25) | collective-permute-done | bytes 262176 | tf_op jit(solution)/shard_map/ppermute | solution.py:30
  242.0 5.2 ffn.6
  253.2 5.2 ffn.7
  261.2 4.8 ffn_back.5
  267.3 4.8 ffn_back.4
  274.4 4.5 weight_grad.6
  280.9 5.7 collective-permute-done.34.refs_3_
  301.9 22.6 %collective-permute-done.37 = bf16[512,1024]{1,0:T(8,128)(2,1)S(1)} collective-permute-done((bf16[512,1024]{1,0:T(8,128)(2,1)S(1)}, bf16[512,1024]{1,0:T(8,128)(2,1)S(1)}, u32[]{:S(2)}, u32[]{:S(2)}) %collective-permute-start.37) | collective-permute-done | bytes 1048608 | tf_op jit(solution)/shard_map/ppermute | solution.py:30
  329.7 16.3 %attend_back.2 = (bf16[1024,768]{1,0:T(8,128)(2,1)}, f32[256,1024]{1,0:T(8,128)S(1)}, bf16[256,1024]{1,0:T(8,128)(2,1)S(1)}, f32[256,1024]{1,0:T(8,128)S(1)}, bf...) custom-call(s32[2]{0:T(128)S(1)} %pad_add_fusion.refs_0_, f32[4]{0:T(128)S(1)} %dynamic_slice.21.refs_1_, ...), custom_call_target="tpu_custom_call" | custom-call | tf_op jit(solution)/shard_map/attend_back/pallas_call | solution.py:214
  387.8 4.9 ffn_back.6
  400.8 5.6 ffn_back.7
  419.7 5.7 weight_grad.9
  426.4 13.2 %reduce-scatter.13.cloned.1.call-done.refs_8_ = bf16[128,512]{1,0:T(8,128)(2,1)} async-done(((bf16[512,512]{1,0:T(8,128)(2,1)}), bf16[128,512]{1,0:T(8,128)(2,1)}) %reduce-scatter.13.cloned.1.call-update) | async-done | bytes 131088 | tf_op jit(solution)/shard_map/reduce_scatter | solution.py:182
  440.8 4.7 out_back.3
  454.7 4.5 weight_grad.10
  465.4 19.9 %collective-permute-done.56 = bf16[512,1024]{1,0:T(8,128)(2,1)S(1)} collective-permute-done((bf16[512,1024]{1,0:T(8,128)(2,1)S(1)}, bf16[512,1024]{1,0:T(8,128)(2,1)S(1)}, u32[]{:S(2)}, u32[]{:S(2)}) %collective-permute-start.56) | collective-permute-done | bytes 1048608 | tf_op jit(solution)/shard_map/ppermute | solution.py:30
  489.4 15.8 %attend_back.3 = (bf16[1024,768]{1,0:T(8,128)(2,1)}, f32[256,1024]{1,0:T(8,128)S(1)}, bf16[256,1024]{1,0:T(8,128)(2,1)}, f32[256,1024]{1,0:T(8,128)S(1)}, bf16[2...) custom-call(s32[2]{0:T(128)S(1)} %pad_add_fusion.refs_0_, f32[4]{0:T(128)S(1)} %dynamic_slice.21.refs_1_, ...), custom_call_target="tpu_custom_call" | custom-call | tf_op jit(solution)/shard_map/attend_back/pallas_call | solution.py:214
  562.9 5.2 collective-permute-done.89.refs_14_
  583.1 4.9 finish.2
  594.7 4.5 collective-permute-done.92.refs_14_
  (722 shorter events, 327.3 us)
Async XLA Ops:
  7.2 61.9 %all-gather.5.cloned.1.call-start = ((), (), s32[]{:S(2)}) async-start(), calls=%async_computation.8 | async-start | bytes 1966080 | tf_op jit(solution)/shard_map/all_gather | solution.py:170
  12.1 85.1 %all-gather.7.cloned.1.call-start = ((), (), s32[]{:S(2)}) async-start(), calls=%async_computation.9 | async-start | bytes 1310720 | tf_op jit(solution)/shard_map/all_gather | solution.py:170
  16.5 115.1 %all-gather.9.cloned.1.call-start = ((), (), s32[]{:S(2)}) async-start(), calls=%async_computation.10 | async-start | bytes 1638400 | tf_op jit(solution)/shard_map/all_gather | solution.py:170
  20.5 26.7 %collective-permute-start.7 = (bf16[144,768]{1,0:T(8,128)(2,1)S(1)}, bf16[144,768]{1,0:T(8,128)(2,1)S(1)}, u32[]{:S(2)}, u32[]{:S(2)}) collective-permute-start(bf16[144,768]{1,0:T(8,128)(2,1)S(1)} %pack.5), channel_id=1, source_target_pairs={{0,16},{4,20},{8,24},{12,28},{16,0},{20,4},{24,8},{28,12},{1,17},{... | collective-permute-start | bytes 663560 | tf_op jit(solution)/shard_map/ppermute | solution.py:30
  23.1 25.8 %collective-permute-start.8 = (bf16[144,768]{1,0:T(8,128)(2,1)S(1)}, bf16[144,768]{1,0:T(8,128)(2,1)S(1)}, u32[]{:S(2)}, u32[]{:S(2)}) collective-permute-start(bf16[144,768]{1,0:T(8,128)(2,1)S(1)} %pack.5), channel_id=1, source_target_pairs={{0,24},{4,28},{8,16},{12,20},{16,8},{20,12},{24,0},{28,4},{1,25},{... | collective-permute-start | bytes 663560 | tf_op jit(solution)/shard_map/ppermute | solution.py:30
  27.2 31.7 %collective-permute-start.4 = (bf16[256,1024]{1,0:T(8,128)(2,1)S(1)}, bf16[256,1024]{1,0:T(8,128)(2,1)S(1)}, u32[]{:S(2)}, u32[]{:S(2)}) collective-permute-start(bf16[256,1024]{1,0:T(8,128)(2,1)S(1)} %bitcast.116), channel_id=1, source_target_pairs={{0,2},{1,3},{2,0},{3,1},{4,6},{5,7},{6,4},{7,5},{8,10},{9,11},{10,... | collective-permute-start | bytes 1572872 | tf_op jit(solution)/shard_map/ppermute | solution.py:30
  53.8 124.1 %all-gather.11.cloned.1.call-start = ((), (), s32[]{:S(2)}) async-start(), calls=%async_computation.11 | async-start | bytes 2621440 | tf_op jit(solution)/shard_map/all_gather | solution.py:170
  69.1 35.4 %collective-permute-start.11 = (bf16[512,1536]{1,0:T(8,128)(2,1)}, bf16[512,1536]{1,0:T(8,128)(2,1)S(1)}, u32[]{:S(2)}, u32[]{:S(2)}) collective-permute-start(bf16[512,1536]{1,0:T(8,128)(2,1)} %all-gather.5.cloned.1.call-done.same), channel_id=1, source_target_pairs={{0,4},{4,0},{8,12},{12,8},{16,20},{20,16},{24,28},{28,24},{1,5},{5... | collective-permute-start | bytes 4718600 | tf_op jit(solution)/shard_map/ppermute | solution.py:30
  110.2 261.7 %reduce-scatter.9.cloned.1.call-start = ((), (), s32[]{:S(2)}) async-start(), calls=%async_computation.12 | async-start | bytes 1310720 | tf_op jit(solution)/shard_map/reduce_scatter | solution.py:182
  110.5 25.9 %collective-permute-start.16 = (bf16[512,1024]{1,0:T(8,128)(2,1)}, bf16[512,1024]{1,0:T(8,128)(2,1)}, u32[]{:S(2)}, u32[]{:S(2)}) collective-permute-start(bf16[512,1024]{1,0:T(8,128)(2,1)} %all-gather.7.cloned.1.call-done.same), channel_id=1, source_target_pairs={{0,4},{4,0},{8,12},{12,8},{16,20},{20,16},{24,28},{28,24},{1,5},{5... | collective-permute-start | bytes 3145736 | tf_op jit(solution)/shard_map/ppermute | solution.py:30
  153.8 31.3 %collective-permute-start.21 = (bf16[512,1280]{1,0:T(8,128)(2,1)S(1)}, bf16[512,1280]{1,0:T(8,128)(2,1)}, u32[]{:S(2)}, u32[]{:S(2)}) collective-permute-start(bf16[512,1280]{1,0:T(8,128)(2,1)S(1)} %copy-done.19), channel_id=1, source_target_pairs={{0,4},{4,0},{8,12},{12,8},{16,20},{20,16},{24,28},{28,24},{1,5},{5... | collective-permute-start | bytes 3932168 | tf_op jit(solution)/shard_map/ppermute | solution.py:30
  185.0 48.0 %collective-permute-start.26 = (bf16[512,2048]{1,0:T(8,128)(2,1)}, bf16[512,2048]{1,0:T(8,128)(2,1)S(1)}, u32[]{:S(2)}, u32[]{:S(2)}) collective-permute-start(bf16[512,2048]{1,0:T(8,128)(2,1)} %all-gather.11.cloned.1.call-done.same), channel_id=1, source_target_pairs={{0,4},{4,0},{8,12},{12,8},{16,20},{20,16},{24,28},{28,24},{1,5},{5... | collective-permute-start | bytes 6291464 | tf_op jit(solution)/shard_map/ppermute | solution.py:30
  206.5 26.7 %collective-permute-start.28 = (bf16[1024,512]{1,0:T(8,128)(2,1)S(1)}, bf16[1024,512]{1,0:T(8,128)(2,1)S(1)}, u32[]{:S(2)}, u32[]{:S(2)}) collective-permute-start(bf16[1024,512]{1,0:T(8,128)(2,1)S(1)} %assemble.13.refs_4_.refs_7_), channel_id=1, source_target_pairs={{0,1},{1,0},{2,3},{3,2},{4,5},{5,4},{6,7},{7,6},{8,9},{9,8},{10,11... | collective-permute-start | bytes 3145736 | tf_op jit(solution)/shard_map/ppermute | solution.py:30
  299.0 25.5 %collective-permute-start.37 = (bf16[512,1024]{1,0:T(8,128)(2,1)S(1)}, bf16[512,1024]{1,0:T(8,128)(2,1)S(1)}, u32[]{:S(2)}, u32[]{:S(2)}) collective-permute-start(bf16[512,1024]{1,0:T(8,128)(2,1)S(1)} %get-tuple-element.335), channel_id=1, source_target_pairs={{0,4},{4,0},{8,12},{12,8},{16,20},{20,16},{24,28},{28,24},{1,5},{5... | collective-permute-start | bytes 3145736 | tf_op jit(solution)/shard_map/ppermute | solution.py:30
  300.0 24.5 %collective-permute-start.36 = (bf16[2,256,256]{2,1,0:T(8,128)(2,1)S(1)}, bf16[2,256,256]{2,1,0:T(8,128)(2,1)S(1)}, u32[]{:S(2)}, u32[]{:S(2)}) collective-permute-start(bf16[2,256,256]{2,1,0:T(8,128)(2,1)S(1)} %pad_maximum_fusion.3), channel_id=1, source_target_pairs={{0,2},{1,3},{2,0},{3,1},{4,6},{5,7},{6,4},{7,5},{8,10},{9,11},{10,... | collective-permute-start | bytes 786440 | tf_op jit(solution)/shard_map/ppermute | solution.py:30
  326.7 70.8 %reduce-scatter.11.cloned.1.call-start = ((), (), s32[]{:S(2)}) async-start(), calls=%async_computation.13 | async-start | bytes 1310720 | tf_op jit(solution)/shard_map/reduce_scatter | solution.py:182
  326.8 25.8 %collective-permute-start.39 = (bf16[512,1024]{1,0:T(8,128)(2,1)}, bf16[512,1024]{1,0:T(8,128)(2,1)S(1)}, u32[]{:S(2)}, u32[]{:S(2)}) collective-permute-start(bf16[512,1024]{1,0:T(8,128)(2,1)} %copy-done.161), channel_id=1, source_target_pairs={{0,4},{4,0},{8,12},{12,8},{16,20},{20,16},{24,28},{28,24},{1,5},{5... | collective-permute-start | bytes 3145736 | tf_op jit(solution)/shard_map/ppermute | solution.py:30
  327.8 24.8 %collective-permute-start.40 = (bf16[256,1024]{1,0:T(8,128)(2,1)}, bf16[256,1024]{1,0:T(8,128)(2,1)S(1)}, u32[]{:S(2)}, u32[]{:S(2)}) collective-permute-start(bf16[256,1024]{1,0:T(8,128)(2,1)} %copy-done.162), channel_id=1, source_target_pairs={{0,1},{1,0},{2,3},{3,2},{4,5},{5,4},{6,7},{7,6},{8,9},{9,8},{10,11... | collective-permute-start | bytes 1572872 | tf_op jit(solution)/shard_map/ppermute | solution.py:30
  329.1 24.3 %collective-permute-start.42 = (bf16[256,1024]{1,0:T(8,128)(2,1)S(1)}, bf16[256,1024]{1,0:T(8,128)(2,1)S(1)}, u32[]{:S(2)}, u32[]{:S(2)}) collective-permute-start(bf16[256,1024]{1,0:T(8,128)(2,1)S(1)} %add_convert_fusion.11), channel_id=1, source_target_pairs={{0,2},{1,3},{2,0},{3,1},{4,6},{5,7},{6,4},{7,5},{8,10},{9,11},{10,... | collective-permute-start | bytes 1572872 | tf_op jit(solution)/shard_map/ppermute | solution.py:30
  355.8 83.7 %reduce-scatter.13.cloned.1.call-start = ((), (), s32[]{:S(2)}) async-start(), calls=%async_computation.14 | async-start | bytes 655360 | tf_op jit(solution)/shard_map/reduce_scatter | solution.py:182
  370.0 25.5 %collective-permute-start.49 = (bf16[512,768]{1,0:T(8,128)(2,1)}, bf16[512,768]{1,0:T(8,128)(2,1)}, u32[]{:S(2)}, u32[]{:S(2)}) collective-permute-start(bf16[512,768]{1,0:T(8,128)(2,1)} %get-tuple-element.375), channel_id=1, source_target_pairs={{0,4},{4,0},{8,12},{12,8},{16,20},{20,16},{24,28},{28,24},{1,5},{5... | collective-permute-start | bytes 2359304 | tf_op jit(solution)/shard_map/ppermute | solution.py:30
  408.6 78.9 %reduce-scatter.15.cloned.1.call-start = ((), (), s32[]{:S(2)}) async-start(), calls=%async_computation.15 | async-start | bytes 983040 | tf_op jit(solution)/shard_map/reduce_scatter | solution.py:182
  408.6 30.9 %collective-permute-start.50 = (bf16[256,1024]{1,0:T(8,128)(2,1)}, bf16[256,1024]{1,0:T(8,128)(2,1)}, u32[]{:S(2)}, u32[]{:S(2)}) collective-permute-start(bf16[256,1024]{1,0:T(8,128)(2,1)} %copy-done.164), channel_id=1, source_target_pairs={{0,1},{1,0},{2,3},{3,2},{4,5},{5,4},{6,7},{7,6},{8,9},{9,8},{10,11... | collective-permute-start | bytes 1572872 | tf_op jit(solution)/shard_map/ppermute | solution.py:30
  412.7 26.9 %collective-permute-start.53 = (bf16[256,1024]{1,0:T(8,128)(2,1)}, bf16[256,1024]{1,0:T(8,128)(2,1)}, u32[]{:S(2)}, u32[]{:S(2)}) collective-permute-start(bf16[256,1024]{1,0:T(8,128)(2,1)} %add_convert_fusion.9), channel_id=1, source_target_pairs={{0,2},{1,3},{2,0},{3,1},{4,6},{5,7},{6,4},{7,5},{8,10},{9,11},{10,... | collective-permute-start | bytes 1572872 | tf_op jit(solution)/shard_map/ppermute | solution.py:30
  452.4 74.1 %reduce-scatter.17.cloned.1.call-start = ((), (), s32[]{:S(2)}) async-start(), calls=%async_computation.16 | async-start | bytes 1310720 | tf_op jit(solution)/shard_map/reduce_scatter | solution.py:182
  459.3 26.1 %collective-permute-start.56 = (bf16[512,1024]{1,0:T(8,128)(2,1)S(1)}, bf16[512,1024]{1,0:T(8,128)(2,1)S(1)}, u32[]{:S(2)}, u32[]{:S(2)}) collective-permute-start(bf16[512,1024]{1,0:T(8,128)(2,1)S(1)} %get-tuple-element.423), channel_id=1, source_target_pairs={{0,4},{4,0},{8,12},{12,8},{16,20},{20,16},{24,28},{28,24},{1,5},{5... | collective-permute-start | bytes 3145736 | tf_op jit(solution)/shard_map/ppermute | solution.py:30
  461.0 46.4 %collective-permute-start.58 = (bf16[512,1024]{1,0:T(8,128)(2,1)}, bf16[512,1024]{1,0:T(8,128)(2,1)}, u32[]{:S(2)}, u32[]{:S(2)}) collective-permute-start(bf16[512,1024]{1,0:T(8,128)(2,1)} %get-tuple-element.438), channel_id=1, source_target_pairs={{0,4},{4,0},{8,12},{12,8},{16,20},{20,16},{24,28},{28,24},{1,5},{5... | collective-permute-start | bytes 3145736 | tf_op jit(solution)/shard_map/ppermute | solution.py:30
  487.4 89.4 %reduce-scatter.19.cloned.1.call-start = ((), (), s32[]{:S(2)}) async-start(), calls=%async_computation.17 | async-start | bytes 1310720 | tf_op jit(solution)/shard_map/reduce_scatter | solution.py:182
  517.9 70.1 %reduce-scatter.23.cloned.1.call-start = ((), (), s32[]{:S(2)}) async-start(), calls=%async_computation.19 | async-start | bytes 983040 | tf_op jit(solution)/shard_map/reduce_scatter | solution.py:182
  547.7 44.2 %reduce-scatter.21.cloned.1.call-start = ((), (), s32[]{:S(2)}) async-start(), calls=%async_computation.18 | async-start | bytes 655360 | tf_op jit(solution)/shard_map/reduce_scatter | solution.py:182
  547.7 26.4 %collective-permute-start.80 = (bf16[128,1024]{1,0:T(8,128)(2,1)}, bf16[128,1024]{1,0:T(8,128)(2,1)}, u32[]{:S(2)}, u32[]{:S(2)}) collective-permute-start(bf16[128,1024]{1,0:T(8,128)(2,1)} %reduce-scatter.9.cloned.1.call-done.refs_0_), channel_id=1, source_target_pairs={{0,2},{1,3},{2,0},{3,1},{4,6},{5,7},{6,4},{7,5},{8,10},{9,11},{10,... | collective-permute-start | bytes 786440 | tf_op jit(solution)/shard_map/ppermute | solution.py:30
  548.3 28.5 %collective-permute-start.79 = (bf16[128,1024]{1,0:T(8,128)(2,1)}, bf16[128,1024]{1,0:T(8,128)(2,1)}, u32[]{:S(2)}, u32[]{:S(2)}) collective-permute-start(bf16[128,1024]{1,0:T(8,128)(2,1)} %reduce-scatter.9.cloned.1.call-done.refs_0_), channel_id=1, source_target_pairs={{0,1},{1,0},{2,3},{3,2},{4,5},{5,4},{6,7},{7,6},{8,9},{9,8},{10,11... | collective-permute-start | bytes 786440 | tf_op jit(solution)/shard_map/ppermute | solution.py:30
  (258 other events, 1768.1 us)
Sparse Core Ops, SparseCore 0:
  12.2 55.6 all-gather.4
  70.1 27.0 all-gather.6
  99.3 32.1 all-gather.8
  133.0 44.9 all-gather.10
  326.8 35.5 reduce-scatter.8
  364.7 26.9 reduce-scatter.10
  408.7 30.8 reduce-scatter.12
  452.5 21.8 reduce-scatter.14
  487.6 25.5 reduce-scatter.16
  518.0 23.7 reduce-scatter.18
  547.8 19.7 reduce-scatter.22
  569.7 21.1 reduce-scatter.20

commit v4 on v3

--- a/solution.py
+++ b/solution.py
@@ -174,10 +174,6 @@
     return hop(value, "fsdp", 1)
 
 
-def added(same, received):
-    return (same.astype(F32) + received.astype(F32)).astype(BF)
-
-
 def scatter_z(same):
     return lax.psum_scatter(
         same, "fsdp", scatter_dimension=0, tiled=True, axis_index_groups=z_groups()
@@ -189,38 +185,104 @@
     return total, core_swap(total), across, core_swap(across)
 
 
-def staged(body, held, refs):
-    count = len(held)
-    inputs, rest = refs[:count], refs[count:]
-    places = [i for i in range(count) if held[i]]
-    sems, buffers, rest = rest[-1], rest[-1 - len(places) : -1], rest[: -1 - len(places)]
-    copies = [
-        pltpu.make_async_copy(inputs[i], buffer, sems.at[number])
-        for number, (i, buffer) in enumerate(zip(places, buffers))
-    ]
+class Slots:
+    def __init__(self, halves, column, width, rows, keys, key):
+        self.halves, self.column, self.width, self.rows = halves, column, width, rows
+        self.keys, self.key = keys, key
+
+    def copies(self, keys, same, other, buffer):
+        count = buffer.shape[0] // self.rows
+        stride = 2 * same.shape[0] // count
+        for r in range(count):
+            source = other if r % 2 else same
+            source = source.at[pl.ds(r // 2 * stride, self.rows), pl.ds(self.column, self.width)]
+            start = pl.multiple_of((r ^ keys[self.key]) * self.rows, self.rows)
+            yield source, buffer.at[pl.ds(start, self.rows), :]
+
+
+def staged(body, plan, refs):
+    refs = list(refs)
+    keys = refs.pop(0) if any(isinstance(item, Slots) for item in plan) else None
+    taken = [refs.pop(0) for item in plan for _ in range(1 + isinstance(item, Slots))]
+    sems = refs.pop()
+    places = [i for i, item in enumerate(plan) if item is not None]
+    buffers = refs[len(refs) - len(places) :]
+    refs = refs[: len(refs) - len(places)]
+    inputs, copies = [], []
+    for item in plan:
+        if item is None:
+            inputs.append(taken.pop(0))
+            continue
+        buffer = buffers.pop(0)
+        inputs.append(buffer)
+        if item is VMEM:
+            moves = [(taken.pop(0), buffer)]
+        else:
+            moves = item.copies(keys, taken.pop(0), taken.pop(0), buffer)
+        for source, target in moves:
+            copies.append(pltpu.make_async_copy(source, target, sems.at[len(copies)]))
     for copy in copies:
         copy.start()
     for copy in copies:
         copy.wait()
-    inputs = list(inputs)
-    for i, buffer in zip(places, buffers):
-        inputs[i] = buffer
-    body(*inputs, *rest)
-
-
-def kernel_call(body, name, inputs, outputs, scratch=(), in_specs=None):
-    held = [spec is VMEM for spec in in_specs or [VMEM] * len(inputs)]
-    buffers = [pltpu.VMEM(item.shape, item.dtype) for item, one in zip(inputs, held) if one]
+    body(*inputs, *refs)
+
+
+def kernel_call(body, name, inputs, outputs, scratch=(), in_specs=None, cost=0):
+    plan, arrays, specs, buffers, keys = [], [], [], [], None
+    count = 1
+    hbm = pl.BlockSpec(memory_space=pl.ANY)
+    for item, spec in zip(inputs, in_specs or [VMEM] * len(inputs)):
+        if isinstance(item, Slots):
+            shape = (lax.axis_size("fsdp") * item.rows, item.width)
+            plan.append(item)
+            arrays += item.halves
+            specs += [hbm, hbm]
+            buffers.append(pltpu.VMEM(shape, BF))
+            keys = item.keys
+            count += lax.axis_size("fsdp")
+            continue
+        arrays.append(item)
+        plan.append(VMEM if spec is VMEM else None)
+        specs.append(hbm if spec is VMEM else SMEM)
+        if spec is VMEM:
+            buffers.append(pltpu.VMEM(item.shape, item.dtype))
+            count += 1
+    if keys is not None:
+        arrays, specs = [keys] + arrays, [SMEM] + specs
     return pl.pallas_call(
-        lambda *refs: staged(body, held, refs),
-        in_specs=[pl.BlockSpec(memory_space=pl.ANY) if one else SMEM for one in held],
+        lambda *refs: staged(body, plan, refs),
+        in_specs=specs,
         out_specs=[VMEM] * len(outputs),
         out_shape=[jax.ShapeDtypeStruct(shape, kind) for shape, kind in outputs],
-        scratch_shapes=[*scratch, *buffers, pltpu.SemaphoreType.DMA((max(len(buffers), 1),))],
+        scratch_shapes=[*scratch, *buffers, pltpu.SemaphoreType.DMA((count,))],
         compiler_params=pltpu.CompilerParams(vmem_limit_bytes=48 << 20),
-        cost_estimate=pl.CostEstimate(flops=0, bytes_accessed=0, transcendentals=0),
+        cost_estimate=pl.CostEstimate(flops=0, bytes_accessed=cost, transcendentals=0),
         name=name,
-    )(*inputs)
+    )(*arrays)
+
+
+def pair_kernel(keep, received, same, other):
+    for i, target in enumerate((same, other)):
+        target[...] = (keep[i].astype(F32) + received[i].astype(F32)).astype(BF)
+
+
+def added_pair(keep, received):
+    outs = [(keep.shape[1:], BF)] * 2
+    return kernel_call(pair_kernel, "added_pair", (keep, received), outs)
+
+
+def add_kernel(same, *refs):
+    out = refs[-1]
+    start = 0
+    for item in refs[:-1]:
+        rows = slice(start, start + item.shape[0])
+        out[rows, :] = (same[rows, :].astype(F32) + item[...].astype(F32)).astype(BF)
+        start += item.shape[0]
+
+
+def added(same, *received):
+    return kernel_call(add_kernel, "added", (same, *received), [(same.shape, BF)])[0]
 
 
 def nn(left, right):
@@ -291,11 +353,11 @@
 
 
 def out_kernel(
-    scalars, own, beside, across, w_own, w_other, stream, table, middle, normed, attended
+    scalars, own, beside, across, far, w_own, w_other, stream, table, middle, normed, attended
 ):
     run = scalars[0]
     core = run % 2
-    parts = [own[...], beside[0], across[0], beside[1]]
+    parts = [own[...], beside[...], across[...], far[...]]
     size = parts[0].shape[1]
     starts = [pl.multiple_of((run ^ j) * size, size) for j in range(4)]
     for part, start in zip(parts, starts):
@@ -313,10 +375,10 @@
     normed[...] = (hat * row(table, GAIN_TWO) + row(table, SHIFT_TWO)).astype(BF)
 
 
-def out_step(scalars, own, beside, across, w_outs, stream, table):
+def out_step(scalars, parts, w_outs, stream, table):
     outs = [(stream.shape, F32), (stream.shape, BF), (stream.shape, BF)]
-    inputs = (scalars, own, beside, across, *w_outs, stream, table)
-    return kernel_call(out_kernel, "out_step", inputs, outs, in_specs=[SMEM] + [VMEM] * 7)
+    inputs = (scalars, *parts, *w_outs, stream, table)
+    return kernel_call(out_kernel, "out_step", inputs, outs, in_specs=[SMEM] + [VMEM] * 8)
 
 
 def ffn_kernel(a, b, w_up, bias, w_down, act, slope, keep, send, source):
@@ -338,7 +400,7 @@
 
 def ffn(a, b, w_up, bias, w_down):
     rows, width = a.shape
-    hidden = w_up.shape[1]
+    hidden = w_up.width
     outs = [
         ((2 * rows, hidden), BF),
         ((2 * rows, hidden), BF),
@@ -364,7 +426,7 @@
 
 def ffn_back(a, b, slope, w_up, w_down):
     rows, width = a.shape
-    hidden = w_up.shape[1]
+    hidden = w_up.width
     outs = [
         ((2 * rows, hidden), BF),
         ((rows, width), F32),
@@ -378,7 +440,7 @@
 def weight_grad_kernel(count, parts, scalars, *refs):
     x = scalars[1]
     lefts, rights = refs[: parts[0]], refs[parts[0] : parts[0] + parts[1]]
-    same, other, left, right, total = refs[parts[0] + parts[1] :]
+    same, *others, left, right, total = refs[parts[0] + parts[1] :]
     for sources, target in ((lefts, left), (rights, right)):
         start = 0
         for source in sources:
@@ -386,17 +448,19 @@
             start += source.shape[0]
     total[...] = tn(left[...], right[...]).astype(BF)
     rows = total.shape[0] // count
+    each = count // 2 // len(others)
     for r in range(count):
         start = pl.multiple_of((r ^ x) * rows, rows)
-        target = other if r % 2 else same
-        target[r // 2 * rows : (r // 2 + 1) * rows, :] = total[pl.ds(start, rows), :]
-
-
-def weight_grad(lefts, rights, place):
+        target = others[r // 2 // each] if r % 2 else same
+        slot = r // 2 % each if r % 2 else r // 2
+        target[slot * rows : (slot + 1) * rows, :] = total[pl.ds(start, rows), :]
+
+
+def weight_grad(lefts, rights, place, cuts):
     count = lax.axis_size("fsdp")
     total = sum(item.shape[0] for item in lefts)
     tall, wide = lefts[0].shape[1], rights[0].shape[1]
-    outs = [((tall // 2, wide), BF)] * 2
+    outs = [((tall // 2, wide), BF)] + [((tall // 2 // cuts, wide), BF)] * cuts
     scratch = [
         pltpu.VMEM((total, tall), BF),
         pltpu.VMEM((total, wide), BF),
@@ -405,7 +469,7 @@
     inputs = (place, *lefts, *rights)
     body = functools.partial(weight_grad_kernel, count, (len(lefts), len(rights)))
     specs = [SMEM] + [VMEM] * (len(inputs) - 1)
-    return kernel_call(body, "weight_grad", inputs, outs, scratch, specs)
+    return list(kernel_call(body, "weight_grad", inputs, outs, scratch, specs))
 
 
 def out_grad_kernel(count, place, left, right, keep, send, total):
@@ -504,9 +568,10 @@
     w_other,
     grad_middle,
     branch,
-    own,
-    near,
-    far,
+    first,
+    second,
+    third,
+    fourth,
     sums,
 ):
     run = scalars[0]
@@ -522,22 +587,16 @@
     sums[1:2, :] = grad_shift
     sums[2:3, :] = jnp.sum(low.astype(F32), axis=0, keepdims=True)
     sums[3:4, :] = jnp.sum(grad[...].astype(BF).astype(F32), axis=0, keepdims=True)
-    size = own.shape[1]
+    size = first.shape[1]
     half = w_own.shape[1]
-    for j in range(4):
+    for j, target in enumerate((first, second, third, fourth)):
         rows = pl.ds(pl.multiple_of((run ^ j) * size, size), size)
         result = None
         for weight, place in ((w_own, core), (w_other, 1 - core)):
             lanes = pl.ds(pl.multiple_of(place * half, half), half)
             term = nt(branch[:, lanes], weight[rows, :])
             result = term if result is None else result + term
-        result = result.astype(BF)
-        if j == 0:
-            own[...] = result
-        elif j == 2:
-            far[...] = result
-        else:
-            near[j // 2] = result
+        target[...] = result.astype(BF)
 
 
 def out_back(scalars, sums, middle, grad, table, w_outs):
@@ -547,7 +606,8 @@
         ((rows, width), F32),
         ((rows, width), BF),
         ((rows, mine), BF),
-        ((2, rows, mine), BF),
+        ((rows, mine), BF),
+        ((rows, mine), BF),
         ((rows, mine), BF),
         ((8, width), F32),
     ]
@@ -603,7 +663,24 @@
 
 
 def attend_kernel(
-    scalars, slopes, a, b, c, d, w_qkv, bias, nat, att, own, near, far, lse, low, scores, offsets
+    scalars,
+    slopes,
+    a,
+    b,
+    c,
+    d,
+    w_qkv,
+    bias,
+    nat,
+    att,
+    own,
+    near,
+    far,
+    farther,
+    lse,
+    low,
+    scores,
+    offsets,
 ):
     run, length = scalars[0], scalars[1]
     blocks = nat.shape[0] // BLOCK
@@ -642,7 +719,8 @@
             low[run ^ i, :, lanes] = rows.astype(BF)
     own[...] = low[0]
     near[...] = low[1]
-    far[...] = low[2:4]
+    far[...] = low[2]
+    farther[...] = low[3]
 
 
 def attend_back_kernel(
@@ -652,6 +730,7 @@
     own,
     beside,
     across,
+    far,
     att,
     lse,
     w_qkv,
@@ -670,7 +749,7 @@
     run, length = scalars[0], scalars[1]
     blocks = nat.shape[0] // BLOCK
     mine = nat.shape[1] // 3
-    for j, rows in enumerate((own[...], beside[0], across[0], across[1])):
+    for j, rows in enumerate((own[...], beside[...], across[...], far[...])):
         place = pl.ds(pl.multiple_of((run ^ j) * BLOCK, BLOCK), BLOCK)
         nat_grad[place, :] = rows
     distances(offsets)
@@ -734,14 +813,15 @@
 
 def attend(blocks, w_qkv, bias, scalars, slopes):
     rows, width = blocks[0].shape
-    columns = w_qkv.shape[1]
+    columns = w_qkv.width
     mine = columns // 3
     outs = [
         ((4 * rows, columns), BF),
         ((4 * rows, mine), F32),
         ((rows, mine), BF),
         ((rows, mine), BF),
-        ((2, rows, mine), BF),
+        ((rows, mine), BF),
+        ((rows, mine), BF),
         ((8, 4 * rows), F32),
     ]
     scratch = [
@@ -754,10 +834,10 @@
     return kernel_call(attend_kernel, "attend", inputs, outs, scratch, specs)
 
 
-def attend_back(nat, own, beside, across, att, lse, w_qkv, scalars, slopes):
+def attend_back(nat, parts, att, lse, w_qkv, scalars, slopes):
     total, columns = nat.shape
     rows, mine = total // 4, columns // 3
-    width = w_qkv.shape[0]
+    width = w_qkv.rows * lax.axis_size("fsdp")
     outs = [
         ((total, columns), BF),
         ((rows, width), F32),
@@ -773,8 +853,8 @@
         pltpu.VMEM((total, mine), F32),
         pltpu.VMEM((BLOCK, BLOCK), F32),
     ]
-    inputs = (scalars, slopes, nat, own, beside, across, att, lse, w_qkv)
-    specs = [SMEM, SMEM] + [VMEM] * 7
+    inputs = (scalars, slopes, nat, *parts, att, lse, w_qkv)
+    specs = [SMEM, SMEM] + [VMEM] * 8
     return kernel_call(attend_back_kernel, "attend_back", inputs, outs, scratch, specs)
 
 
@@ -849,10 +929,11 @@
     stride = part + small.shape[0]
     own = pack(["qkv", "small"], [qkv_weight, small], 0, place, stride, columns)
     token_blocks = seq_blocks(tokens[0])
-    even = [own] + [hop(own, "fsdp", 2 * k) for k in range(1, fsdp // 2)]
+    even = [own] + [hop(own, "fsdp", 2 * k) for k in range(1, fsdp // 2 - 1)]
+    even.append(hop(tied(own, even[1]), "fsdp", fsdp - 2))
     first = jnp.concatenate(even)
     first = (first, x_swap(first))
-    cot_blocks = seq_blocks(tied(cotangent[0], token_blocks[2]))
+    cot_blocks = seq_blocks(cotangent[0])
     token_blocks, cot_blocks, first = meet(token_blocks, cot_blocks, first)
     arrays = dict(qkv=qkv_weight, out=out_weight, up=up_weight, down=down_weight)
     sizes = dict(qkv=columns, out=half, up=ffn_size, down=width)
@@ -870,11 +951,15 @@
         bundle(1, ["qkv", "out"]),
         bundle(1, ["up", "down"]),
     ]
-    token_blocks = tied(token_blocks, packs)
+    keys = jnp.stack([me, me % 2]).astype(jnp.int32)
     early_one, late_one, early_two, late_two = (gather_z(item) for item in packs)
 
-    def matrix(halves, column, size, key=me % 2):
-        return assemble(halves, column, size, part, key)
+    def matrix(halves, column, size, key=1):
+        return Slots(halves, column, size, part, keys, key)
+
+    def out_matrices(halves, column):
+        own = assemble(halves, column, half, part, me % 2)
+        return own, core_swap(own)
 
     small = [item.reshape(fsdp // 2, stride, columns)[:, part : part + extra] for item in first]
     small = jnp.stack(small, 1).reshape(fsdp, LAYERS, -1)
@@ -890,40 +975,44 @@
         biases.append((bias_qkv.reshape(1, -1), bias_up.reshape(1, -1)))
 
     stream = tokens[0].astype(F32)
+    token_blocks, tables, biases = meet(token_blocks, tables, biases)
     h1 = first_norm(token_blocks, tables[0])
-    w_qkv = assemble(first, 0, columns, part, me)
-    moved = x_swap(tied(early_one, first))
+    w_qkv = matrix(first, 0, columns, 0)
+    out_one, up_one = early_one[:, :half], early_one[:, half:]
+    moved_out, moved = x_swap(out_one), x_swap(up_one)
     saved, weights = [], []
     for layer in range(LAYERS):
         top = layer + 1 == LAYERS
         bias_qkv, bias_up = biases[layer]
-        packed, attended, own, near, far, lse = attend(h1, w_qkv, bias_qkv, scalars, slopes)
-        across = y_swap(far)
+        packed, attended, *low, lse = attend(h1, w_qkv, bias_qkv, scalars, slopes)
         if top:
-            across, moved = meet(across, moved)
+            w_outs = out_matrices(early_two, columns)
+        else:
+            low, moved_out = meet(low, moved_out)
+            w_outs = out_matrices((out_one, moved_out), 0)
+        far = y_swap(low[3])
+        across = y_swap(low[2])
+        if not top:
+            across, far, moved, late_one = meet(across, far, moved, late_one)
+            moved_late = x_swap(late_one)
+        parts = [low[0], core_swap(low[1]), across, core_swap(far)]
+        middle, normed, att_own = out_step(scalars, parts, w_outs, stream, tables[layer])
+        h2 = seq_blocks(normed)
+        if top:
+            middle, moved = meet(middle, moved)
             late_two = (late_two, moved)
-            w_out = matrix(early_two, columns, half)
             w_up, w_down = matrix(late_two, 0, ffn_size), matrix(late_two, ffn_size, width)
+            near = ffn(h2[0], h2[1], w_up, bias_up, w_down)
+            near_back = ffn_back(cot_blocks[0], cot_blocks[1], near[1], w_up, w_down)
+            h2[2], near, near_back = meet(h2[2], near, near_back)
+            h2[3] = core_swap(h2[2])
         else:
-            across, moved, late_one = meet(across, moved, late_one)
-            early_one = (early_one, moved)
-            w_out, w_up = matrix(early_one, 0, half), matrix(early_one, half, ffn_size)
-            moved = x_swap(late_one)
-        beside = core_swap(jnp.stack([near, across[1]]))
-        w_outs = (w_out, core_swap(w_out))
-        middle, normed, att_own = out_step(
-            scalars, own, beside, across, w_outs, stream, tables[layer]
-        )
-        h2 = seq_blocks(normed)
-        if not top:
-            h2[2], moved, early_two = meet(h2[2], moved, early_two)
-            w_down = matrix((late_one, moved), 0, width)
+            h2[2], moved_late, early_two = meet(h2[2], moved_late, early_two)
+            h2[3] = core_swap(h2[2])
+            w_up = matrix((up_one, moved), 0, ffn_size)
+            w_down = matrix((late_one, moved_late), 0, width)
             moved = x_swap(early_two)
-            h2[3] = core_swap(h2[2])
-        near = ffn(h2[0], h2[1], w_up, bias_up, w_down)
-        if top:
-            h2[2], near = meet(h2[2], near)
-            h2[3] = core_swap(h2[2])
+            near = ffn(h2[0], h2[1], w_up, bias_up, w_down)
         far = ffn(h2[2], h2[3], w_up, bias_up, w_down)
         saved.append((stream, h1, packed, attended, lse, att_own, middle, h2, near[:2], far[:2]))
         weights.append((w_qkv, w_outs, w_up, w_down))
@@ -941,72 +1030,81 @@
     g_down = cot_blocks
     vectors = [None] * LAYERS
     upper, lower = [], []
-    waiting = None
     for layer in reversed(range(LAYERS)):
         top = layer + 1 == LAYERS
         totals = upper if top else lower
         w_qkv, w_outs, w_up, w_down = weights[layer]
         stream, h1, packed, attended, lse, att_own, middle, h2, act_near, act_far = saved[layer]
-        near = ffn_back(g_down[0], g_down[1], act_near[1], w_up, w_down)
-        if not top:
-            g_down[2], near, waiting, reduced, upper[1] = meet(
-                g_down[2], near, waiting, reduced, upper[1]
-            )
+        if top:
+            near = near_back
+        else:
+            near = ffn_back(g_down[0], g_down[1], act_near[1], w_up, w_down)
+            g_down[2], near, late, reduced = meet(g_down[2], near, late, reduced)
             g_down[3] = core_swap(g_down[2])
-            reduced = added(*waiting)
-            upper.append(scatter_z(reduced))
+            moved_late = x_swap(late[1])
         far = ffn_back(g_down[2], g_down[3], act_far[1], w_up, w_down)
         far_low = far_sum(far[1:3])
-        acts, h2_late = tied(([act_near[0], act_far[0]], h2), far_low if not top else near)
-        sent_down = weight_grad(acts, g_down, place)
-        moved_down = x_swap(sent_down[1])
-        sent_up = weight_grad(h2_late, [near[0], far[0]], place)
+        acts, h2, far_low = meet([act_near[0], act_far[0]], h2, far_low)
+        sent_down = weight_grad(acts, g_down, place, 1)
+        sent_up = weight_grad(h2, [near[0], far[0]], place, 1)
+        moved_down, moved_up = x_swap(sent_down[1]), x_swap(sent_up[1])
         sums = near[1], core_swap(near[2]), y_swap(far_low)
-        if not top:
-            sums = tied(sums, (reduced, upper[2]))
-        sums, sent_up = meet(sums, sent_up)
-        moved_up = x_swap(sent_up[1])
-        grad_middle, g_branch, own, near_att, far_att, lines_two = out_back(
+        sums, sent_down[0], sent_up[0] = meet(sums, sent_down[0], sent_up[0])
+        grad_middle, g_branch, *g_att, lines_two = out_back(
             scalars, sums, middle, grad, tables[layer], w_outs
         )
-        beside = core_swap(near_att)
-        across = jnp.stack([far_att, beside[1]])
-        att_late, branch_late = tied((att_own, g_branch), across)
-        across = y_swap(across)
-        keep, send = out_grad(att_late, branch_late, place)
-        sent_out = added(keep, core_swap(send))
-        across, moved, sent_out = meet(across, moved_down, sent_out)
-        reduced = added(sent_down[0], moved)
-        totals.append(scatter_z(reduced))
-        moved_out = x_swap(sent_out[1])
+        g_att = [
+            g_att[0],
+            core_swap(g_att[1]),
+            y_swap(g_att[2]),
+            y_swap(core_swap(g_att[3])),
+        ]
         if not top:
-            across = tied(across, upper[3])
+            g_att, moved_late = meet(g_att, moved_late)
+            reduced = added(late[0], moved_late)
+            g_att, reduced, upper[:2] = meet(g_att, reduced, upper[:2])
+            upper.append(scatter_z(reduced))
+            upper_far = [y_swap(item) for item in upper[:2]]
+        if top:
+            g_att, last_sums = meet(g_att, last_sums)
         g_packed, *parts, packed_sum = attend_back(
-            packed, own, beside, across, attended, lse, w_qkv, scalars, slopes
+            packed, g_att, attended, lse, w_qkv, scalars, slopes
         )
         if top:
-            one, two = tied(last_sums, across)
-            last_sums = summed(one, two)
-            parts, moved, last_sums, reduced = meet(parts, moved_up, last_sums, reduced)
+            last_sums = summed(*last_sums)
+            parts, moved_down, last_sums = meet(parts, moved_down, last_sums)
             result = layer_end(saved[layer][6], last_sums, tables[layer], None)[1]
         else:
-            parts, moved, reduced = meet(parts, moved_up, reduced)
-        reduced = added(sent_up[0], moved)
+            parts, moved_down, upper_far = meet(parts, moved_down, upper_far)
+        far_low = far_sum(parts[2:])
+        h1, sent_down[0], far_low = meet(h1, sent_down[0], far_low)
+        if not layer:
+            att_own, g_branch, far_low = meet(att_own, g_branch, far_low)
+            keep, send = out_grad(att_own, g_branch, place)
+        sent_qkv = weight_grad(h1, [g_packed], place, 1)
+        sums = parts[0], core_swap(parts[1]), y_swap(far_low)
+        reduced = added(sent_down[0], moved_down)
         totals.append(scatter_z(reduced))
-        far_low = far_sum(parts[2:])
-        sent_qkv = weight_grad(tied(h1, far_low), [g_packed], place)
-        sums = parts[0], core_swap(parts[1]), y_swap(far_low)
-        sums = tied(sums, (sent_qkv, reduced, totals[0]))
-        sums, moved = meet(sums, moved_out)
-        reduced = added(sent_out[0], moved)
-        totals.append(scatter_z(reduced))
-        waiting = sent_qkv[0], x_swap(sent_qkv[1])
+        sums, moved_up, reduced, sent_qkv[0] = meet(sums, moved_up, reduced, sent_qkv[0])
         if not top:
-            totals.append(scatter_z(added(*waiting)))
+            reduced = added(sent_up[0], moved_up)
+            totals.append(scatter_z(reduced))
+            sums, upper[2] = meet(sums, upper[2])
         up_sum = near[3] + far[3]
         grad, normed, lines_one = layer_begin(sums, stream, grad_middle, tables[layer])
         if layer:
+            normed, sent_up[0], att_own, g_branch = meet(normed, sent_up[0], att_own, g_branch)
             g_down = seq_blocks(normed)
+            keep, send = out_grad(att_own, g_branch, place)
+            reduced = added(sent_up[0], moved_up)
+            upper.append(scatter_z(reduced))
+        else:
+            grad, totals[0] = meet(grad, totals[0])
+        sent_out = added_pair(keep, core_swap(send))
+        late = [jnp.concatenate(pair, axis=1) for pair in zip(sent_qkv, sent_out)]
+        if not layer:
+            last, *totals = meet(added(late[0], x_swap(late[1])), *totals)
+            lower = totals + [scatter_z(last)]
 
         vectors[layer] = (lines_two, lines_two, packed_sum, lines_one, up_sum)
 
@@ -1017,7 +1115,8 @@
         return lax.dynamic_update_slice_in_dim(jnp.zeros(shape, F32), value, run * size, axis)
 
     small_sums = []
-    for _, lines_two, packed_sum, lines_one, up_sum in tied(vectors, grad):
+    vectors, upper[2], grad = meet(vectors, upper[2], grad)
+    for _, lines_two, packed_sum, lines_one, up_sum in vectors:
         members = [
             lines_one[0],
             lines_one[1],
@@ -1036,17 +1135,20 @@
             )
         )
 
-    upper = [four(item) for item in tied(upper, grad)]
-    starts = ((3, 0), (2, 0), (1, 0), (0, 0))
+    own = zip(upper[:2], upper_far)
+    upper[:2] = [(item, core_swap(item), far, core_swap(far)) for item, far in own]
+    upper[2] = four(upper[2])
+    starts = ((2, 0), (2, columns), (1, 0), (0, 0))
     matrices = finish(1, LAYERS, upper, starts, place, None)
-    lower[3] = tied(lower[3], matrices)
-    lower = [four(item) for item in lower]
+    vector = sum_small(jnp.stack(small_sums, axis=1))
+    early = [four(item) for item in lower[:2]]
+    last, early, matrices, vector, result = meet(lower[2], early, matrices, vector, result)
+    lower = [*early, four(last)]
     matrices = finish(0, LAYERS, lower, starts, place, matrices)
     grad_qkv_w, grad_out_w, grad_up_w, grad_down_w = matrices
     if piece % 128:
         grad_up_w = grad_up_w.reshape(LAYERS, part, 4, fsdp, piece)
         grad_up_w = jnp.swapaxes(grad_up_w, 2, 3).reshape(LAYERS, part, hidden)
-    vector = sum_small(jnp.stack(small_sums, axis=1))
     lines = [vector[:, i * part : (i + 1) * part] for i in range(8)]
     gain_one, shift_one, bias_q, bias_v, bias_o, gain_two, shift_two, bias_down = lines
     return (

time: 628 us -> 570 us (0.908)
  waiting for transfers between devices: 218 us -> 182 us
  local copies, waits for them, and re-layouts: 107 us -> 81.7 us
  other arithmetic: 34.7 us -> 13.9 us
  starting transfers between devices: 56.6 us -> 74.1 us
    ppermute x94 -> x95, waiting for transfers between devices: 178 us -> 140 us  [hop(): return lax.ppermute(value, axis, [(i, i ^ mask) for i in range(size)])]
    unnamed x391 -> x419, local copies, waits for them, and re-layouts: 93.8 us -> 70.8 us
    convert_element_type x10 -> x0, other arithmetic: 19.4 us -> none  [added(): return (same.astype(F32) + received.astype(F32)).astype(BF)]
    ppermute x94 -> x95, starting transfers between devices: 55.9 us -> 73.4 us  [hop(): return lax.ppermute(value, axis, [(i, i ^ mask) for i in range(size)])]
    pallas_call x29 -> x37, Pallas kernels: 154 us -> 171 us  [kernel_call(): pl.pallas_call(lambda *refs: staged(body, plan, refs), in_specs=specs, ou...]
    all_gather x4, waiting for transfers between devices: 27.2 us -> 40.2 us  [gather_z(): lax.all_gather(own, 'fsdp', axis=0, tiled=True, axis_index_groups=z_group...]
    reduce_scatter x8 -> x6, waiting for transfers between devices: 13.2 us -> 1.73 us  [scatter_z(): lax.psum_scatter(same, 'fsdp', scatter_dimension=0, tiled=True, axis_inde...]
    pallas_call x8 -> x2, Pallas kernels: 13 us -> 5.1 us  [assemble(): pl.pallas_call(functools.partial(assemble_kernel, column, stride), grid_s...]
  transfers between devices with their start and end apart: 106 -> 105, of which waited for: 47 -> 45; matrix products, arithmetic and copies ran while one was open for 7% -> 4% of each run, Pallas kernels for 24% -> 30%
where the time goes in v4:
time: 570 us; the launch traced here: 559 us
  Pallas kernels  189 us (33%)
  waiting for transfers between devices  182 us (32%)
  local copies, waits for them, and re-layouts  81.7 us (14%)
  starting transfers between devices  74.1 us (13%)
  between operations  17.7 us (3%)
  other arithmetic  13.9 us (2%)
    pallas_call x37, Pallas kernels, kernel_call(): pl.pallas_call(lambda *refs: staged(body, plan, refs), in_specs=specs, ou...  171 us
    ppermute x95, waiting for transfers between devices, hop(): return lax.ppermute(value, axis, [(i, i ^ mask) for i in range(size)])  140 us
    ppermute x95, starting transfers between devices, hop(): return lax.ppermute(value, axis, [(i, i ^ mask) for i in range(size)])  73.4 us
    unnamed x419, local copies, waits for them, and re-layouts  70.8 us
    all_gather x4, waiting for transfers between devices, gather_z(): lax.all_gather(own, 'fsdp', axis=0, tiled=True, axis_index_groups=z_group...  40.2 us
  transfers between devices with their start and end apart: 105, of which 45 were waited for; matrix products, arithmetic and copies ran while one was open for 4% of the time, Pallas kernels for 30%

profile of v4, /device:TPU:0, one launch (start us, length us, event | category | flops | bytes accessed | tf_op | source)
XLA Modules:
  0.0 558.6 jit_solution(4736846487924263398)
XLA Ops:
  21.5 11.4 %collective-permute-done.6 = bf16[144,768]{1,0:T(8,128)(2,1)S(1)} collective-permute-done((bf16[144,768]{1,0:T(8,128)(2,1)S(1)}, bf16[144,768]{1,0:T(8,128)(2,1)S(1)}, u32[]{:S(2)}, u32[]{:S(2)}) %collective-permute-start.6) | collective-permute-done | bytes 221216 | tf_op jit(solution)/shard_map/ppermute | solution.py:30
  32.9 5.5 collective-permute-start.8
  40.4 7.4 %collective-permute-done.8 = bf16[144,768]{1,0:T(8,128)(2,1)S(1)} collective-permute-done((bf16[144,768]{1,0:T(8,128)(2,1)S(1)}, bf16[144,768]{1,0:T(8,128)(2,1)S(1)}, u32[]{:S(2)}, u32[]{:S(2)}) %collective-permute-start.8) | collective-permute-done | bytes 221216 | tf_op jit(solution)/shard_map/ppermute | solution.py:30
  53.2 5.5 collective-permute-done.4.refs_1_.refs_5_
  75.8 11.7 %attend.2 = (bf16[1024,768]{1,0:T(8,128)(2,1)}, f32[1024,256]{1,0:T(8,128)S(1)}, bf16[256,256]{1,0:T(8,128)(2,1)S(1)}, bf16[256,256]{1,0:T(8,128)(2,1)S(1)}, bf1...) custom-call(s32[2]{0:T(128)S(1)} %pad_add_fusion.refs_0_, s32[2]{0:T(128)S(1)} %copy-done.158, ...), custom_call_target="tpu_custom_call" | custom-call | tf_op jit(solution)/shard_map/attend/pallas_call | solution.py:253
  116.5 14.7 %all-gather.9.cloned.1.call-done.refs_7_.same.refs_10_ = bf16[512,1280]{1,0:T(8,128)(2,1)} async-done(((bf16[128,1280]{1,0:T(8,128)(2,1)}), bf16[512,1280]{1,0:T(8,128)(2,1)}) %all-gather.9.cloned.1.call-update) | async-done | bytes 1310736 | tf_op jit(solution)/shard_map/all_gather | solution.py:170
  133.2 5.5 ffn.5
  142.4 6.4 %ffn.4 = (bf16[512,1024]{1,0:T(8,128)(2,1)S(1)}, bf16[512,1024]{1,0:T(8,128)(2,1)S(1)}, f32[256,1024]{1,0:T(8,128)S(1)}, bf16[256,1024]{1,0:T(8,128)(2,1)}) custom-call(s32[2]{0:T(128)S(1)} %pad_add_fusion.refs_0_, bf16[256,1024]{1,0:T(8,128)(2,1)} %get-tuple-element.478.refs_1_, bf16[256,1024]{1,0:T(8,128)(2,1)S(1)} %collective-permute-done.17.refs_2_, ...), custom_call_target="tpu_custom_call" | custom-call | tf_op jit(solution)/shard_map/ffn/pallas_call | solution.py:253
  154.2 23.4 %all-gather.11.cloned.1.call-done.refs_3_.refs_6_.refs_4_ = bf16[512,2048]{1,0:T(8,128)(2,1)} async-done(((bf16[128,2048]{1,0:T(8,128)(2,1)}), bf16[512,2048]{1,0:T(8,128)(2,1)}) %all-gather.11.cloned.1.call-update) | async-done | bytes 2097168 | tf_op jit(solution)/shard_map/all_gather | solution.py:170
  186.7 9.1 %collective-permute-done.26.refs_5_.refs_3_ = bf16[256,1024]{1,0:T(8,128)(2,1)S(1)} collective-permute-done((bf16[256,1024]{1,0:T(8,128)(2,1)S(1)}, bf16[256,1024]{1,0:T(8,128)(2,1)S(1)}, u32[]{:S(2)}, u32[]{:S(2)}) %collective-permute-start.26) | collective-permute-done | bytes 524320 | tf_op jit(solution)/shard_map/ppermute | solution.py:30
  197.7 11.1 %attend.3 = (bf16[1024,768]{1,0:T(8,128)(2,1)}, f32[1024,256]{1,0:T(8,128)S(1)}, bf16[256,256]{1,0:T(8,128)(2,1)S(1)}, bf16[256,256]{1,0:T(8,128)(2,1)S(1)}, bf1...) custom-call(s32[2]{0:T(128)S(1)} %pad_add_fusion.refs_0_, s32[2]{0:T(128)S(1)} %copy-done.159, ...), custom_call_target="tpu_custom_call" | custom-call | tf_op jit(solution)/shard_map/attend/pallas_call | solution.py:253
  226.6 5.8 %ffn.6 = (bf16[512,1024]{1,0:T(8,128)(2,1)S(1)}, bf16[512,1024]{1,0:T(8,128)(2,1)S(1)}, f32[256,1024]{1,0:T(8,128)S(1)}, bf16[256,1024]{1,0:T(8,128)(2,1)S(1)}) custom-call(s32[2]{0:T(128)S(1)} %pad_add_fusion.refs_0_, bf16[256,1024]{1,0:T(8,128)(2,1)S(1)} %get-tuple-element.393.refs_1_, bf16[256,1024]{1,0:T(8,128)(2,1)S(1)} %collective-permute-done.34.refs_2_, ...), custom_call_target="tpu_custom_call" | custom-call | tf_op jit(solution)/shard_map/ffn/pallas_call | solution.py:253
  233.4 6.4 %ffn_back.4 = (bf16[512,1024]{1,0:T(8,128)(2,1)S(1)}, f32[256,1024]{1,0:T(8,128)S(1)}, bf16[256,1024]{1,0:T(8,128)(2,1)}, f32[1,1024]{1,0:T(1,128)S(1)}) custom-call(s32[2]{0:T(128)S(1)} %pad_add_fusion.refs_0_, bf16[256,1024]{1,0:T(8,128)(2,1)S(1)} %bitcast.105, bf16[256,1024]{1,0:T(8,128)(2,1)S(1)} %copy-done.53, ...), custom_call_target="tpu_custom_call" | custom-call | tf_op jit(solution)/shard_map/ffn_back/pallas_call | solution.py:253
  242.7 5.8 %ffn.7 = (bf16[512,1024]{1,0:T(8,128)(2,1)S(1)}, bf16[512,1024]{1,0:T(8,128)(2,1)S(1)}, f32[256,1024]{1,0:T(8,128)S(1)}, bf16[256,1024]{1,0:T(8,128)(2,1)S(1)}) custom-call(s32[2]{0:T(128)S(1)} %pad_add_fusion.refs_0_, bf16[256,1024]{1,0:T(8,128)(2,1)S(1)} %collective-permute-done.33.refs_1_.refs_3_, ...), custom_call_target="tpu_custom_call" | custom-call | tf_op jit(solution)/shard_map/ffn/pallas_call | solution.py:253
  250.5 5.4 ffn_back.5
  261.3 4.4 weight_grad.6
  266.8 5.5 weight_grad.7
  273.3 4.7 out_back.2
  280.6 4.3 collective-permute-done.41.refs_6_
  290.2 15.4 %attend_back.2 = (bf16[1024,768]{1,0:T(8,128)(2,1)}, f32[256,1024]{1,0:T(8,128)S(1)}, bf16[256,1024]{1,0:T(8,128)(2,1)}, f32[256,1024]{1,0:T(8,128)S(1)}, bf16[2...) custom-call(s32[2]{0:T(128)S(1)} %pad_add_fusion.refs_0_, s32[2]{0:T(128)S(1)} %copy-done.159, f32[4]{0:T(128)S(1)} %copy-done.162, ...), custom_call_target="tpu_custom_call" | custom-call | tf_op jit(solution)/shard_map/attend_back/pallas_call | solution.py:253
  306.2 6.3 %collective-permute-done.44.refs_1_ = bf16[512,1024]{1,0:T(8,128)(2,1)S(1)} collective-permute-done((bf16[512,1024]{1,0:T(8,128)(2,1)S(1)}, bf16[512,1024]{1,0:T(8,128)(2,1)S(1)}, u32[]{:S(2)}, u32[]{:S(2)}) %collective-permute-start.44) | collective-permute-done | bytes 1048608 | tf_op jit(solution)/shard_map/ppermute | solution.py:30
  328.8 9.6 %collective-permute-done.51.refs_1_ = bf16[512,1024]{1,0:T(8,128)(2,1)} collective-permute-done((bf16[512,1024]{1,0:T(8,128)(2,1)}, bf16[512,1024]{1,0:T(8,128)(2,1)}, u32[]{:S(2)}, u32[]{:S(2)}) %collective-permute-start.51) | collective-permute-done | bytes 1048608 | tf_op jit(solution)/shard_map/ppermute | solution.py:30
  350.8 5.3 ffn_back.6
  365.0 5.6 ffn_back.7
  375.0 4.6 weight_grad.10
  381.5 5.1 weight_grad.9
  388.6 4.6 out_back.3
  414.5 16.2 %attend_back.3 = (bf16[1024,768]{1,0:T(8,128)(2,1)}, f32[256,1024]{1,0:T(8,128)S(1)}, bf16[256,1024]{1,0:T(8,128)(2,1)S(1)}, f32[256,1024]{1,0:T(8,128)S(1)}, bf...) custom-call(s32[2]{0:T(128)S(1)} %pad_add_fusion.refs_0_, s32[2]{0:T(128)S(1)} %copy-done.159, f32[4]{0:T(128)S(1)} %copy-done.162, ...), custom_call_target="tpu_custom_call" | custom-call | tf_op jit(solution)/shard_map/attend_back/pallas_call | solution.py:253
  450.3 11.7 %collective-permute-done.70.refs_1_ = bf16[512,1024]{1,0:T(8,128)(2,1)S(1)} collective-permute-done((bf16[512,1024]{1,0:T(8,128)(2,1)}, bf16[512,1024]{1,0:T(8,128)(2,1)S(1)}, u32[]{:S(2)}, u32[]{:S(2)}) %collective-permute-start.70) | collective-permute-done | bytes 1048608 | tf_op jit(solution)/shard_map/ppermute | solution.py:30
  488.4 9.9 %collective-permute-done.72.refs_1_ = bf16[512,1280]{1,0:T(8,128)(2,1)S(1)} collective-permute-done((bf16[512,1280]{1,0:T(8,128)(2,1)}, bf16[512,1280]{1,0:T(8,128)(2,1)S(1)}, u32[]{:S(2)}, u32[]{:S(2)}) %collective-permute-start.72) | collective-permute-done | bytes 1310752 | tf_op jit(solution)/shard_map/ppermute | solution.py:30
  510.7 4.4 collective-permute-done.91
  535.0 8.0 %collective-permute-done.93.refs_10_ = bf16[128,1280]{1,0:T(8,128)(2,1)S(1)} collective-permute-done((bf16[128,1280]{1,0:T(8,128)(2,1)}, bf16[128,1280]{1,0:T(8,128)(2,1)S(1)}, u32[]{:S(2)}, u32[]{:S(2)}) %collective-permute-start.93) | collective-permute-done | bytes 327712 | tf_op jit(solution)/shard_map/ppermute | solution.py:30
  (735 shorter events, 280.5 us)
Async XLA Ops:
  7.2 59.4 %all-gather.5.cloned.1.call-start = ((), (), s32[]{:S(2)}) async-start(), calls=%async_computation.6 | async-start | bytes 1966080 | tf_op jit(solution)/shard_map/all_gather | solution.py:170
  12.1 84.7 %all-gather.7.cloned.1.call-start = ((), (), s32[]{:S(2)}) async-start(), calls=%async_computation.7 | async-start | bytes 1310720 | tf_op jit(solution)/shard_map/all_gather | solution.py:170
  13.5 117.8 %all-gather.9.cloned.1.call-start = ((), (), s32[]{:S(2)}) async-start(), calls=%async_computation.8 | async-start | bytes 1638400 | tf_op jit(solution)/shard_map/all_gather | solution.py:170
  18.9 21.5 %collective-permute-start.7 = (bf16[144,768]{1,0:T(8,128)(2,1)S(1)}, bf16[144,768]{1,0:T(8,128)(2,1)S(1)}, u32[]{:S(2)}, u32[]{:S(2)}) collective-permute-start(bf16[144,768]{1,0:T(8,128)(2,1)S(1)} %pack.5), channel_id=1, source_target_pairs={{0,16},{4,20},{8,24},{12,28},{16,0},{20,4},{24,8},{28,12},{1,17},{... | collective-permute-start | bytes 663560 | tf_op jit(solution)/shard_map/ppermute | solution.py:30
  51.2 126.4 %all-gather.11.cloned.1.call-start = ((), (), s32[]{:S(2)}) async-start(), calls=%async_computation.9 | async-start | bytes 2621440 | tf_op jit(solution)/shard_map/all_gather | solution.py:170
  70.5 33.7 %collective-permute-start.14 = (bf16[512,1024]{1,0:T(8,128)(2,1)S(1)}, bf16[512,1024]{1,0:T(8,128)(2,1)}, u32[]{:S(2)}, u32[]{:S(2)}) collective-permute-start(bf16[512,1024]{1,0:T(8,128)(2,1)S(1)} %slice.191.refs_3_.refs_4_), channel_id=1, source_target_pairs={{0,4},{4,0},{8,12},{12,8},{16,20},{20,16},{24,28},{28,24},{1,5},{5... | collective-permute-start | bytes 3145736 | tf_op jit(solution)/shard_map/ppermute | solution.py:30
  92.7 314.5 %reduce-scatter.7.cloned.1.call-start = ((), (), s32[]{:S(2)}) async-start(), calls=%async_computation.10 | async-start | bytes 1310720 | tf_op jit(solution)/shard_map/reduce_scatter | solution.py:178
  104.2 27.0 %collective-permute-start.19 = (bf16[512,1024]{1,0:T(8,128)(2,1)}, bf16[512,1024]{1,0:T(8,128)(2,1)}, u32[]{:S(2)}, u32[]{:S(2)}) collective-permute-start(bf16[512,1024]{1,0:T(8,128)(2,1)} %all-gather.7.cloned.1.call-done.refs_6_), channel_id=1, source_target_pairs={{0,4},{4,0},{8,12},{12,8},{16,20},{20,16},{24,28},{28,24},{1,5},{5... | collective-permute-start | bytes 3145736 | tf_op jit(solution)/shard_map/ppermute | solution.py:30
  140.9 36.7 %collective-permute-start.24 = (bf16[512,1280]{1,0:T(8,128)(2,1)S(1)}, bf16[512,1280]{1,0:T(8,128)(2,1)}, u32[]{:S(2)}, u32[]{:S(2)}) collective-permute-start(bf16[512,1280]{1,0:T(8,128)(2,1)S(1)} %copy-done), channel_id=1, source_target_pairs={{0,4},{4,0},{8,12},{12,8},{16,20},{20,16},{24,28},{28,24},{1,5},{5... | collective-permute-start | bytes 3932168 | tf_op jit(solution)/shard_map/ppermute | solution.py:30
  151.7 25.9 %collective-permute-start.20 = (bf16[256,1024]{1,0:T(8,128)(2,1)}, bf16[256,1024]{1,0:T(8,128)(2,1)}, u32[]{:S(2)}, u32[]{:S(2)}) collective-permute-start(bf16[256,1024]{1,0:T(8,128)(2,1)} %get-tuple-element.346), channel_id=1, source_target_pairs={{0,1},{1,0},{2,3},{3,2},{4,5},{5,4},{6,7},{7,6},{8,9},{9,8},{10,11... | collective-permute-start | bytes 1572872 | tf_op jit(solution)/shard_map/ppermute | solution.py:30
  152.8 24.8 %collective-permute-start.23 = (bf16[256,1024]{1,0:T(8,128)(2,1)}, bf16[256,1024]{1,0:T(8,128)(2,1)}, u32[]{:S(2)}, u32[]{:S(2)}) collective-permute-start(bf16[256,1024]{1,0:T(8,128)(2,1)} %add_convert_fusion.5), channel_id=1, source_target_pairs={{0,2},{1,3},{2,0},{3,1},{4,6},{5,7},{6,4},{7,5},{8,10},{9,11},{10,... | collective-permute-start | bytes 1572872 | tf_op jit(solution)/shard_map/ppermute | solution.py:30
  177.6 47.6 %collective-permute-start.35 = (bf16[512,2048]{1,0:T(8,128)(2,1)}, bf16[512,2048]{1,0:T(8,128)(2,1)S(1)}, u32[]{:S(2)}, u32[]{:S(2)}) collective-permute-start(bf16[512,2048]{1,0:T(8,128)(2,1)} %all-gather.11.cloned.1.call-done.refs_3_.refs_6_.refs_4_), channel_id=1, source_target_pairs={{0,4},{4,0},{8,12},{12,8},{16,20},{20,16},{24,28},{28,24},{1,5},{5... | collective-permute-start | bytes 6291464 | tf_op jit(solution)/shard_map/ppermute | solution.py:30
  186.1 29.2 %collective-permute-start.32 = (bf16[1024,512]{1,0:T(8,128)(2,1)S(1)}, bf16[1024,512]{1,0:T(8,128)(2,1)S(1)}, u32[]{:S(2)}, u32[]{:S(2)}) collective-permute-start(bf16[1024,512]{1,0:T(8,128)(2,1)S(1)} %assemble.3.refs_5_.refs_7_), channel_id=1, source_target_pairs={{0,1},{1,0},{2,3},{3,2},{4,5},{5,4},{6,7},{7,6},{8,9},{9,8},{10,11... | collective-permute-start | bytes 3145736 | tf_op jit(solution)/shard_map/ppermute | solution.py:30
  220.7 20.0 %collective-permute-start.33 = (bf16[256,1024]{1,0:T(8,128)(2,1)S(1)}, bf16[256,1024]{1,0:T(8,128)(2,1)S(1)}, u32[]{:S(2)}, u32[]{:S(2)}) collective-permute-start(bf16[256,1024]{1,0:T(8,128)(2,1)S(1)} %get-tuple-element.393.refs_1_), channel_id=1, source_target_pairs={{0,2},{1,3},{2,0},{3,1},{4,6},{5,7},{6,4},{7,5},{8,10},{9,11},{10,... | collective-permute-start | bytes 1572872 | tf_op jit(solution)/shard_map/ppermute | solution.py:30
  286.9 25.6 %collective-permute-start.44 = (bf16[512,1024]{1,0:T(8,128)(2,1)S(1)}, bf16[512,1024]{1,0:T(8,128)(2,1)S(1)}, u32[]{:S(2)}, u32[]{:S(2)}) collective-permute-start(bf16[512,1024]{1,0:T(8,128)(2,1)S(1)} %copy-done.174), channel_id=1, source_target_pairs={{0,4},{4,0},{8,12},{12,8},{16,20},{20,16},{24,28},{28,24},{1,5},{5... | collective-permute-start | bytes 3145736 | tf_op jit(solution)/shard_map/ppermute | solution.py:30
  288.4 24.0 %collective-permute-start.45 = (bf16[256,1024]{1,0:T(8,128)(2,1)S(1)}, bf16[256,1024]{1,0:T(8,128)(2,1)S(1)}, u32[]{:S(2)}, u32[]{:S(2)}) collective-permute-start(bf16[256,1024]{1,0:T(8,128)(2,1)S(1)} %copy-done.176), channel_id=1, source_target_pairs={{0,1},{1,0},{2,3},{3,2},{4,5},{5,4},{6,7},{7,6},{8,9},{9,8},{10,11... | collective-permute-start | bytes 1572872 | tf_op jit(solution)/shard_map/ppermute | solution.py:30
  289.0 23.5 %collective-permute-start.47 = (bf16[256,1024]{1,0:T(8,128)(2,1)S(1)}, bf16[256,1024]{1,0:T(8,128)(2,1)S(1)}, u32[]{:S(2)}, u32[]{:S(2)}) collective-permute-start(bf16[256,1024]{1,0:T(8,128)(2,1)S(1)} %add_convert_fusion.3), channel_id=1, source_target_pairs={{0,2},{1,3},{2,0},{3,1},{4,6},{5,7},{6,4},{7,5},{8,10},{9,11},{10,... | collective-permute-start | bytes 1572872 | tf_op jit(solution)/shard_map/ppermute | solution.py:30
  312.6 25.9 %collective-permute-start.51 = (bf16[512,1024]{1,0:T(8,128)(2,1)}, bf16[512,1024]{1,0:T(8,128)(2,1)}, u32[]{:S(2)}, u32[]{:S(2)}) collective-permute-start(bf16[512,1024]{1,0:T(8,128)(2,1)} %get-tuple-element.433), channel_id=1, source_target_pairs={{0,4},{4,0},{8,12},{12,8},{16,20},{20,16},{24,28},{28,24},{1,5},{5... | collective-permute-start | bytes 3145736 | tf_op jit(solution)/shard_map/ppermute | solution.py:30
  314.1 24.4 %collective-permute-start.48 = (bf16[256,1024]{1,0:T(8,128)(2,1)}, bf16[256,1024]{1,0:T(8,128)(2,1)}, u32[]{:S(2)}, u32[]{:S(2)}) collective-permute-start(bf16[256,1024]{1,0:T(8,128)(2,1)} %get-tuple-element.428), channel_id=1, source_target_pairs={{0,1},{1,0},{2,3},{3,2},{4,5},{5,4},{6,7},{7,6},{8,9},{9,8},{10,11... | collective-permute-start | bytes 1572872 | tf_op jit(solution)/shard_map/ppermute | solution.py:30
  315.9 22.6 %collective-permute-start.50 = (bf16[256,1024]{1,0:T(8,128)(2,1)}, bf16[256,1024]{1,0:T(8,128)(2,1)}, u32[]{:S(2)}, u32[]{:S(2)}) collective-permute-start(bf16[256,1024]{1,0:T(8,128)(2,1)} %add_convert_fusion.2), channel_id=1, source_target_pairs={{0,2},{1,3},{2,0},{3,1},{4,6},{5,7},{6,4},{7,5},{8,10},{9,11},{10,... | collective-permute-start | bytes 1572872 | tf_op jit(solution)/shard_map/ppermute | solution.py:30
  318.5 88.7 %reduce-scatter.9.cloned.1.call-start = ((), (), s32[]{:S(2)}) async-start(), calls=%async_computation.11 | async-start | bytes 1310720 | tf_op jit(solution)/shard_map/reduce_scatter | solution.py:178
  361.7 107.8 %reduce-scatter.11.cloned.1.call-start = ((), (), s32[]{:S(2)}) async-start(), calls=%async_computation.12 | async-start | bytes 1638400 | tf_op jit(solution)/shard_map/reduce_scatter | solution.py:178
  371.8 31.1 %collective-permute-start.63 = (bf16[512,1280]{1,0:T(8,128)(2,1)S(1)}, bf16[512,1280]{1,0:T(8,128)(2,1)S(1)}, u32[]{:S(2)}, u32[]{:S(2)}) collective-permute-start(bf16[512,1280]{1,0:T(8,128)(2,1)S(1)} %copy-done.186), channel_id=1, source_target_pairs={{0,4},{4,0},{8,12},{12,8},{16,20},{20,16},{24,28},{28,24},{1,5},{5... | collective-permute-start | bytes 3932168 | tf_op jit(solution)/shard_map/ppermute | solution.py:30
  407.2 69.8 %reduce-scatter.13.cloned.1.call-start = ((), (), s32[]{:S(2)}) async-start(), calls=%async_computation.13 | async-start | bytes 1310720 | tf_op jit(solution)/shard_map/reduce_scatter | solution.py:178
  407.3 24.5 %collective-permute-start.64 = (bf16[512,1024]{1,0:T(8,128)(2,1)}, bf16[512,1024]{1,0:T(8,128)(2,1)S(1)}, u32[]{:S(2)}, u32[]{:S(2)}) collective-permute-start(bf16[512,1024]{1,0:T(8,128)(2,1)} %copy-done.172), channel_id=1, source_target_pairs={{0,4},{4,0},{8,12},{12,8},{16,20},{20,16},{24,28},{28,24},{1,5},{5... | collective-permute-start | bytes 3145736 | tf_op jit(solution)/shard_map/ppermute | solution.py:30
  408.8 23.0 %collective-permute-start.65 = (bf16[128,1024]{1,0:T(8,128)(2,1)}, bf16[128,1024]{1,0:T(8,128)(2,1)S(1)}, u32[]{:S(2)}, u32[]{:S(2)}) collective-permute-start(bf16[128,1024]{1,0:T(8,128)(2,1)} %reduce-scatter.7.cloned.1.call-done.refs_0_), channel_id=1, source_target_pairs={{0,2},{1,3},{2,0},{3,1},{4,6},{5,7},{6,4},{7,5},{8,10},{9,11},{10,... | collective-permute-start | bytes 786440 | tf_op jit(solution)/shard_map/ppermute | solution.py:30
  409.7 22.1 %collective-permute-start.66 = (bf16[128,1024]{1,0:T(8,128)(2,1)}, bf16[128,1024]{1,0:T(8,128)(2,1)S(1)}, u32[]{:S(2)}, u32[]{:S(2)}) collective-permute-start(bf16[128,1024]{1,0:T(8,128)(2,1)} %reduce-scatter.9.cloned.1.call-done.refs_4_), channel_id=1, source_target_pairs={{0,2},{1,3},{2,0},{3,1},{4,6},{5,7},{6,4},{7,5},{8,10},{9,11},{10,... | collective-permute-start | bytes 786440 | tf_op jit(solution)/shard_map/ppermute | solution.py:30
  436.5 63.5 %reduce-scatter.15.cloned.1.call-start = ((), (), s32[]{:S(2)}) async-start(), calls=%async_computation.14 | async-start | bytes 1310720 | tf_op jit(solution)/shard_map/reduce_scatter | solution.py:178
  436.5 25.5 %collective-permute-start.70 = (bf16[512,1024]{1,0:T(8,128)(2,1)}, bf16[512,1024]{1,0:T(8,128)(2,1)S(1)}, u32[]{:S(2)}, u32[]{:S(2)}) collective-permute-start(bf16[512,1024]{1,0:T(8,128)(2,1)} %copy-done.171), channel_id=1, source_target_pairs={{0,4},{4,0},{8,12},{12,8},{16,20},{20,16},{24,28},{28,24},{1,5},{5... | collective-permute-start | bytes 3145736 | tf_op jit(solution)/shard_map/ppermute | solution.py:30
  443.7 21.4 %collective-permute-start.71 = (bf16[2,512,512]{2,1,0:T(8,128)(2,1)}, bf16[2,512,512]{2,1,0:T(8,128)(2,1)}, u32[]{:S(2)}, u32[]{:S(2)}) collective-permute-start(bf16[2,512,512]{2,1,0:T(8,128)(2,1)} %get-tuple-element.535), channel_id=1, source_target_pairs={{0,1},{1,0},{2,3},{3,2},{4,5},{5,4},{6,7},{7,6},{8,9},{9,8},{10,11... | collective-permute-start | bytes 3145736 | tf_op jit(solution)/shard_map/ppermute | solution.py:30
  465.0 68.6 %reduce-scatter.17.cloned.1.call-start = ((), (), s32[]{:S(2)}) async-start(), calls=%async_computation.15 | async-start | bytes 1638400 | tf_op jit(solution)/shard_map/reduce_scatter | solution.py:178
  468.0 30.3 %collective-permute-start.72 = (bf16[512,1280]{1,0:T(8,128)(2,1)}, bf16[512,1280]{1,0:T(8,128)(2,1)S(1)}, u32[]{:S(2)}, u32[]{:S(2)}) collective-permute-start(bf16[512,1280]{1,0:T(8,128)(2,1)} %pad_maximum_fusion.3), channel_id=1, source_target_pairs={{0,4},{4,0},{8,12},{12,8},{16,20},{20,16},{24,28},{28,24},{1,5},{5... | collective-permute-start | bytes 3932168 | tf_op jit(solution)/shard_map/ppermute | solution.py:30
  (271 other events, 1925.0 us)
Sparse Core Ops, SparseCore 0:
  12.2 54.3 all-gather.4
  68.7 28.0 all-gather.6
  99.0 32.1 all-gather.8
  132.6 44.9 all-gather.10
  318.6 28.4 reduce-scatter.6
  361.8 28.8 reduce-scatter.8
  407.4 32.6 reduce-scatter.10
  442.9 25.9 reduce-scatter.12
  471.3 25.7 reduce-scatter.14
  500.1 33.4 reduce-scatter.16

commit v5 on v4

--- a/solution.py
+++ b/solution.py
@@ -440,7 +440,7 @@
 def weight_grad_kernel(count, parts, scalars, *refs):
     x = scalars[1]
     lefts, rights = refs[: parts[0]], refs[parts[0] : parts[0] + parts[1]]
-    same, *others, left, right, total = refs[parts[0] + parts[1] :]
+    *outs, left, right, total = refs[parts[0] + parts[1] :]
     for sources, target in ((lefts, left), (rights, right)):
         start = 0
         for source in sources:
@@ -448,19 +448,21 @@
             start += source.shape[0]
     total[...] = tn(left[...], right[...]).astype(BF)
     rows = total.shape[0] // count
-    each = count // 2 // len(others)
-    for r in range(count):
-        start = pl.multiple_of((r ^ x) * rows, rows)
-        target = others[r // 2 // each] if r % 2 else same
-        slot = r // 2 % each if r % 2 else r // 2
-        target[slot * rows : (slot + 1) * rows, :] = total[pl.ds(start, rows), :]
-
-
-def weight_grad(lefts, rights, place, cuts):
+    first = 0
+    for same, other in zip(outs[::2], outs[1::2]):
+        columns = slice(first, first + same.shape[1])
+        first += same.shape[1]
+        for r in range(count):
+            start = pl.multiple_of((r ^ x) * rows, rows)
+            target = other if r % 2 else same
+            target[r // 2 * rows : (r // 2 + 1) * rows, :] = total[pl.ds(start, rows), columns]
+
+
+def weight_grad(lefts, rights, place, cuts=()):
     count = lax.axis_size("fsdp")
     total = sum(item.shape[0] for item in lefts)
     tall, wide = lefts[0].shape[1], rights[0].shape[1]
-    outs = [((tall // 2, wide), BF)] + [((tall // 2 // cuts, wide), BF)] * cuts
+    outs = [((tall // 2, size), BF) for size in cuts or (wide,) for _ in range(2)]
     scratch = [
         pltpu.VMEM((total, tall), BF),
         pltpu.VMEM((total, wide), BF),
@@ -501,17 +503,22 @@
     for number in range(layout[-1]):
         groups.append(refs[4 * number : 4 * number + 4])
     refs = refs[4 * layout[-1] + aliased :]
-    qkv, out, up, down = refs
-    part, width = out.shape[1], out.shape[2]
-    mine, half, size = width // 4, width // 2, up.shape[2] // 4
+    names = layout[1]
+    outs = dict(zip(names, refs))
+    part = groups[0][0].shape[0]
+    width = part * slots
+    mine, half, size = width // 4, width // 2, width
     piece = size // slots
     (q_group, q_start), (o_group, o_start), (u_group, u_start), (d_group, d_start) = layout[0]
+    qkv, out, up, down = (outs.get(name) for name in ("qkv", "out", "up", "down"))
     for j in range(4):
         owner = run ^ j
-        for third in range(3):
+        for third in range(3 if qkv is not None else 0):
             lanes = pl.ds(pl.multiple_of(third * width + owner * mine, mine), mine)
             start = q_start + third * mine
             qkv[0, :, lanes] = groups[q_group][j][:, start : start + mine].astype(F32)
+        if up is None:
+            continue
         if piece % 128:
             lanes = pl.ds(pl.multiple_of(owner * size, size), size)
             up[0, :, lanes] = groups[u_group][j][:, u_start : u_start + size].astype(F32)
@@ -522,27 +529,30 @@
                 up[0, :, lanes] = groups[u_group][j][:, start : start + piece].astype(F32)
         rows = pl.ds(pl.multiple_of(owner * part, part), part)
         down[0, rows, :] = groups[d_group][j][:, d_start : d_start + width].astype(F32)
-    for j in range(2):
+    for j in range(2 if out is not None else 0):
         lanes = pl.ds(pl.multiple_of((run ^ j) % 2 * half, half), half)
         columns = slice(o_start, o_start + half)
         first, second = groups[o_group][j][:, columns], groups[o_group][j + 2][:, columns]
         out[0, :, lanes] = first.astype(F32) + second.astype(F32)
 
 
-def finish(layer, layers, groups, starts, place, before):
+def finish(layer, layers, groups, starts, place, before, names):
     slots = lax.axis_size("fsdp")
     part = groups[0][0].shape[0]
     width = part * slots
-    shapes = [(part, 3 * width), (part, width), (part, 4 * width), (4 * part, width)]
+    shapes = dict(
+        qkv=(part, 3 * width), out=(part, width), up=(part, 4 * width), down=(4 * part, width)
+    )
+    shapes = [shapes[name] for name in names]
     inputs = [place] + [item for group in groups for item in group]
     count = len(inputs)
     specs = [SMEM] + [VMEM] * (count - 1)
     aliases = {}
     if before is not None:
         inputs += before
-        specs += [pl.BlockSpec(memory_space=pl.ANY)] * 4
-        aliases = {count + i: i for i in range(4)}
-    layout = (starts, len(groups))
+        specs += [pl.BlockSpec(memory_space=pl.ANY)] * len(names)
+        aliases = {count + i: i for i in range(len(names))}
+    layout = (starts, names, len(groups))
     return pl.pallas_call(
         functools.partial(finish_kernel, layout, slots, len(aliases)),
         grid=(1,),
@@ -949,10 +959,11 @@
         bundle(0, ["out", "up"]),
         bundle(0, ["down"]),
         bundle(1, ["qkv", "out"]),
-        bundle(1, ["up", "down"]),
+        bundle(1, ["up"]),
+        bundle(1, ["down"]),
     ]
     keys = jnp.stack([me, me % 2]).astype(jnp.int32)
-    early_one, late_one, early_two, late_two = (gather_z(item) for item in packs)
+    early_one, late_one, early_two, up_two, down_two = (gather_z(item) for item in packs)
 
     def matrix(halves, column, size, key=1):
         return Slots(halves, column, size, part, keys, key)
@@ -999,9 +1010,9 @@
         middle, normed, att_own = out_step(scalars, parts, w_outs, stream, tables[layer])
         h2 = seq_blocks(normed)
         if top:
-            middle, moved = meet(middle, moved)
-            late_two = (late_two, moved)
-            w_up, w_down = matrix(late_two, 0, ffn_size), matrix(late_two, ffn_size, width)
+            middle, moved_late = meet(middle, moved_late)
+            w_up = matrix((up_two, moved_up), 0, ffn_size)
+            w_down = matrix((down_two, moved_late), 0, width)
             near = ffn(h2[0], h2[1], w_up, bias_up, w_down)
             near_back = ffn_back(cot_blocks[0], cot_blocks[1], near[1], w_up, w_down)
             h2[2], near, near_back = meet(h2[2], near, near_back)
@@ -1019,12 +1030,15 @@
         if top:
             last_sums = near[2:], far[2:]
         else:
-            sums, moved, late_two = meet(summed(near[2:], far[2:]), moved, late_two)
+            sums, moved, up_two = meet(summed(near[2:], far[2:]), moved, up_two)
             early_two = (early_two, moved)
             w_qkv = matrix(early_two, 0, columns)
-            moved = x_swap(late_two)
+            moved_up = x_swap(up_two)
             stream, normed = layer_end(middle, sums, tables[layer], tables[layer + 1])
             h1 = seq_blocks(normed)
+            h1[2], moved_up, down_two = meet(h1[2], moved_up, down_two)
+            h1[3] = core_swap(h1[2])
+            moved_late = x_swap(down_two)
 
     grad = cotangent[0].astype(F32)
     g_down = cot_blocks
@@ -1039,16 +1053,31 @@
             near = near_back
         else:
             near = ffn_back(g_down[0], g_down[1], act_near[1], w_up, w_down)
-            g_down[2], near, late, reduced = meet(g_down[2], near, late, reduced)
+            g_down[2], near, late, moved_above = meet(g_down[2], near, late, moved_above)
             g_down[3] = core_swap(g_down[2])
             moved_late = x_swap(late[1])
         far = ffn_back(g_down[2], g_down[3], act_far[1], w_up, w_down)
         far_low = far_sum(far[1:3])
         acts, h2, far_low = meet([act_near[0], act_far[0]], h2, far_low)
-        sent_down = weight_grad(acts, g_down, place, 1)
-        sent_up = weight_grad(h2, [near[0], far[0]], place, 1)
+        if not top:
+            far_low, up_above = meet(far_low, up_above)
+            reduced = added(up_above, moved_above)
+            upper.append(scatter_z(reduced))
+        sums = near[1], core_swap(near[2]), y_swap(far_low)
+        if top:
+            size = width * 3 // 4
+            sent_down = weight_grad(acts, g_down, place, (size, width - size))
+            size = ffn_size * 3 // 8
+            sent_up = weight_grad(h2, [near[0], far[0]], place, (size, ffn_size - size))
+            pair = zip(sent_down[2:], sent_up[:2])
+            sent_both = [jnp.concatenate(item, axis=1) for item in pair]
+            sent_down, sent_up = sent_down[:2], sent_up[2:]
+            moved_both = x_swap(sent_both[1])
+            sums, sent_both[0] = meet(sums, sent_both[0])
+        else:
+            sent_down = weight_grad(acts, g_down, place)
+            sent_up = weight_grad(h2, [near[0], far[0]], place)
         moved_down, moved_up = x_swap(sent_down[1]), x_swap(sent_up[1])
-        sums = near[1], core_swap(near[2]), y_swap(far_low)
         sums, sent_down[0], sent_up[0] = meet(sums, sent_down[0], sent_up[0])
         grad_middle, g_branch, *g_att, lines_two = out_back(
             scalars, sums, middle, grad, tables[layer], w_outs
@@ -1062,9 +1091,8 @@
         if not top:
             g_att, moved_late = meet(g_att, moved_late)
             reduced = added(late[0], moved_late)
-            g_att, reduced, upper[:2] = meet(g_att, reduced, upper[:2])
+            g_att, reduced, upper[:3] = meet(g_att, reduced, upper[:3])
             upper.append(scatter_z(reduced))
-            upper_far = [y_swap(item) for item in upper[:2]]
         if top:
             g_att, last_sums = meet(g_att, last_sums)
         g_packed, *parts, packed_sum = attend_back(
@@ -1075,35 +1103,52 @@
             parts, moved_down, last_sums = meet(parts, moved_down, last_sums)
             result = layer_end(saved[layer][6], last_sums, tables[layer], None)[1]
         else:
-            parts, moved_down, upper_far = meet(parts, moved_down, upper_far)
+            parts, moved_down = meet(parts, moved_down)
         far_low = far_sum(parts[2:])
         h1, sent_down[0], far_low = meet(h1, sent_down[0], far_low)
         if not layer:
             att_own, g_branch, far_low = meet(att_own, g_branch, far_low)
             keep, send = out_grad(att_own, g_branch, place)
-        sent_qkv = weight_grad(h1, [g_packed], place, 1)
+        sent_qkv = weight_grad(h1, [g_packed], place)
         sums = parts[0], core_swap(parts[1]), y_swap(far_low)
         reduced = added(sent_down[0], moved_down)
         totals.append(scatter_z(reduced))
-        sums, moved_up, reduced, sent_qkv[0] = meet(sums, moved_up, reduced, sent_qkv[0])
-        if not top:
+        sums, reduced, sent_qkv[0] = meet(sums, reduced, sent_qkv[0])
+        if top:
+            sums, moved_both = meet(sums, moved_both)
+        else:
+            sums, moved_up = meet(sums, moved_up)
             reduced = added(sent_up[0], moved_up)
             totals.append(scatter_z(reduced))
-            sums, upper[2] = meet(sums, upper[2])
+            sent_out = added_pair(keep, core_swap(send))
+            late = [jnp.concatenate(pair, axis=1) for pair in zip(sent_qkv, sent_out)]
+            sums, upper[3], late[0] = meet(sums, upper[3], late[0])
+            one, two, three, last_piece = upper
+            size = width // 4
+            upper = [
+                jnp.concatenate([one, two[:, :size]], axis=1),
+                jnp.concatenate([two[:, size:], three], axis=1),
+                last_piece,
+            ]
         up_sum = near[3] + far[3]
         grad, normed, lines_one = layer_begin(sums, stream, grad_middle, tables[layer])
         if layer:
-            normed, sent_up[0], att_own, g_branch = meet(normed, sent_up[0], att_own, g_branch)
+            normed, sent_both[0], sent_up[0], att_own, g_branch = meet(
+                normed, sent_both[0], sent_up[0], att_own, g_branch
+            )
+            upper.append(scatter_z(added(sent_both[0], moved_both)))
             g_down = seq_blocks(normed)
+            up_above, moved_above = sent_up[0], moved_up
             keep, send = out_grad(att_own, g_branch, place)
-            reduced = added(sent_up[0], moved_up)
-            upper.append(scatter_z(reduced))
         else:
             grad, totals[0] = meet(grad, totals[0])
-        sent_out = added_pair(keep, core_swap(send))
-        late = [jnp.concatenate(pair, axis=1) for pair in zip(sent_qkv, sent_out)]
-        if not layer:
-            last, *totals = meet(added(late[0], x_swap(late[1])), *totals)
+        if layer:
+            sent_out = added_pair(keep, core_swap(send))
+            late = [jnp.concatenate(pair, axis=1) for pair in zip(sent_qkv, sent_out)]
+        else:
+            upper = [four(item) for item in upper]
+            totals[0] = four(totals[0])
+            last, upper, totals = meet(added(late[0], x_swap(late[1])), upper, totals)
             lower = totals + [scatter_z(last)]
 
         vectors[layer] = (lines_two, lines_two, packed_sum, lines_one, up_sum)
@@ -1115,7 +1160,7 @@
         return lax.dynamic_update_slice_in_dim(jnp.zeros(shape, F32), value, run * size, axis)
 
     small_sums = []
-    vectors, upper[2], grad = meet(vectors, upper[2], grad)
+    vectors, grad = meet(vectors, grad)
     for _, lines_two, packed_sum, lines_one, up_sum in vectors:
         members = [
             lines_one[0],
@@ -1135,17 +1180,18 @@
             )
         )
 
-    own = zip(upper[:2], upper_far)
-    upper[:2] = [(item, core_swap(item), far, core_swap(far)) for item, far in own]
-    upper[2] = four(upper[2])
     starts = ((2, 0), (2, columns), (1, 0), (0, 0))
-    matrices = finish(1, LAYERS, upper, starts, place, None)
+    names = ("qkv", "out", "up", "down")
+    matrices = finish(1, LAYERS, upper, starts, place, None, names)
     vector = sum_small(jnp.stack(small_sums, axis=1))
-    early = [four(item) for item in lower[:2]]
-    last, early, matrices, vector, result = meet(lower[2], early, matrices, vector, result)
-    lower = [*early, four(last)]
-    matrices = finish(0, LAYERS, lower, starts, place, matrices)
-    grad_qkv_w, grad_out_w, grad_up_w, grad_down_w = matrices
+    middle, vector, result = meet(four(lower[1]), vector, result)
+    groups = [lower[0], middle]
+    ffn_grads = finish(0, LAYERS, groups, starts, place, list(matrices[2:]), names[2:])
+    last, ffn_grads, matrices, vector = meet(lower[2], ffn_grads, matrices[:2], vector)
+    starts = ((0, 0), (0, columns), (0, 0), (0, 0))
+    matrices = finish(0, LAYERS, [four(last)], starts, place, list(matrices), names[:2])
+    grad_qkv_w, grad_out_w = matrices
+    grad_up_w, grad_down_w = ffn_grads
     if piece % 128:
         grad_up_w = grad_up_w.reshape(LAYERS, part, 4, fsdp, piece)
         grad_up_w = jnp.swapaxes(grad_up_w, 2, 3).reshape(LAYERS, part, hidden)

time: 570 us -> 561 us (0.984)
  local copies, waits for them, and re-layouts: 81.7 us -> 69.4 us
  waiting for transfers between devices: 182 us -> 172 us
  Pallas kernels: 189 us -> 198 us
    all_gather x4 -> x5, waiting for transfers between devices: 40.2 us -> 27.8 us  [gather_z(): lax.all_gather(own, 'fsdp', axis=0, tiled=True, axis_index_groups=z_group...]
    unnamed x419 -> x423, local copies, waits for them, and re-layouts: 70.8 us -> 58.5 us
    reduce_scatter x6 -> x7, waiting for transfers between devices: 1.73 us -> 13.9 us  [scatter_z(): lax.psum_scatter(same, 'fsdp', scatter_dimension=0, tiled=True, axis_inde...]
    ppermute x95 -> x97, waiting for transfers between devices: 140 us -> 130 us  [hop(): return lax.ppermute(value, axis, [(i, i ^ mask) for i in range(size)])]
    ppermute x95 -> x97, starting transfers between devices: 73.4 us -> 78.8 us  [hop(): return lax.ppermute(value, axis, [(i, i ^ mask) for i in range(size)])]
    pallas_call x37 -> x38, Pallas kernels: 171 us -> 175 us  [kernel_call(): pl.pallas_call(lambda *refs: staged(body, plan, refs), in_specs=specs, ou...]
  transfers between devices with their start and end apart: 105 -> 109, of which waited for: 45 -> 50; matrix products, arithmetic and copies ran while one was open for 4% -> 5% of each run, Pallas kernels for 30% -> 32%
where the time goes in v5:
time: 561 us; the launch traced here: 551 us
  Pallas kernels  198 us (35%)
  waiting for transfers between devices  172 us (31%)
  starting transfers between devices  79.3 us (14%)
  local copies, waits for them, and re-layouts  69.4 us (12%)
  between operations  17.7 us (3%)
  other arithmetic  15 us (3%)
    pallas_call x38, Pallas kernels, kernel_call(): pl.pallas_call(lambda *refs: staged(body, plan, refs), in_specs=specs, ou...  175 us
    ppermute x97, waiting for transfers between devices, hop(): return lax.ppermute(value, axis, [(i, i ^ mask) for i in range(size)])  130 us
    ppermute x97, starting transfers between devices, hop(): return lax.ppermute(value, axis, [(i, i ^ mask) for i in range(size)])  78.8 us
    unnamed x423, local copies, waits for them, and re-layouts  58.5 us
    all_gather x5, waiting for transfers between devices, gather_z(): lax.all_gather(own, 'fsdp', axis=0, tiled=True, axis_index_groups=z_group...  27.8 us
    reduce_scatter x7, waiting for transfers between devices, scatter_z(): lax.psum_scatter(same, 'fsdp', scatter_dimension=0, tiled=True, axis_inde...  13.9 us
  transfers between devices with their start and end apart: 109, of which 50 were waited for; matrix products, arithmetic and copies ran while one was open for 5% of the time, Pallas kernels for 32%

profile of v5, /device:TPU:0, one launch (start us, length us, event | category | flops | bytes accessed | tf_op | source)
XLA Modules:
  0.0 550.9 jit_solution(7108435959846422296)
XLA Ops:
  21.5 11.4 %collective-permute-done.6 = bf16[144,768]{1,0:T(8,128)(2,1)S(1)} collective-permute-done((bf16[144,768]{1,0:T(8,128)(2,1)S(1)}, bf16[144,768]{1,0:T(8,128)(2,1)S(1)}, u32[]{:S(2)}, u32[]{:S(2)}) %collective-permute-start.6) | collective-permute-done | bytes 221216 | tf_op jit(solution)/shard_map/ppermute | solution.py:30
  32.9 5.5 collective-permute-start.8
  40.4 7.4 %collective-permute-done.8 = bf16[144,768]{1,0:T(8,128)(2,1)S(1)} collective-permute-done((bf16[144,768]{1,0:T(8,128)(2,1)S(1)}, bf16[144,768]{1,0:T(8,128)(2,1)S(1)}, u32[]{:S(2)}, u32[]{:S(2)}) %collective-permute-start.8) | collective-permute-done | bytes 221216 | tf_op jit(solution)/shard_map/ppermute | solution.py:30
  53.2 5.5 collective-permute-done.4.refs_1_.refs_5_
  74.8 12.5 %attend.2 = (bf16[1024,768]{1,0:T(8,128)(2,1)}, f32[1024,256]{1,0:T(8,128)S(1)}, bf16[256,256]{1,0:T(8,128)(2,1)S(1)}, bf16[256,256]{1,0:T(8,128)(2,1)S(1)}, bf1...) custom-call(s32[2]{0:T(128)S(1)} %pad_add_fusion.refs_0_, s32[2]{0:T(128)S(1)} %copy-done.156, ...), custom_call_target="tpu_custom_call" | custom-call | tf_op jit(solution)/shard_map/attend/pallas_call | solution.py:253
  99.5 4.8 collective-permute-done.14.refs_4_.refs_5_
  117.9 13.3 %all-gather.10.cloned.1.call-done.refs_7_.same.refs_10_ = bf16[512,1280]{1,0:T(8,128)(2,1)} async-done(((bf16[128,1280]{1,0:T(8,128)(2,1)}), bf16[512,1280]{1,0:T(8,128)(2,1)}) %all-gather.10.cloned.1.call-update) | async-done | bytes 1310736 | tf_op jit(solution)/shard_map/all_gather | solution.py:170
  133.2 5.9 %ffn.5 = (bf16[512,1024]{1,0:T(8,128)(2,1)S(1)}, bf16[512,1024]{1,0:T(8,128)(2,1)S(1)}, f32[256,1024]{1,0:T(8,128)S(1)}, bf16[256,1024]{1,0:T(8,128)(2,1)S(1)}) custom-call(s32[2]{0:T(128)S(1)} %pad_add_fusion.refs_0_, bf16[256,1024]{1,0:T(8,128)(2,1)S(1)} %collective-permute-done.18.refs_1_.refs_3_, ...), custom_call_target="tpu_custom_call" | custom-call | tf_op jit(solution)/shard_map/ffn/pallas_call | solution.py:253
  142.7 6.4 %ffn.4 = (bf16[512,1024]{1,0:T(8,128)(2,1)S(1)}, bf16[512,1024]{1,0:T(8,128)(2,1)S(1)}, f32[256,1024]{1,0:T(8,128)S(1)}, bf16[256,1024]{1,0:T(8,128)(2,1)}) custom-call(s32[2]{0:T(128)S(1)} %pad_add_fusion.refs_0_, bf16[256,1024]{1,0:T(8,128)(2,1)} %get-tuple-element.524.refs_1_, bf16[256,1024]{1,0:T(8,128)(2,1)S(1)} %collective-permute-done.17.refs_2_, ...), custom_call_target="tpu_custom_call" | custom-call | tf_op jit(solution)/shard_map/ffn/pallas_call | solution.py:253
  159.6 12.8 %collective-permute-done.24.refs_8_.other.refs_11_ = bf16[512,1280]{1,0:T(8,128)(2,1)} collective-permute-done((bf16[512,1280]{1,0:T(8,128)(2,1)S(1)}, bf16[512,1280]{1,0:T(8,128)(2,1)}, u32[]{:S(2)}, u32[]{:S(2)}) %collective-permute-start.24) | collective-permute-done | bytes 1310752 | tf_op jit(solution)/shard_map/ppermute | solution.py:30
  182.3 6.2 %all-gather.14.cloned.1.call-done.refs_6_ = bf16[512,1024]{1,0:T(8,128)(2,1)} async-done(((bf16[128,1024]{1,0:T(8,128)(2,1)}), bf16[512,1024]{1,0:T(8,128)(2,1)}) %all-gather.14.cloned.1.call-update) | async-done | bytes 1048592 | tf_op jit(solution)/shard_map/all_gather | solution.py:170
  191.4 6.0 %collective-permute-done.27.refs_4_.refs_5_ = bf16[512,1024]{1,0:T(8,128)(2,1)} collective-permute-done((bf16[512,1024]{1,0:T(8,128)(2,1)}, bf16[512,1024]{1,0:T(8,128)(2,1)}, u32[]{:S(2)}, u32[]{:S(2)}) %collective-permute-start.27) | collective-permute-done | bytes 1048608 | tf_op jit(solution)/shard_map/ppermute | solution.py:30
  199.5 11.9 %attend.3 = (bf16[1024,768]{1,0:T(8,128)(2,1)}, f32[1024,256]{1,0:T(8,128)S(1)}, bf16[256,256]{1,0:T(8,128)(2,1)S(1)}, bf16[256,256]{1,0:T(8,128)(2,1)S(1)}, bf1...) custom-call(s32[2]{0:T(128)S(1)} %pad_add_fusion.refs_0_, s32[2]{0:T(128)S(1)} %copy-done.157, ...), custom_call_target="tpu_custom_call" | custom-call | tf_op jit(solution)/shard_map/attend/pallas_call | solution.py:253
  226.3 5.5 %ffn.6 = (bf16[512,1024]{1,0:T(8,128)(2,1)S(1)}, bf16[512,1024]{1,0:T(8,128)(2,1)S(1)}, f32[256,1024]{1,0:T(8,128)S(1)}, bf16[256,1024]{1,0:T(8,128)(2,1)S(1)}) custom-call(s32[2]{0:T(128)S(1)} %pad_add_fusion.refs_0_, bf16[256,1024]{1,0:T(8,128)(2,1)S(1)} %get-tuple-element.428.refs_1_, bf16[256,1024]{1,0:T(8,128)(2,1)S(1)} %collective-permute-done.35.refs_2_, ...), custom_call_target="tpu_custom_call" | custom-call | tf_op jit(solution)/shard_map/ffn/pallas_call | solution.py:253
  232.8 5.9 %ffn_back.4 = (bf16[512,1024]{1,0:T(8,128)(2,1)S(1)}, f32[256,1024]{1,0:T(8,128)S(1)}, bf16[256,1024]{1,0:T(8,128)(2,1)}, f32[1,1024]{1,0:T(1,128)S(1)}) custom-call(s32[2]{0:T(128)S(1)} %pad_add_fusion.refs_0_, bf16[256,1024]{1,0:T(8,128)(2,1)S(1)} %bitcast.105, bf16[256,1024]{1,0:T(8,128)(2,1)S(1)} %copy-done.38, ...), custom_call_target="tpu_custom_call" | custom-call | tf_op jit(solution)/shard_map/ffn_back/pallas_call | solution.py:253
  240.8 5.5 ffn.7
  248.3 5.1 ffn_back.5
  258.2 4.4 weight_grad.6
  263.6 4.6 weight_grad.7
  269.9 4.6 out_back.2
  286.8 15.5 %attend_back.2 = (bf16[1024,768]{1,0:T(8,128)(2,1)}, f32[256,1024]{1,0:T(8,128)S(1)}, bf16[256,1024]{1,0:T(8,128)(2,1)}, f32[256,1024]{1,0:T(8,128)S(1)}, bf16[2...) custom-call(s32[2]{0:T(128)S(1)} %pad_add_fusion.refs_0_, s32[2]{0:T(128)S(1)} %copy-done.157, f32[4]{0:T(128)S(1)} %copy-done.161, ...), custom_call_target="tpu_custom_call" | custom-call | tf_op jit(solution)/shard_map/attend_back/pallas_call | solution.py:253
  333.1 5.1 ffn_back.6
  351.7 5.3 ffn_back.7
  366.2 4.5 weight_grad.10
  372.8 4.8 weight_grad.9
  379.6 4.6 out_back.3
  398.9 6.5 %reduce-scatter.12.cloned.1.call-done = bf16[128,640]{1,0:T(8,128)(2,1)} async-done(((bf16[512,640]{1,0:T(8,128)(2,1)}), bf16[128,640]{1,0:T(8,128)(2,1)}) %reduce-scatter.12.cloned.1.call-update) | async-done | bytes 163856 | tf_op jit(solution)/shard_map/reduce_scatter | solution.py:178
  408.8 16.4 %attend_back.3 = (bf16[1024,768]{1,0:T(8,128)(2,1)}, f32[256,1024]{1,0:T(8,128)S(1)}, bf16[256,1024]{1,0:T(8,128)(2,1)S(1)}, f32[256,1024]{1,0:T(8,128)S(1)}, bf...) custom-call(s32[2]{0:T(128)S(1)} %pad_add_fusion.refs_0_, s32[2]{0:T(128)S(1)} %copy-done.158, f32[4]{0:T(128)S(1)} %copy-done.161, ...), custom_call_target="tpu_custom_call" | custom-call | tf_op jit(solution)/shard_map/attend_back/pallas_call | solution.py:253
  478.3 13.4 %collective-permute-done.88 = f32[8,2,1536]{2,1,0:T(2,128)S(1)} collective-permute-done((f32[8,2,1536]{2,1,0:T(2,128)S(1)}, f32[8,2,1536]{2,1,0:T(2,128)S(1)}, u32[]{:S(2)}, u32[]{:S(2)}) %collective-permute-start.88) | collective-permute-done | bytes 98336 | tf_op jit(solution)/shard_map/ppermute | solution.py:30
  514.1 4.9 finish.3
  522.5 7.2 %reduce-scatter.20.cloned.1.call-done.refs_0_ = bf16[128,1280]{1,0:T(8,128)(2,1)} async-done(((bf16[512,1280]{1,0:T(8,128)(2,1)}), bf16[128,1280]{1,0:T(8,128)(2,1)}) %reduce-scatter.20.cloned.1.call-update) | async-done | bytes 327696 | tf_op jit(solution)/shard_map/reduce_scatter | solution.py:178
  531.3 8.0 %collective-permute-done.95.refs_2_ = bf16[128,1280]{1,0:T(8,128)(2,1)S(1)} collective-permute-done((bf16[128,1280]{1,0:T(8,128)(2,1)}, bf16[128,1280]{1,0:T(8,128)(2,1)S(1)}, u32[]{:S(2)}, u32[]{:S(2)}) %collective-permute-start.95) | collective-permute-done | bytes 327712 | tf_op jit(solution)/shard_map/ppermute | solution.py:30
  (759 shorter events, 291.7 us)
Async XLA Ops:
  7.2 59.4 %all-gather.6.cloned.1.call-start = ((), (), s32[]{:S(2)}) async-start(), calls=%async_computation.7 | async-start | bytes 1966080 | tf_op jit(solution)/shard_map/all_gather | solution.py:170
  12.1 84.8 %all-gather.8.cloned.1.call-start = ((), (), s32[]{:S(2)}) async-start(), calls=%async_computation.8 | async-start | bytes 1310720 | tf_op jit(solution)/shard_map/all_gather | solution.py:170
  13.5 117.8 %all-gather.10.cloned.1.call-start = ((), (), s32[]{:S(2)}) async-start(), calls=%async_computation.9 | async-start | bytes 1638400 | tf_op jit(solution)/shard_map/all_gather | solution.py:170
  18.9 21.5 %collective-permute-start.7 = (bf16[144,768]{1,0:T(8,128)(2,1)S(1)}, bf16[144,768]{1,0:T(8,128)(2,1)S(1)}, u32[]{:S(2)}, u32[]{:S(2)}) collective-permute-start(bf16[144,768]{1,0:T(8,128)(2,1)S(1)} %pack.6), channel_id=1, source_target_pairs={{0,16},{4,20},{8,24},{12,28},{16,0},{20,4},{24,8},{28,12},{1,17},{... | collective-permute-start | bytes 663560 | tf_op jit(solution)/shard_map/ppermute | solution.py:30
  39.7 19.0 %collective-permute-start.4 = (bf16[256,1024]{1,0:T(8,128)(2,1)S(1)}, bf16[256,1024]{1,0:T(8,128)(2,1)S(1)}, u32[]{:S(2)}, u32[]{:S(2)}) collective-permute-start(bf16[256,1024]{1,0:T(8,128)(2,1)S(1)} %bitcast.103), channel_id=1, source_target_pairs={{0,2},{1,3},{2,0},{3,1},{4,6},{5,7},{6,4},{7,5},{8,10},{9,11},{10,... | collective-permute-start | bytes 1572872 | tf_op jit(solution)/shard_map/ppermute | solution.py:30
  51.2 108.4 %all-gather.12.cloned.1.call-start = ((), (), s32[]{:S(2)}) async-start(), calls=%async_computation.10 | async-start | bytes 1310720 | tf_op jit(solution)/shard_map/all_gather | solution.py:170
  67.7 19.7 %collective-permute-start.10 = (bf16[512,512]{1,0:T(8,128)(2,1)S(1)}, bf16[512,512]{1,0:T(8,128)(2,1)S(1)}, u32[]{:S(2)}, u32[]{:S(2)}) collective-permute-start(bf16[512,512]{1,0:T(8,128)(2,1)S(1)} %slice.198.same), channel_id=1, source_target_pairs={{0,4},{4,0},{8,12},{12,8},{16,20},{20,16},{24,28},{28,24},{1,5},{5... | collective-permute-start | bytes 1572872 | tf_op jit(solution)/shard_map/ppermute | solution.py:30
  70.6 33.6 %collective-permute-start.14 = (bf16[512,1024]{1,0:T(8,128)(2,1)S(1)}, bf16[512,1024]{1,0:T(8,128)(2,1)}, u32[]{:S(2)}, u32[]{:S(2)}) collective-permute-start(bf16[512,1024]{1,0:T(8,128)(2,1)S(1)} %slice.199.refs_3_.refs_4_), channel_id=1, source_target_pairs={{0,4},{4,0},{8,12},{12,8},{16,20},{20,16},{24,28},{28,24},{1,5},{5... | collective-permute-start | bytes 3145736 | tf_op jit(solution)/shard_map/ppermute | solution.py:30
  104.3 27.0 %collective-permute-start.19 = (bf16[512,1024]{1,0:T(8,128)(2,1)}, bf16[512,1024]{1,0:T(8,128)(2,1)}, u32[]{:S(2)}, u32[]{:S(2)}) collective-permute-start(bf16[512,1024]{1,0:T(8,128)(2,1)} %all-gather.8.cloned.1.call-done.refs_6_), channel_id=1, source_target_pairs={{0,4},{4,0},{8,12},{12,8},{16,20},{20,16},{24,28},{28,24},{1,5},{5... | collective-permute-start | bytes 3145736 | tf_op jit(solution)/shard_map/ppermute | solution.py:30
  117.8 70.7 %all-gather.14.cloned.1.call-start = ((), (), s32[]{:S(2)}) async-start(), calls=%async_computation.11 | async-start | bytes 1310720 | tf_op jit(solution)/shard_map/all_gather | solution.py:170
  141.3 31.2 %collective-permute-start.24 = (bf16[512,1280]{1,0:T(8,128)(2,1)S(1)}, bf16[512,1280]{1,0:T(8,128)(2,1)}, u32[]{:S(2)}, u32[]{:S(2)}) collective-permute-start(bf16[512,1280]{1,0:T(8,128)(2,1)S(1)} %copy-done.1), channel_id=1, source_target_pairs={{0,4},{4,0},{8,12},{12,8},{16,20},{20,16},{24,28},{28,24},{1,5},{5... | collective-permute-start | bytes 3932168 | tf_op jit(solution)/shard_map/ppermute | solution.py:30
  153.1 19.3 %collective-permute-start.23 = (bf16[256,1024]{1,0:T(8,128)(2,1)}, bf16[256,1024]{1,0:T(8,128)(2,1)}, u32[]{:S(2)}, u32[]{:S(2)}) collective-permute-start(bf16[256,1024]{1,0:T(8,128)(2,1)} %add_convert_fusion.5), channel_id=1, source_target_pairs={{0,2},{1,3},{2,0},{3,1},{4,6},{5,7},{6,4},{7,5},{8,10},{9,11},{10,... | collective-permute-start | bytes 1572872 | tf_op jit(solution)/shard_map/ppermute | solution.py:30
  156.0 242.9 %reduce-scatter.8.cloned.1.call-start = ((), (), s32[]{:S(2)}) async-start(), calls=%async_computation.12 | async-start | bytes 983040 | tf_op jit(solution)/shard_map/reduce_scatter | solution.py:178
  172.4 24.9 %collective-permute-start.27 = (bf16[512,1024]{1,0:T(8,128)(2,1)}, bf16[512,1024]{1,0:T(8,128)(2,1)}, u32[]{:S(2)}, u32[]{:S(2)}) collective-permute-start(bf16[512,1024]{1,0:T(8,128)(2,1)} %all-gather.12.cloned.1.call-done.refs_3_.refs_4_), channel_id=1, source_target_pairs={{0,4},{4,0},{8,12},{12,8},{16,20},{20,16},{24,28},{28,24},{1,5},{5... | collective-permute-start | bytes 3145736 | tf_op jit(solution)/shard_map/ppermute | solution.py:30
  181.7 36.1 %collective-permute-start.33 = (bf16[1024,512]{1,0:T(8,128)(2,1)S(1)}, bf16[1024,512]{1,0:T(8,128)(2,1)}, u32[]{:S(2)}, u32[]{:S(2)}) collective-permute-start(bf16[1024,512]{1,0:T(8,128)(2,1)S(1)} %assemble.3.refs_5_.refs_7_), channel_id=1, source_target_pairs={{0,1},{1,0},{2,3},{3,2},{4,5},{5,4},{6,7},{7,6},{8,9},{9,8},{10,11... | collective-permute-start | bytes 3145736 | tf_op jit(solution)/shard_map/ppermute | solution.py:30
  197.4 28.5 %collective-permute-start.36 = (bf16[512,1024]{1,0:T(8,128)(2,1)}, bf16[512,1024]{1,0:T(8,128)(2,1)}, u32[]{:S(2)}, u32[]{:S(2)}) collective-permute-start(bf16[512,1024]{1,0:T(8,128)(2,1)} %all-gather.14.cloned.1.call-done.refs_6_), channel_id=1, source_target_pairs={{0,4},{4,0},{8,12},{12,8},{16,20},{20,16},{24,28},{28,24},{1,5},{5... | collective-permute-start | bytes 3145736 | tf_op jit(solution)/shard_map/ppermute | solution.py:30
  283.5 20.0 %collective-permute-start.45 = (bf16[512,768]{1,0:T(8,128)(2,1)S(1)}, bf16[512,768]{1,0:T(8,128)(2,1)S(1)}, u32[]{:S(2)}, u32[]{:S(2)}) collective-permute-start(bf16[512,768]{1,0:T(8,128)(2,1)S(1)} %copy-done.180), channel_id=1, source_target_pairs={{0,4},{4,0},{8,12},{12,8},{16,20},{20,16},{24,28},{28,24},{1,5},{5... | collective-permute-start | bytes 2359304 | tf_op jit(solution)/shard_map/ppermute | solution.py:30
  285.0 18.4 %collective-permute-start.46 = (bf16[256,1024]{1,0:T(8,128)(2,1)S(1)}, bf16[256,1024]{1,0:T(8,128)(2,1)S(1)}, u32[]{:S(2)}, u32[]{:S(2)}) collective-permute-start(bf16[256,1024]{1,0:T(8,128)(2,1)S(1)} %copy-done.183), channel_id=1, source_target_pairs={{0,1},{1,0},{2,3},{3,2},{4,5},{5,4},{6,7},{7,6},{8,9},{9,8},{10,11... | collective-permute-start | bytes 1572872 | tf_op jit(solution)/shard_map/ppermute | solution.py:30
  329.7 69.2 %reduce-scatter.10.cloned.1.call-start = ((), (), s32[]{:S(2)}) async-start(), calls=%async_computation.13 | async-start | bytes 819200 | tf_op jit(solution)/shard_map/reduce_scatter | solution.py:178
  350.4 55.0 %reduce-scatter.12.cloned.1.call-start = ((), (), s32[]{:S(2)}) async-start(), calls=%async_computation.14 | async-start | bytes 819200 | tf_op jit(solution)/shard_map/reduce_scatter | solution.py:178
  359.2 31.0 %collective-permute-start.65 = (bf16[512,1280]{1,0:T(8,128)(2,1)}, bf16[512,1280]{1,0:T(8,128)(2,1)}, u32[]{:S(2)}, u32[]{:S(2)}) collective-permute-start(bf16[512,1280]{1,0:T(8,128)(2,1)} %pad_maximum_fusion.1), channel_id=1, source_target_pairs={{0,4},{4,0},{8,12},{12,8},{16,20},{20,16},{24,28},{28,24},{1,5},{5... | collective-permute-start | bytes 3932168 | tf_op jit(solution)/shard_map/ppermute | solution.py:30
  363.2 101.6 %reduce-scatter.14.cloned.1.call-start = ((), (), s32[]{:S(2)}) async-start(), calls=%async_computation.15 | async-start | bytes 1638400 | tf_op jit(solution)/shard_map/reduce_scatter | solution.py:178
  405.4 65.4 %reduce-scatter.16.cloned.1.call-start = ((), (), s32[]{:S(2)}) async-start(), calls=%async_computation.16 | async-start | bytes 1310720 | tf_op jit(solution)/shard_map/reduce_scatter | solution.py:178
  405.5 22.8 %collective-permute-start.66 = (bf16[512,1024]{1,0:T(8,128)(2,1)}, bf16[512,1024]{1,0:T(8,128)(2,1)S(1)}, u32[]{:S(2)}, u32[]{:S(2)}) collective-permute-start(bf16[512,1024]{1,0:T(8,128)(2,1)} %copy-done.178), channel_id=1, source_target_pairs={{0,4},{4,0},{8,12},{12,8},{16,20},{20,16},{24,28},{28,24},{1,5},{5... | collective-permute-start | bytes 3145736 | tf_op jit(solution)/shard_map/ppermute | solution.py:30
  432.9 64.3 %reduce-scatter.18.cloned.1.call-start = ((), (), s32[]{:S(2)}) async-start(), calls=%async_computation.17 | async-start | bytes 1310720 | tf_op jit(solution)/shard_map/reduce_scatter | solution.py:178
  432.9 25.5 %collective-permute-start.70 = (bf16[512,1024]{1,0:T(8,128)(2,1)}, bf16[512,1024]{1,0:T(8,128)(2,1)S(1)}, u32[]{:S(2)}, u32[]{:S(2)}) collective-permute-start(bf16[512,1024]{1,0:T(8,128)(2,1)} %copy-done.177), channel_id=1, source_target_pairs={{0,4},{4,0},{8,12},{12,8},{16,20},{20,16},{24,28},{28,24},{1,5},{5... | collective-permute-start | bytes 3145736 | tf_op jit(solution)/shard_map/ppermute | solution.py:30
  437.1 23.4 %collective-permute-start.71 = (bf16[2,512,512]{2,1,0:T(8,128)(2,1)}, bf16[2,512,512]{2,1,0:T(8,128)(2,1)}, u32[]{:S(2)}, u32[]{:S(2)}) collective-permute-start(bf16[2,512,512]{2,1,0:T(8,128)(2,1)} %get-tuple-element.590), channel_id=1, source_target_pairs={{0,1},{1,0},{2,3},{3,2},{4,5},{5,4},{6,7},{7,6},{8,9},{9,8},{10,11... | collective-permute-start | bytes 3145736 | tf_op jit(solution)/shard_map/ppermute | solution.py:30
  448.7 25.6 %collective-permute-start.76 = (bf16[128,1024]{1,0:T(8,128)(2,1)S(1)}, bf16[128,1024]{1,0:T(8,128)(2,1)}, u32[]{:S(2)}, u32[]{:S(2)}) collective-permute-start(bf16[128,1024]{1,0:T(8,128)(2,1)S(1)} %pad_maximum_fusion.8.refs_4_), channel_id=1, source_target_pairs={{0,1},{1,0},{2,3},{3,2},{4,5},{5,4},{6,7},{7,6},{8,9},{9,8},{10,11... | collective-permute-start | bytes 786440 | tf_op jit(solution)/shard_map/ppermute | solution.py:30
  453.4 22.5 %collective-permute-start.74 = (bf16[128,1024]{1,0:T(8,128)(2,1)S(1)}, bf16[128,1024]{1,0:T(8,128)(2,1)}, u32[]{:S(2)}, u32[]{:S(2)}) collective-permute-start(bf16[128,1024]{1,0:T(8,128)(2,1)S(1)} %pad_maximum_fusion.7.refs_0_), channel_id=1, source_target_pairs={{0,2},{1,3},{2,0},{3,1},{4,6},{5,7},{6,4},{7,5},{8,10},{9,11},{10,... | collective-permute-start | bytes 786440 | tf_op jit(solution)/shard_map/ppermute | solution.py:30
  460.4 69.4 %reduce-scatter.20.cloned.1.call-start = ((), (), s32[]{:S(2)}) async-start(), calls=%async_computation.18 | async-start | bytes 1638400 | tf_op jit(solution)/shard_map/reduce_scatter | solution.py:178
  463.2 31.0 %collective-permute-start.72 = (bf16[512,1280]{1,0:T(8,128)(2,1)}, bf16[512,1280]{1,0:T(8,128)(2,1)}, u32[]{:S(2)}, u32[]{:S(2)}) collective-permute-start(bf16[512,1280]{1,0:T(8,128)(2,1)} %pad_maximum_fusion.3), channel_id=1, source_target_pairs={{0,4},{4,0},{8,12},{12,8},{16,20},{20,16},{24,28},{28,24},{1,5},{5... | collective-permute-start | bytes 3932168 | tf_op jit(solution)/shard_map/ppermute | solution.py:30
  478.3 18.9 %collective-permute-start.82 = (bf16[128,1024]{1,0:T(8,128)(2,1)}, bf16[128,1024]{1,0:T(8,128)(2,1)}, u32[]{:S(2)}, u32[]{:S(2)}) collective-permute-start(bf16[128,1024]{1,0:T(8,128)(2,1)} %reduce-scatter.16.cloned.1.call-done.refs_0_), channel_id=1, source_target_pairs={{0,1},{1,0},{2,3},{3,2},{4,5},{5,4},{6,7},{7,6},{8,9},{9,8},{10,11... | collective-permute-start | bytes 786440 | tf_op jit(solution)/shard_map/ppermute | solution.py:30
  (278 other events, 2123.3 us)
Sparse Core Ops, SparseCore 0:
  12.2 54.3 all-gather.5
  68.7 28.0 all-gather.7
  99.0 32.1 all-gather.9
  132.6 26.9 all-gather.11
  161.0 27.4 all-gather.13
  329.8 28.4 reduce-scatter.7
  360.6 21.3 reduce-scatter.9
  384.3 21.0 reduce-scatter.11
  408.3 30.0 reduce-scatter.13
  440.6 25.9 reduce-scatter.15
  469.5 25.7 reduce-scatter.17
  497.5 32.2 reduce-scatter.19

commit v6 on v5

--- a/solution.py
+++ b/solution.py
@@ -200,11 +200,12 @@
             yield source, buffer.at[pl.ds(start, self.rows), :]
 
 
-def staged(body, plan, refs):
+def staged(body, plan, stored, refs):
     refs = list(refs)
     keys = refs.pop(0) if any(isinstance(item, Slots) for item in plan) else None
     taken = [refs.pop(0) for item in plan for _ in range(1 + isinstance(item, Slots))]
     sems = refs.pop()
+    results = [refs.pop() for _ in stored][::-1]
     places = [i for i, item in enumerate(plan) if item is not None]
     buffers = refs[len(refs) - len(places) :]
     refs = refs[: len(refs) - len(places)]
@@ -225,10 +226,23 @@
         copy.start()
     for copy in copies:
         copy.wait()
-    body(*inputs, *refs)
-
-
-def kernel_call(body, name, inputs, outputs, scratch=(), in_specs=None, cost=0):
+    first = len(copies)
+    stores = {}
+    for number, (i, result) in enumerate(zip(stored, results)):
+        stores[i] = pltpu.make_async_copy(result, refs[i], sems.at[first + number])
+        refs[i] = result
+    waiting = list(stored)
+    steps = body(*inputs, *refs)
+    for i in steps if stored and steps is not None else ():
+        stores[i].start()
+        waiting.remove(i)
+    for i in waiting:
+        stores[i].start()
+    for store in stores.values():
+        store.wait()
+
+
+def kernel_call(body, name, inputs, outputs, scratch=(), in_specs=None, cost=0, stored=()):
     plan, arrays, specs, buffers, keys = [], [], [], [], None
     count = 1
     hbm = pl.BlockSpec(memory_space=pl.ANY)
@@ -250,12 +264,14 @@
             count += 1
     if keys is not None:
         arrays, specs = [keys] + arrays, [SMEM] + specs
+    buffers += [pltpu.VMEM(*outputs[i]) for i in stored]
+    there = pl.BlockSpec(memory_space=pltpu.HBM)
     return pl.pallas_call(
-        lambda *refs: staged(body, plan, refs),
+        lambda *refs: staged(body, plan, stored, refs),
         in_specs=specs,
-        out_specs=[VMEM] * len(outputs),
+        out_specs=[there if i in stored else VMEM for i in range(len(outputs))],
         out_shape=[jax.ShapeDtypeStruct(shape, kind) for shape, kind in outputs],
-        scratch_shapes=[*scratch, *buffers, pltpu.SemaphoreType.DMA((count,))],
+        scratch_shapes=[*scratch, *buffers, pltpu.SemaphoreType.DMA((count + len(stored),))],
         compiler_params=pltpu.CompilerParams(vmem_limit_bytes=48 << 20),
         cost_estimate=pl.CostEstimate(flops=0, bytes_accessed=cost, transcendentals=0),
         name=name,
@@ -349,7 +365,8 @@
     outs = [(middle.shape, F32), (middle.shape, BF)]
     if after is None:
         return kernel_call(last_end_kernel, "last_end", (middle, *sums, table), outs)
-    return kernel_call(layer_end_kernel, "layer_end", (middle, *sums, table, after), outs)
+    inputs = (middle, *sums, table, after)
+    return kernel_call(layer_end_kernel, "layer_end", inputs, outs, stored=(0,))
 
 
 def out_kernel(
@@ -362,6 +379,7 @@
     starts = [pl.multiple_of((run ^ j) * size, size) for j in range(4)]
     for part, start in zip(parts, starts):
         attended[:, pl.ds(start, size)] = part
+    yield 2
     half = w_own.shape[1]
     for weight, place in ((w_own, core), (w_other, 1 - core)):
         total = None
@@ -371,6 +389,7 @@
         lanes = pl.ds(pl.multiple_of(place * half, half), half)
         bias = table[BIAS_OUT : BIAS_OUT + 1, lanes]
         middle[:, lanes] = stream[:, lanes] + (total + bias)
+    yield 0
     hat, _ = normalized(middle[...])
     normed[...] = (hat * row(table, GAIN_TWO) + row(table, SHIFT_TWO)).astype(BF)
 
@@ -378,7 +397,8 @@
 def out_step(scalars, parts, w_outs, stream, table):
     outs = [(stream.shape, F32), (stream.shape, BF), (stream.shape, BF)]
     inputs = (scalars, *parts, *w_outs, stream, table)
-    return kernel_call(out_kernel, "out_step", inputs, outs, in_specs=[SMEM] + [VMEM] * 8)
+    specs = [SMEM] + [VMEM] * 8
+    return kernel_call(out_kernel, "out_step", inputs, outs, in_specs=specs, stored=(0, 2))
 
 
 def ffn_kernel(a, b, w_up, bias, w_down, act, slope, keep, send, source):
@@ -391,8 +411,10 @@
     half = 0.5 + 0.5 * bent
     value = (pre * half).astype(BF)
     act[...] = value
+    yield 0
     rise = half + (0.5 * GELU) * pre * (1.0 - bent * bent) * (1.0 + 3.0 * CUBIC * square)
     slope[...] = rise.astype(BF)
+    yield 1
     total = nn(value, w_down[...])
     keep[...] = total[:rows, :]
     send[...] = total[rows:, :].astype(BF)
@@ -408,7 +430,8 @@
         ((rows, width), BF),
     ]
     scratch = [pltpu.VMEM((2 * rows, width), BF)]
-    return kernel_call(ffn_kernel, "ffn", (a, b, w_up, bias, w_down), outs, scratch)
+    inputs = (a, b, w_up, bias, w_down)
+    return kernel_call(ffn_kernel, "ffn", inputs, outs, scratch, stored=(0, 1))
 
 
 def ffn_back_kernel(a, b, slope, w_up, w_down, grad_pre, keep, send, sums, source):
@@ -698,6 +721,7 @@
     for j, rows in enumerate((a, b, c, d)):
         place = pl.ds(pl.multiple_of((run ^ j) * BLOCK, BLOCK), BLOCK)
         nat[place, :] = (nn(rows[...], w_qkv[...]) + bias[...]).astype(BF)
+    yield 0
     distances(offsets)
     for i in range(blocks):
         for pair in range(mine // 128):
@@ -841,7 +865,7 @@
     ]
     inputs = (scalars, slopes, *blocks, w_qkv, bias)
     specs = [SMEM, SMEM] + [VMEM] * 6
-    return kernel_call(attend_kernel, "attend", inputs, outs, scratch, specs)
+    return kernel_call(attend_kernel, "attend", inputs, outs, scratch, specs, stored=(0, 1))
 
 
 def attend_back(nat, parts, att, lse, w_qkv, scalars, slopes):
@@ -1091,24 +1115,23 @@
         if not top:
             g_att, moved_late = meet(g_att, moved_late)
             reduced = added(late[0], moved_late)
-            g_att, reduced, upper[:3] = meet(g_att, reduced, upper[:3])
+            g_att, reduced, upper[:2] = meet(g_att, reduced, upper[:2])
             upper.append(scatter_z(reduced))
         if top:
             g_att, last_sums = meet(g_att, last_sums)
+        keep, send = out_grad(att_own, g_branch, place)
+        send = core_swap(send)
         g_packed, *parts, packed_sum = attend_back(
             packed, g_att, attended, lse, w_qkv, scalars, slopes
         )
         if top:
             last_sums = summed(*last_sums)
-            parts, moved_down, last_sums = meet(parts, moved_down, last_sums)
+            parts, moved_down, last_sums, send = meet(parts, moved_down, last_sums, send)
             result = layer_end(saved[layer][6], last_sums, tables[layer], None)[1]
         else:
-            parts, moved_down = meet(parts, moved_down)
+            parts, moved_down, send = meet(parts, moved_down, send)
         far_low = far_sum(parts[2:])
         h1, sent_down[0], far_low = meet(h1, sent_down[0], far_low)
-        if not layer:
-            att_own, g_branch, far_low = meet(att_own, g_branch, far_low)
-            keep, send = out_grad(att_own, g_branch, place)
         sent_qkv = weight_grad(h1, [g_packed], place)
         sums = parts[0], core_swap(parts[1]), y_swap(far_low)
         reduced = added(sent_down[0], moved_down)
@@ -1120,9 +1143,9 @@
             sums, moved_up = meet(sums, moved_up)
             reduced = added(sent_up[0], moved_up)
             totals.append(scatter_z(reduced))
-            sent_out = added_pair(keep, core_swap(send))
+            sent_out = added_pair(keep, send)
             late = [jnp.concatenate(pair, axis=1) for pair in zip(sent_qkv, sent_out)]
-            sums, upper[3], late[0] = meet(sums, upper[3], late[0])
+            sums, upper[2:], late[0] = meet(sums, upper[2:], late[0])
             one, two, three, last_piece = upper
             size = width // 4
             upper = [
@@ -1133,17 +1156,16 @@
         up_sum = near[3] + far[3]
         grad, normed, lines_one = layer_begin(sums, stream, grad_middle, tables[layer])
         if layer:
-            normed, sent_both[0], sent_up[0], att_own, g_branch = meet(
-                normed, sent_both[0], sent_up[0], att_own, g_branch
+            normed, sent_both[0], sent_up[0], keep = meet(
+                normed, sent_both[0], sent_up[0], keep
             )
             upper.append(scatter_z(added(sent_both[0], moved_both)))
             g_down = seq_blocks(normed)
             up_above, moved_above = sent_up[0], moved_up
-            keep, send = out_grad(att_own, g_branch, place)
         else:
             grad, totals[0] = meet(grad, totals[0])
         if layer:
-            sent_out = added_pair(keep, core_swap(send))
+            sent_out = added_pair(keep, send)
             late = [jnp.concatenate(pair, axis=1) for pair in zip(sent_qkv, sent_out)]
         else:
             upper = [four(item) for item in upper]

time: 561 us -> 555 us (0.989); the launches traced: 551 us -> 551 us
    ppermute x97, waiting for transfers between devices: 130 us -> 137 us  [hop(): return lax.ppermute(value, axis, [(i, i ^ mask) for i in range(size)])]
    reduce_scatter x7, waiting for transfers between devices: 13.9 us -> 7.57 us  [scatter_z(): lax.psum_scatter(same, 'fsdp', scatter_dimension=0, tiled=True, axis_inde...]
    unnamed x423 -> x427, local copies, waits for them, and re-layouts: 58.5 us -> 63.3 us
  transfers between devices with their start and end apart: 109 -> 109, of which waited for: 50 -> 47; matrix products, arithmetic and copies ran while one was open for 5% -> 4% of each run, Pallas kernels for 32% -> 32%
where the time goes in v6:
time: 555 us; the launch traced here: 551 us
  Pallas kernels  196 us (35%)
  waiting for transfers between devices  170 us (31%)
  starting transfers between devices  78.4 us (14%)
  local copies, waits for them, and re-layouts  73.3 us (13%)
  between operations  17.7 us (3%)
  other arithmetic  14.5 us (3%)
    pallas_call x38, Pallas kernels, kernel_call(): pl.pallas_call(lambda *refs: staged(body, plan, stored, refs), in_specs=s...  174 us
    ppermute x97, waiting for transfers between devices, hop(): return lax.ppermute(value, axis, [(i, i ^ mask) for i in range(size)])  137 us
    ppermute x97, starting transfers between devices, hop(): return lax.ppermute(value, axis, [(i, i ^ mask) for i in range(size)])  77.3 us
    unnamed x427, local copies, waits for them, and re-layouts  63.3 us
    all_gather x5, waiting for transfers between devices, gather_z(): lax.all_gather(own, 'fsdp', axis=0, tiled=True, axis_index_groups=z_group...  25.6 us
  transfers between devices with their start and end apart: 109, of which 47 were waited for; matrix products, arithmetic and copies ran while one was open for 4% of the time, Pallas kernels for 32%

profile of v6, /device:TPU:0, one launch (start us, length us, event | category | flops | bytes accessed | tf_op | source)
XLA Modules:
  0.0 550.8 jit_solution(12313002142181286219)
XLA Ops:
  21.5 11.4 %collective-permute-done.6 = bf16[144,768]{1,0:T(8,128)(2,1)S(1)} collective-permute-done((bf16[144,768]{1,0:T(8,128)(2,1)S(1)}, bf16[144,768]{1,0:T(8,128)(2,1)S(1)}, u32[]{:S(2)}, u32[]{:S(2)}) %collective-permute-start.6) | collective-permute-done | bytes 221216 | tf_op jit(solution)/shard_map/ppermute | solution.py:30
  32.9 5.5 collective-permute-start.8
  40.4 7.4 %collective-permute-done.8 = bf16[144,768]{1,0:T(8,128)(2,1)S(1)} collective-permute-done((bf16[144,768]{1,0:T(8,128)(2,1)S(1)}, bf16[144,768]{1,0:T(8,128)(2,1)S(1)}, u32[]{:S(2)}, u32[]{:S(2)}) %collective-permute-start.8) | collective-permute-done | bytes 221216 | tf_op jit(solution)/shard_map/ppermute | solution.py:30
  53.2 5.5 %collective-permute-done.4.refs_1_.refs_5_ = bf16[256,1024]{1,0:T(8,128)(2,1)S(1)} collective-permute-done((bf16[256,1024]{1,0:T(8,128)(2,1)S(1)}, bf16[256,1024]{1,0:T(8,128)(2,1)S(1)}, u32[]{:S(2)}, u32[]{:S(2)}) %collective-permute-start.4) | collective-permute-done | bytes 524320 | tf_op jit(solution)/shard_map/ppermute | solution.py:30
  74.8 13.2 %attend.2 = (bf16[1024,768]{1,0:T(8,128)(2,1)}, f32[1024,256]{1,0:T(8,128)S(1)}, bf16[256,256]{1,0:T(8,128)(2,1)S(1)}, bf16[256,256]{1,0:T(8,128)(2,1)S(1)}, bf1...) custom-call(s32[2]{0:T(128)S(1)} %pad_add_fusion.refs_0_, s32[2]{0:T(128)S(1)} %copy-done.159, ...), custom_call_target="tpu_custom_call" | custom-call | tf_op jit(solution)/shard_map/attend/pallas_call | solution.py:269
  118.3 12.9 %all-gather.10.cloned.1.call-done.refs_7_.same.refs_10_ = bf16[512,1280]{1,0:T(8,128)(2,1)} async-done(((bf16[128,1280]{1,0:T(8,128)(2,1)}), bf16[512,1280]{1,0:T(8,128)(2,1)}) %all-gather.10.cloned.1.call-update) | async-done | bytes 1310736 | tf_op jit(solution)/shard_map/all_gather | solution.py:170
  133.2 6.5 %ffn.5 = (bf16[512,1024]{1,0:T(8,128)(2,1)S(1)}, bf16[512,1024]{1,0:T(8,128)(2,1)S(1)}, f32[256,1024]{1,0:T(8,128)S(1)}, bf16[256,1024]{1,0:T(8,128)(2,1)S(1)}) custom-call(s32[2]{0:T(128)S(1)} %pad_add_fusion.refs_0_, bf16[256,1024]{1,0:T(8,128)(2,1)S(1)} %collective-permute-done.18.refs_1_.refs_3_, ...), custom_call_target="tpu_custom_call" | custom-call | tf_op jit(solution)/shard_map/ffn/pallas_call | solution.py:269
  143.3 7.3 %ffn.4 = (bf16[512,1024]{1,0:T(8,128)(2,1)S(1)}, bf16[512,1024]{1,0:T(8,128)(2,1)S(1)}, f32[256,1024]{1,0:T(8,128)S(1)}, bf16[256,1024]{1,0:T(8,128)(2,1)}) custom-call(s32[2]{0:T(128)S(1)} %pad_add_fusion.refs_0_, bf16[256,1024]{1,0:T(8,128)(2,1)} %get-tuple-element.522.refs_1_, bf16[256,1024]{1,0:T(8,128)(2,1)S(1)} %collective-permute-done.17.refs_2_, ...), custom_call_target="tpu_custom_call" | custom-call | tf_op jit(solution)/shard_map/ffn/pallas_call | solution.py:269
  159.6 13.4 %collective-permute-done.24.refs_8_.other.refs_11_ = bf16[512,1280]{1,0:T(8,128)(2,1)} collective-permute-done((bf16[512,1280]{1,0:T(8,128)(2,1)S(1)}, bf16[512,1280]{1,0:T(8,128)(2,1)}, u32[]{:S(2)}, u32[]{:S(2)}) %collective-permute-start.24) | collective-permute-done | bytes 1310752 | tf_op jit(solution)/shard_map/ppermute | solution.py:30
  182.9 6.9 %all-gather.14.cloned.1.call-done.refs_6_ = bf16[512,1024]{1,0:T(8,128)(2,1)} async-done(((bf16[128,1024]{1,0:T(8,128)(2,1)}), bf16[512,1024]{1,0:T(8,128)(2,1)}) %all-gather.14.cloned.1.call-update) | async-done | bytes 1048592 | tf_op jit(solution)/shard_map/all_gather | solution.py:170
  192.0 5.9 %collective-permute-done.27.refs_4_.refs_5_ = bf16[512,1024]{1,0:T(8,128)(2,1)} collective-permute-done((bf16[512,1024]{1,0:T(8,128)(2,1)}, bf16[512,1024]{1,0:T(8,128)(2,1)}, u32[]{:S(2)}, u32[]{:S(2)}) %collective-permute-start.27) | collective-permute-done | bytes 1048608 | tf_op jit(solution)/shard_map/ppermute | solution.py:30
  200.0 11.9 %attend.3 = (bf16[1024,768]{1,0:T(8,128)(2,1)}, f32[1024,256]{1,0:T(8,128)S(1)}, bf16[256,256]{1,0:T(8,128)(2,1)S(1)}, bf16[256,256]{1,0:T(8,128)(2,1)S(1)}, bf1...) custom-call(s32[2]{0:T(128)S(1)} %pad_add_fusion.refs_0_, s32[2]{0:T(128)S(1)} %copy-done.160, ...), custom_call_target="tpu_custom_call" | custom-call | tf_op jit(solution)/shard_map/attend/pallas_call | solution.py:269
  227.1 6.5 %ffn.6 = (bf16[512,1024]{1,0:T(8,128)(2,1)S(1)}, bf16[512,1024]{1,0:T(8,128)(2,1)S(1)}, f32[256,1024]{1,0:T(8,128)S(1)}, bf16[256,1024]{1,0:T(8,128)(2,1)S(1)}) custom-call(s32[2]{0:T(128)S(1)} %pad_add_fusion.refs_0_, bf16[256,1024]{1,0:T(8,128)(2,1)S(1)} %get-tuple-element.426.refs_1_, bf16[256,1024]{1,0:T(8,128)(2,1)S(1)} %collective-permute-done.35.refs_2_, ...), custom_call_target="tpu_custom_call" | custom-call | tf_op jit(solution)/shard_map/ffn/pallas_call | solution.py:269
  234.6 5.9 %ffn_back.4 = (bf16[512,1024]{1,0:T(8,128)(2,1)S(1)}, f32[256,1024]{1,0:T(8,128)S(1)}, bf16[256,1024]{1,0:T(8,128)(2,1)}, f32[1,1024]{1,0:T(1,128)S(1)}) custom-call(s32[2]{0:T(128)S(1)} %pad_add_fusion.refs_0_, bf16[256,1024]{1,0:T(8,128)(2,1)S(1)} %bitcast.105, bf16[256,1024]{1,0:T(8,128)(2,1)S(1)} %copy-done.38, ...), custom_call_target="tpu_custom_call" | custom-call | tf_op jit(solution)/shard_map/ffn_back/pallas_call | solution.py:269
  242.6 6.5 %ffn.7 = (bf16[512,1024]{1,0:T(8,128)(2,1)S(1)}, bf16[512,1024]{1,0:T(8,128)(2,1)S(1)}, f32[256,1024]{1,0:T(8,128)S(1)}, bf16[256,1024]{1,0:T(8,128)(2,1)S(1)}) custom-call(s32[2]{0:T(128)S(1)} %pad_add_fusion.refs_0_, bf16[256,1024]{1,0:T(8,128)(2,1)S(1)} %collective-permute-done.34.refs_1_.refs_3_, ...), custom_call_target="tpu_custom_call" | custom-call | tf_op jit(solution)/shard_map/ffn/pallas_call | solution.py:269
  251.0 5.1 ffn_back.5
  266.3 4.6 weight_grad.7
  272.8 4.5 out_back.2
  292.6 15.9 %attend_back.2 = (bf16[1024,768]{1,0:T(8,128)(2,1)}, f32[256,1024]{1,0:T(8,128)S(1)}, bf16[256,1024]{1,0:T(8,128)(2,1)S(1)}, f32[256,1024]{1,0:T(8,128)S(1)}, bf...) custom-call(s32[2]{0:T(128)S(1)} %pad_add_fusion.refs_0_, s32[2]{0:T(128)S(1)} %copy-done.161, f32[4]{0:T(128)S(1)} %copy-done.164, ...), custom_call_target="tpu_custom_call" | custom-call | tf_op jit(solution)/shard_map/attend_back/pallas_call | solution.py:269
  324.8 6.9 %collective-permute-done.52.refs_2_ = bf16[256,1024]{1,0:T(8,128)(2,1)S(1)} collective-permute-done((bf16[256,1024]{1,0:T(8,128)(2,1)}, bf16[256,1024]{1,0:T(8,128)(2,1)S(1)}, u32[]{:S(2)}, u32[]{:S(2)}) %collective-permute-start.52) | collective-permute-done | bytes 524320 | tf_op jit(solution)/shard_map/ppermute | solution.py:30
  339.2 5.1 ffn_back.6
  353.1 5.3 ffn_back.7
  366.8 5.6 %weight_grad.10 = (bf16[512,1024]{1,0:T(8,128)(2,1)S(1)}, bf16[512,1024]{1,0:T(8,128)(2,1)}) custom-call(s32[2]{0:T(128)S(1)} %pad_add_fusion.2.place.refs_0_, bf16[256,1024]{1,0:T(8,128)(2,1)} %get-tuple-element.522.refs_1_, bf16[256,1024]{1,0:T(8,128)(2,1)S(1)} %copy-done.34, bf16[256,1024]{1,0:T(8,128)(2,1)S(1)} %copy-done.30, ...), custom_call_target="tpu_custom_call" | custom-call | tf_op jit(solution)/shard_map/weight_grad/pallas_call | solution.py:269
  373.4 4.7 weight_grad.9
  380.1 4.5 out_back.3
  402.5 16.4 %attend_back.3 = (bf16[1024,768]{1,0:T(8,128)(2,1)}, f32[256,1024]{1,0:T(8,128)S(1)}, bf16[256,1024]{1,0:T(8,128)(2,1)}, f32[256,1024]{1,0:T(8,128)S(1)}, bf16[2...) custom-call(s32[2]{0:T(128)S(1)} %pad_add_fusion.refs_0_, s32[2]{0:T(128)S(1)} %copy-done.161, f32[4]{0:T(128)S(1)} %copy-done.164, ...), custom_call_target="tpu_custom_call" | custom-call | tf_op jit(solution)/shard_map/attend_back/pallas_call | solution.py:269
  433.3 6.3 %collective-permute-done.74.refs_2_ = bf16[128,1024]{1,0:T(8,128)(2,1)} collective-permute-done((bf16[128,1024]{1,0:T(8,128)(2,1)S(1)}, bf16[128,1024]{1,0:T(8,128)(2,1)}, u32[]{:S(2)}, u32[]{:S(2)}) %collective-permute-start.74) | collective-permute-done | bytes 262176 | tf_op jit(solution)/shard_map/ppermute | solution.py:30
  472.4 10.4 %collective-permute-done.72.refs_1_ = bf16[512,1280]{1,0:T(8,128)(2,1)} collective-permute-done((bf16[512,1280]{1,0:T(8,128)(2,1)}, bf16[512,1280]{1,0:T(8,128)(2,1)}, u32[]{:S(2)}, u32[]{:S(2)}) %collective-permute-start.72) | collective-permute-done | bytes 1310752 | tf_op jit(solution)/shard_map/ppermute | solution.py:30
  499.9 6.7 %collective-permute-start.91 = (f32[2,1536]{1,0:T(2,128)S(1)}, f32[2,1536]{1,0:T(2,128)S(1)}, u32[]{:S(2)}, u32[]{:S(2)}) collective-permute-start(f32[2,1536]{1,0:T(2,128)S(1)} %get-tuple-element.669), channel_id=1, source_target_pairs={{0,8},{4,12},{8,0},{12,4},{16,24},{20,28},{24,16},{28,20},{1,9},{5... | collective-permute-start | bytes 36872 | tf_op jit(solution)/shard_map/ppermute | solution.py:30
  513.9 4.8 finish.3
  522.2 7.5 %reduce-scatter.20.cloned.1.call-done.refs_0_ = bf16[128,1280]{1,0:T(8,128)(2,1)} async-done(((bf16[512,1280]{1,0:T(8,128)(2,1)}), bf16[128,1280]{1,0:T(8,128)(2,1)}) %reduce-scatter.20.cloned.1.call-update) | async-done | bytes 327696 | tf_op jit(solution)/shard_map/reduce_scatter | solution.py:178
  531.1 8.0 %collective-permute-done.95.refs_2_ = bf16[128,1280]{1,0:T(8,128)(2,1)S(1)} collective-permute-done((bf16[128,1280]{1,0:T(8,128)(2,1)}, bf16[128,1280]{1,0:T(8,128)(2,1)S(1)}, u32[]{:S(2)}, u32[]{:S(2)}) %collective-permute-start.95) | collective-permute-done | bytes 327712 | tf_op jit(solution)/shard_map/ppermute | solution.py:30
  (763 shorter events, 284.2 us)
Async XLA Ops:
  7.2 59.4 %all-gather.6.cloned.1.call-start = ((), (), s32[]{:S(2)}) async-start(), calls=%async_computation.7 | async-start | bytes 1966080 | tf_op jit(solution)/shard_map/all_gather | solution.py:170
  12.1 84.8 %all-gather.8.cloned.1.call-start = ((), (), s32[]{:S(2)}) async-start(), calls=%async_computation.8 | async-start | bytes 1310720 | tf_op jit(solution)/shard_map/all_gather | solution.py:170
  13.5 117.8 %all-gather.10.cloned.1.call-start = ((), (), s32[]{:S(2)}) async-start(), calls=%async_computation.9 | async-start | bytes 1638400 | tf_op jit(solution)/shard_map/all_gather | solution.py:170
  18.9 21.5 %collective-permute-start.7 = (bf16[144,768]{1,0:T(8,128)(2,1)S(1)}, bf16[144,768]{1,0:T(8,128)(2,1)S(1)}, u32[]{:S(2)}, u32[]{:S(2)}) collective-permute-start(bf16[144,768]{1,0:T(8,128)(2,1)S(1)} %pack.6), channel_id=1, source_target_pairs={{0,16},{4,20},{8,24},{12,28},{16,0},{20,4},{24,8},{28,12},{1,17},{... | collective-permute-start | bytes 663560 | tf_op jit(solution)/shard_map/ppermute | solution.py:30
  51.2 108.4 %all-gather.12.cloned.1.call-start = ((), (), s32[]{:S(2)}) async-start(), calls=%async_computation.10 | async-start | bytes 1310720 | tf_op jit(solution)/shard_map/all_gather | solution.py:170
  67.7 20.3 %collective-permute-start.10 = (bf16[512,512]{1,0:T(8,128)(2,1)S(1)}, bf16[512,512]{1,0:T(8,128)(2,1)S(1)}, u32[]{:S(2)}, u32[]{:S(2)}) collective-permute-start(bf16[512,512]{1,0:T(8,128)(2,1)S(1)} %slice.198.same), channel_id=1, source_target_pairs={{0,4},{4,0},{8,12},{12,8},{16,20},{20,16},{24,28},{28,24},{1,5},{5... | collective-permute-start | bytes 1572872 | tf_op jit(solution)/shard_map/ppermute | solution.py:30
  70.6 33.6 %collective-permute-start.14 = (bf16[512,1024]{1,0:T(8,128)(2,1)S(1)}, bf16[512,1024]{1,0:T(8,128)(2,1)}, u32[]{:S(2)}, u32[]{:S(2)}) collective-permute-start(bf16[512,1024]{1,0:T(8,128)(2,1)S(1)} %slice.199.refs_3_.refs_4_), channel_id=1, source_target_pairs={{0,4},{4,0},{8,12},{12,8},{16,20},{20,16},{24,28},{28,24},{1,5},{5... | collective-permute-start | bytes 3145736 | tf_op jit(solution)/shard_map/ppermute | solution.py:30
  104.3 27.0 %collective-permute-start.19 = (bf16[512,1024]{1,0:T(8,128)(2,1)}, bf16[512,1024]{1,0:T(8,128)(2,1)}, u32[]{:S(2)}, u32[]{:S(2)}) collective-permute-start(bf16[512,1024]{1,0:T(8,128)(2,1)} %all-gather.8.cloned.1.call-done.refs_6_), channel_id=1, source_target_pairs={{0,4},{4,0},{8,12},{12,8},{16,20},{20,16},{24,28},{28,24},{1,5},{5... | collective-permute-start | bytes 3145736 | tf_op jit(solution)/shard_map/ppermute | solution.py:30
  118.0 71.8 %all-gather.14.cloned.1.call-start = ((), (), s32[]{:S(2)}) async-start(), calls=%async_computation.11 | async-start | bytes 1310720 | tf_op jit(solution)/shard_map/all_gather | solution.py:170
  141.8 31.2 %collective-permute-start.24 = (bf16[512,1280]{1,0:T(8,128)(2,1)S(1)}, bf16[512,1280]{1,0:T(8,128)(2,1)}, u32[]{:S(2)}, u32[]{:S(2)}) collective-permute-start(bf16[512,1280]{1,0:T(8,128)(2,1)S(1)} %copy-done.1), channel_id=1, source_target_pairs={{0,4},{4,0},{8,12},{12,8},{16,20},{20,16},{24,28},{28,24},{1,5},{5... | collective-permute-start | bytes 3932168 | tf_op jit(solution)/shard_map/ppermute | solution.py:30
  157.5 241.2 %reduce-scatter.8.cloned.1.call-start = ((), (), s32[]{:S(2)}) async-start(), calls=%async_computation.12 | async-start | bytes 983040 | tf_op jit(solution)/shard_map/reduce_scatter | solution.py:178
  173.0 24.9 %collective-permute-start.27 = (bf16[512,1024]{1,0:T(8,128)(2,1)}, bf16[512,1024]{1,0:T(8,128)(2,1)}, u32[]{:S(2)}, u32[]{:S(2)}) collective-permute-start(bf16[512,1024]{1,0:T(8,128)(2,1)} %all-gather.12.cloned.1.call-done.refs_3_.refs_4_), channel_id=1, source_target_pairs={{0,4},{4,0},{8,12},{12,8},{16,20},{20,16},{24,28},{28,24},{1,5},{5... | collective-permute-start | bytes 3145736 | tf_op jit(solution)/shard_map/ppermute | solution.py:30
  182.3 36.1 %collective-permute-start.33 = (bf16[1024,512]{1,0:T(8,128)(2,1)S(1)}, bf16[1024,512]{1,0:T(8,128)(2,1)}, u32[]{:S(2)}, u32[]{:S(2)}) collective-permute-start(bf16[1024,512]{1,0:T(8,128)(2,1)S(1)} %assemble.3.refs_5_.refs_7_), channel_id=1, source_target_pairs={{0,1},{1,0},{2,3},{3,2},{4,5},{5,4},{6,7},{7,6},{8,9},{9,8},{10,11... | collective-permute-start | bytes 3145736 | tf_op jit(solution)/shard_map/ppermute | solution.py:30
  197.9 28.7 %collective-permute-start.36 = (bf16[512,1024]{1,0:T(8,128)(2,1)}, bf16[512,1024]{1,0:T(8,128)(2,1)}, u32[]{:S(2)}, u32[]{:S(2)}) collective-permute-start(bf16[512,1024]{1,0:T(8,128)(2,1)} %all-gather.14.cloned.1.call-done.refs_6_), channel_id=1, source_target_pairs={{0,4},{4,0},{8,12},{12,8},{16,20},{20,16},{24,28},{28,24},{1,5},{5... | collective-permute-start | bytes 3145736 | tf_op jit(solution)/shard_map/ppermute | solution.py:30
  289.3 21.5 %collective-permute-start.49 = (bf16[2,512,512]{2,1,0:T(8,128)(2,1)S(1)}, bf16[2,512,512]{2,1,0:T(8,128)(2,1)S(1)}, u32[]{:S(2)}, u32[]{:S(2)}) collective-permute-start(bf16[2,512,512]{2,1,0:T(8,128)(2,1)S(1)} %get-tuple-element.467), channel_id=1, source_target_pairs={{0,1},{1,0},{2,3},{3,2},{4,5},{5,4},{6,7},{7,6},{8,9},{9,8},{10,11... | collective-permute-start | bytes 3145736 | tf_op jit(solution)/shard_map/ppermute | solution.py:30
  289.8 20.1 %collective-permute-start.45 = (bf16[512,768]{1,0:T(8,128)(2,1)S(1)}, bf16[512,768]{1,0:T(8,128)(2,1)S(1)}, u32[]{:S(2)}, u32[]{:S(2)}) collective-permute-start(bf16[512,768]{1,0:T(8,128)(2,1)S(1)} %copy-done.179), channel_id=1, source_target_pairs={{0,4},{4,0},{8,12},{12,8},{16,20},{20,16},{24,28},{28,24},{1,5},{5... | collective-permute-start | bytes 2359304 | tf_op jit(solution)/shard_map/ppermute | solution.py:30
  316.0 82.7 %reduce-scatter.10.cloned.1.call-start = ((), (), s32[]{:S(2)}) async-start(), calls=%async_computation.13 | async-start | bytes 819200 | tf_op jit(solution)/shard_map/reduce_scatter | solution.py:178
  318.2 29.6 %collective-permute-start.56 = (bf16[512,640]{1,0:T(8,128)(2,1)}, bf16[512,640]{1,0:T(8,128)(2,1)S(1)}, u32[]{:S(2)}, u32[]{:S(2)}) collective-permute-start(bf16[512,640]{1,0:T(8,128)(2,1)} %copy-done.180), channel_id=1, source_target_pairs={{0,4},{4,0},{8,12},{12,8},{16,20},{20,16},{24,28},{28,24},{1,5},{5... | collective-permute-start | bytes 1966088 | tf_op jit(solution)/shard_map/ppermute | solution.py:30
  351.1 107.0 %reduce-scatter.12.cloned.1.call-start = ((), (), s32[]{:S(2)}) async-start(), calls=%async_computation.14 | async-start | bytes 819200 | tf_op jit(solution)/shard_map/reduce_scatter | solution.py:178
  360.1 31.4 %collective-permute-start.65 = (bf16[512,1280]{1,0:T(8,128)(2,1)}, bf16[512,1280]{1,0:T(8,128)(2,1)}, u32[]{:S(2)}, u32[]{:S(2)}) collective-permute-start(bf16[512,1280]{1,0:T(8,128)(2,1)} %pad_maximum_fusion.1), channel_id=1, source_target_pairs={{0,4},{4,0},{8,12},{12,8},{16,20},{20,16},{24,28},{28,24},{1,5},{5... | collective-permute-start | bytes 3932168 | tf_op jit(solution)/shard_map/ppermute | solution.py:30
  364.3 93.8 %reduce-scatter.14.cloned.1.call-start = ((), (), s32[]{:S(2)}) async-start(), calls=%async_computation.15 | async-start | bytes 1638400 | tf_op jit(solution)/shard_map/reduce_scatter | solution.py:178
  398.7 69.5 %reduce-scatter.16.cloned.1.call-start = ((), (), s32[]{:S(2)}) async-start(), calls=%async_computation.16 | async-start | bytes 1310720 | tf_op jit(solution)/shard_map/reduce_scatter | solution.py:178
  398.8 24.7 %collective-permute-start.66 = (bf16[512,1024]{1,0:T(8,128)(2,1)}, bf16[512,1024]{1,0:T(8,128)(2,1)S(1)}, u32[]{:S(2)}, u32[]{:S(2)}) collective-permute-start(bf16[512,1024]{1,0:T(8,128)(2,1)} %copy-done.177), channel_id=1, source_target_pairs={{0,4},{4,0},{8,12},{12,8},{16,20},{20,16},{24,28},{28,24},{1,5},{5... | collective-permute-start | bytes 3145736 | tf_op jit(solution)/shard_map/ppermute | solution.py:30
  402.4 21.1 %collective-permute-start.67 = (bf16[2,512,512]{2,1,0:T(8,128)(2,1)S(1)}, bf16[2,512,512]{2,1,0:T(8,128)(2,1)S(1)}, u32[]{:S(2)}, u32[]{:S(2)}) collective-permute-start(bf16[2,512,512]{2,1,0:T(8,128)(2,1)S(1)} %get-tuple-element.559), channel_id=1, source_target_pairs={{0,1},{1,0},{2,3},{3,2},{4,5},{5,4},{6,7},{7,6},{8,9},{9,8},{10,11... | collective-permute-start | bytes 3145736 | tf_op jit(solution)/shard_map/ppermute | solution.py:30
  429.1 63.4 %reduce-scatter.18.cloned.1.call-start = ((), (), s32[]{:S(2)}) async-start(), calls=%async_computation.17 | async-start | bytes 1310720 | tf_op jit(solution)/shard_map/reduce_scatter | solution.py:178
  429.1 26.3 %collective-permute-start.71 = (bf16[512,1024]{1,0:T(8,128)(2,1)}, bf16[512,1024]{1,0:T(8,128)(2,1)S(1)}, u32[]{:S(2)}, u32[]{:S(2)}) collective-permute-start(bf16[512,1024]{1,0:T(8,128)(2,1)} %get-tuple-element.577), channel_id=1, source_target_pairs={{0,4},{4,0},{8,12},{12,8},{16,20},{20,16},{24,28},{28,24},{1,5},{5... | collective-permute-start | bytes 3145736 | tf_op jit(solution)/shard_map/ppermute | solution.py:30
  433.0 38.1 %collective-permute-start.73 = (bf16[128,1024]{1,0:T(8,128)(2,1)S(1)}, bf16[128,1024]{1,0:T(8,128)(2,1)}, u32[]{:S(2)}, u32[]{:S(2)}) collective-permute-start(bf16[128,1024]{1,0:T(8,128)(2,1)S(1)} %pad_maximum_fusion.7.refs_0_), channel_id=1, source_target_pairs={{0,1},{1,0},{2,3},{3,2},{4,5},{5,4},{6,7},{7,6},{8,9},{9,8},{10,11... | collective-permute-start | bytes 786440 | tf_op jit(solution)/shard_map/ppermute | solution.py:30
  439.6 31.6 %collective-permute-start.75 = (bf16[128,1024]{1,0:T(8,128)(2,1)}, bf16[128,1024]{1,0:T(8,128)(2,1)}, u32[]{:S(2)}, u32[]{:S(2)}) collective-permute-start(bf16[128,1024]{1,0:T(8,128)(2,1)} %collective-permute-done.74.refs_2_), channel_id=1, source_target_pairs={{0,1},{1,0},{2,3},{3,2},{4,5},{5,4},{6,7},{7,6},{8,9},{9,8},{10,11... | collective-permute-start | bytes 786440 | tf_op jit(solution)/shard_map/ppermute | solution.py:30
  449.5 33.3 %collective-permute-start.72 = (bf16[512,1280]{1,0:T(8,128)(2,1)}, bf16[512,1280]{1,0:T(8,128)(2,1)}, u32[]{:S(2)}, u32[]{:S(2)}) collective-permute-start(bf16[512,1280]{1,0:T(8,128)(2,1)} %pad_maximum_fusion.3), channel_id=1, source_target_pairs={{0,4},{4,0},{8,12},{12,8},{16,20},{20,16},{24,28},{28,24},{1,5},{5... | collective-permute-start | bytes 3932168 | tf_op jit(solution)/shard_map/ppermute | solution.py:30
  456.8 72.9 %reduce-scatter.20.cloned.1.call-start = ((), (), s32[]{:S(2)}) async-start(), calls=%async_computation.18 | async-start | bytes 1638400 | tf_op jit(solution)/shard_map/reduce_scatter | solution.py:178
  459.2 24.7 %collective-permute-start.77 = (bf16[128,1024]{1,0:T(8,128)(2,1)S(1)}, bf16[128,1024]{1,0:T(8,128)(2,1)}, u32[]{:S(2)}, u32[]{:S(2)}) collective-permute-start(bf16[128,1024]{1,0:T(8,128)(2,1)S(1)} %pad_maximum_fusion.8.refs_4_), channel_id=1, source_target_pairs={{0,2},{1,3},{2,0},{3,1},{4,6},{5,7},{6,4},{7,5},{8,10},{9,11},{10,... | collective-permute-start | bytes 786440 | tf_op jit(solution)/shard_map/ppermute | solution.py:30
  460.3 24.1 %collective-permute-start.80 = (bf16[128,1280]{1,0:T(8,128)(2,1)}, bf16[128,1280]{1,0:T(8,128)(2,1)}, u32[]{:S(2)}, u32[]{:S(2)}) collective-permute-start(bf16[128,1280]{1,0:T(8,128)(2,1)} %reduce-scatter.14.cloned.1.call-done.refs_8_), channel_id=1, source_target_pairs={{0,2},{1,3},{2,0},{3,1},{4,6},{5,7},{6,4},{7,5},{8,10},{9,11},{10,... | collective-permute-start | bytes 983048 | tf_op jit(solution)/shard_map/ppermute | solution.py:30
  (280 other events, 2117.8 us)
Sparse Core Ops, SparseCore 0:
  12.2 54.3 all-gather.5
  68.7 28.0 all-gather.7
  99.0 32.1 all-gather.9
  132.6 26.9 all-gather.11
  161.0 28.7 all-gather.13
  316.1 28.2 reduce-scatter.7
  351.2 27.2 reduce-scatter.9
  380.8 21.0 reduce-scatter.11
  404.8 30.2 reduce-scatter.13
  437.2 25.9 reduce-scatter.15
  466.1 25.8 reduce-scatter.17
  494.1 35.4 reduce-scatter.19

commit v7 on v6

--- a/solution.py
+++ b/solution.py
@@ -17,6 +17,7 @@
 F32 = jnp.float32
 GELU = 0.7978845608028654
 CUBIC = 0.044715
+GRANT = [24]
 VMEM = pl.BlockSpec(memory_space=pltpu.VMEM)
 SMEM = pl.BlockSpec(memory_space=pltpu.SMEM)
 
@@ -90,7 +91,7 @@
             ],
         ),
         out_shape=jax.ShapeDtypeStruct((slots * rows, width), BF),
-        compiler_params=pltpu.CompilerParams(vmem_limit_bytes=32 << 20),
+        compiler_params=pltpu.CompilerParams(vmem_limit_bytes=12 << 20),
         cost_estimate=pl.CostEstimate(flops=0, bytes_accessed=0, transcendentals=0),
         name="assemble",
     )(key, *halves)
@@ -155,7 +156,7 @@
         out_specs=VMEM,
         out_shape=jax.ShapeDtypeStruct((rows, columns), BF),
         scratch_shapes=[pltpu.SemaphoreType.DMA((min(count, 64),))],
-        compiler_params=pltpu.CompilerParams(vmem_limit_bytes=32 << 20),
+        compiler_params=pltpu.CompilerParams(vmem_limit_bytes=12 << 20),
         cost_estimate=pl.CostEstimate(flops=0, bytes_accessed=0, transcendentals=0),
         name="pack",
     )(place, *arrays)
@@ -272,7 +273,7 @@
         out_specs=[there if i in stored else VMEM for i in range(len(outputs))],
         out_shape=[jax.ShapeDtypeStruct(shape, kind) for shape, kind in outputs],
         scratch_shapes=[*scratch, *buffers, pltpu.SemaphoreType.DMA((count + len(stored),))],
-        compiler_params=pltpu.CompilerParams(vmem_limit_bytes=48 << 20),
+        compiler_params=pltpu.CompilerParams(vmem_limit_bytes=GRANT[0] << 20),
         cost_estimate=pl.CostEstimate(flops=0, bytes_accessed=cost, transcendentals=0),
         name=name,
     )(*arrays)
@@ -910,6 +911,7 @@
     down_weight,
     down_bias,
 ):
+    GRANT[0] = 24
     fsdp = lax.axis_size("fsdp")
     run = lax.axis_index("seq")
     rows, width = tokens.shape[1:]
@@ -1071,6 +1073,7 @@
     for layer in reversed(range(LAYERS)):
         top = layer + 1 == LAYERS
         totals = upper if top else lower
+        GRANT[0] = 24 if top else 48
         w_qkv, w_outs, w_up, w_down = weights[layer]
         stream, h1, packed, attended, lse, att_own, middle, h2, act_near, act_far = saved[layer]
         if top:

time: 555 us -> 551 us (level)
  Pallas kernels: 196 us -> 188 us
    pallas_call x38, Pallas kernels: 174 us -> 164 us  [kernel_call(): pl.pallas_call(lambda *refs: staged(body, plan, stored, refs), in_specs=s...]
    unnamed x427 -> x339, local copies, waits for them, and re-layouts: 63.3 us -> 64.2 us
  transfers between devices with their start and end apart: 109 -> 109, of which waited for: 47 -> 47; matrix products, arithmetic and copies ran while one was open for 4% -> 5% of each run, Pallas kernels for 32% -> 31%
where the time goes in v7:
time: 551 us; the launch traced here: 546 us
  Pallas kernels  188 us (34%)
  waiting for transfers between devices  172 us (31%)
  starting transfers between devices  76.6 us (14%)
  local copies, waits for them, and re-layouts  76.3 us (14%)
  between operations  17.2 us (3%)
  other arithmetic  15.8 us (3%)
    pallas_call x38, Pallas kernels, kernel_call(): pl.pallas_call(lambda *refs: staged(body, plan, stored, refs), in_specs=s...  164 us
    ppermute x97, waiting for transfers between devices, hop(): return lax.ppermute(value, axis, [(i, i ^ mask) for i in range(size)])  139 us
    ppermute x97, starting transfers between devices, hop(): return lax.ppermute(value, axis, [(i, i ^ mask) for i in range(size)])  75.5 us
    unnamed x339, local copies, waits for them, and re-layouts  64.2 us
    all_gather x5, waiting for transfers between devices, gather_z(): lax.all_gather(own, 'fsdp', axis=0, tiled=True, axis_index_groups=z_group...  24.5 us
  transfers between devices with their start and end apart: 109, of which 47 were waited for; matrix products, arithmetic and copies ran while one was open for 5% of the time, Pallas kernels for 31%

profile of v7, /device:TPU:0, one launch (start us, length us, event | category | flops | bytes accessed | tf_op | source)
XLA Modules:
  0.0 546.1 jit_solution(15583652229038980928)
XLA Ops:
  21.5 11.4 %collective-permute-done.6 = bf16[144,768]{1,0:T(8,128)(2,1)S(1)} collective-permute-done((bf16[144,768]{1,0:T(8,128)(2,1)S(1)}, bf16[144,768]{1,0:T(8,128)(2,1)S(1)}, u32[]{:S(2)}, u32[]{:S(2)}) %collective-permute-start.6) | collective-permute-done | bytes 221216 | tf_op jit(solution)/shard_map/ppermute | solution.py:31
  32.9 5.5 %collective-permute-start.8 = (bf16[144,768]{1,0:T(8,128)(2,1)S(1)}, bf16[144,768]{1,0:T(8,128)(2,1)S(1)}, u32[]{:S(2)}, u32[]{:S(2)}) collective-permute-start(bf16[144,768]{1,0:T(8,128)(2,1)S(1)} %pack.6), channel_id=1, source_target_pairs={{0,24},{4,28},{8,16},{12,20},{16,8},{20,12},{24,0},{28,4},{1,25},{... | collective-permute-start | bytes 663560 | tf_op jit(solution)/shard_map/ppermute | solution.py:31
  40.4 7.4 %collective-permute-done.8 = bf16[144,768]{1,0:T(8,128)(2,1)S(1)} collective-permute-done((bf16[144,768]{1,0:T(8,128)(2,1)S(1)}, bf16[144,768]{1,0:T(8,128)(2,1)S(1)}, u32[]{:S(2)}, u32[]{:S(2)}) %collective-permute-start.8) | collective-permute-done | bytes 221216 | tf_op jit(solution)/shard_map/ppermute | solution.py:31
  53.2 5.5 %collective-permute-done.4.refs_1_.refs_5_ = bf16[256,1024]{1,0:T(8,128)(2,1)S(1)} collective-permute-done((bf16[256,1024]{1,0:T(8,128)(2,1)S(1)}, bf16[256,1024]{1,0:T(8,128)(2,1)S(1)}, u32[]{:S(2)}, u32[]{:S(2)}) %collective-permute-start.4) | collective-permute-done | bytes 524320 | tf_op jit(solution)/shard_map/ppermute | solution.py:31
  74.2 12.5 %attend.2 = (bf16[1024,768]{1,0:T(8,128)(2,1)S(1)}, f32[1024,256]{1,0:T(8,128)S(1)}, bf16[256,256]{1,0:T(8,128)(2,1)S(1)}, bf16[256,256]{1,0:T(8,128)(2,1)S(1)},...) custom-call(s32[2]{0:T(128)S(1)} %pad_add_fusion.refs_0_, ...), custom_call_target="tpu_custom_call" | custom-call | tf_op jit(solution)/shard_map/attend/pallas_call | solution.py:270
  99.7 4.4 collective-permute-done.14.refs_4_.refs_5_
  107.4 4.7 out_step.2
  117.6 13.6 %all-gather.10.cloned.1.call-done.refs_7_.same.refs_10_ = bf16[512,1280]{1,0:T(8,128)(2,1)} async-done(((bf16[128,1280]{1,0:T(8,128)(2,1)}), bf16[512,1280]{1,0:T(8,128)(2,1)}) %all-gather.10.cloned.1.call-update) | async-done | bytes 1310736 | tf_op jit(solution)/shard_map/all_gather | solution.py:171
  133.4 6.0 %ffn.5 = (bf16[512,1024]{1,0:T(8,128)(2,1)S(1)}, bf16[512,1024]{1,0:T(8,128)(2,1)S(1)}, f32[256,1024]{1,0:T(8,128)S(1)}, bf16[256,1024]{1,0:T(8,128)(2,1)S(1)}) custom-call(s32[2]{0:T(128)S(1)} %pad_add_fusion.refs_0_, bf16[256,1024]{1,0:T(8,128)(2,1)} %collective-permute-done.18.refs_1_.refs_3_, ...), custom_call_target="tpu_custom_call" | custom-call | tf_op jit(solution)/shard_map/ffn/pallas_call | solution.py:270
  143.0 6.8 %ffn.4 = (bf16[512,1024]{1,0:T(8,128)(2,1)S(1)}, bf16[512,1024]{1,0:T(8,128)(2,1)S(1)}, f32[256,1024]{1,0:T(8,128)S(1)}, bf16[256,1024]{1,0:T(8,128)(2,1)}) custom-call(s32[2]{0:T(128)S(1)} %pad_add_fusion.refs_0_, bf16[256,1024]{1,0:T(8,128)(2,1)} %get-tuple-element.522.refs_1_, bf16[256,1024]{1,0:T(8,128)(2,1)S(1)} %collective-permute-done.17.refs_2_, ...), custom_call_target="tpu_custom_call" | custom-call | tf_op jit(solution)/shard_map/ffn/pallas_call | solution.py:270
  160.4 12.4 %collective-permute-done.24.refs_8_.other.refs_11_ = bf16[512,1280]{1,0:T(8,128)(2,1)} collective-permute-done((bf16[512,1280]{1,0:T(8,128)(2,1)}, bf16[512,1280]{1,0:T(8,128)(2,1)}, u32[]{:S(2)}, u32[]{:S(2)}) %collective-permute-start.24) | collective-permute-done | bytes 1310752 | tf_op jit(solution)/shard_map/ppermute | solution.py:31
  188.5 5.2 collective-permute-done.26.refs_5_.refs_3_
  193.7 4.7 collective-permute-done.27.refs_4_.refs_5_
  200.6 11.4 %attend.3 = (bf16[1024,768]{1,0:T(8,128)(2,1)S(1)}, f32[1024,256]{1,0:T(8,128)S(1)}, bf16[256,256]{1,0:T(8,128)(2,1)S(1)}, bf16[256,256]{1,0:T(8,128)(2,1)S(1)},...) custom-call(s32[2]{0:T(128)S(1)} %pad_add_fusion.refs_0_, ...), custom_call_target="tpu_custom_call" | custom-call | tf_op jit(solution)/shard_map/attend/pallas_call | solution.py:270
  214.2 4.3 collective-permute-done.31
  226.4 5.1 ffn.6
  240.7 4.9 ffn.7
  253.1 4.4 weight_grad.6
  283.8 16.1 %attend_back.2 = (bf16[1024,768]{1,0:T(8,128)(2,1)S(1)}, f32[256,1024]{1,0:T(8,128)S(1)}, bf16[256,1024]{1,0:T(8,128)(2,1)S(1)}, f32[256,1024]{1,0:T(8,128)S(1)}...) custom-call(s32[2]{0:T(128)S(1)} %pad_add_fusion.refs_0_, s32[2]{0:T(128)S(1)} %pad_add_fusion.1.refs_1_.refs_0_, ...), custom_call_target="tpu_custom_call" | custom-call | tf_op jit(solution)/shard_map/attend_back/pallas_call | solution.py:270
  315.4 8.3 %collective-permute-done.52.refs_2_ = bf16[256,1024]{1,0:T(8,128)(2,1)S(1)} collective-permute-done((bf16[256,1024]{1,0:T(8,128)(2,1)}, bf16[256,1024]{1,0:T(8,128)(2,1)S(1)}, u32[]{:S(2)}, u32[]{:S(2)}) %collective-permute-start.52) | collective-permute-done | bytes 524320 | tf_op jit(solution)/shard_map/ppermute | solution.py:31
  331.8 5.1 ffn_back.6
  346.4 5.3 ffn_back.7
  359.0 4.7 weight_grad.10
  365.7 4.7 weight_grad.9
  372.4 4.5 out_back.3
  400.4 16.4 %attend_back.3 = (bf16[1024,768]{1,0:T(8,128)(2,1)}, f32[256,1024]{1,0:T(8,128)S(1)}, bf16[256,1024]{1,0:T(8,128)(2,1)S(1)}, f32[256,1024]{1,0:T(8,128)S(1)}, bf...) custom-call(s32[2]{0:T(128)S(1)} %pad_add_fusion.refs_0_, s32[2]{0:T(128)S(1)} %pad_add_fusion.1.refs_1_.refs_0_, ...), custom_call_target="tpu_custom_call" | custom-call | tf_op jit(solution)/shard_map/attend_back/pallas_call | solution.py:270
  431.4 5.4 collective-permute-done.74.refs_2_
  470.5 8.2 %collective-permute-done.72.refs_1_ = bf16[512,1280]{1,0:T(8,128)(2,1)} collective-permute-done((bf16[512,1280]{1,0:T(8,128)(2,1)}, bf16[512,1280]{1,0:T(8,128)(2,1)}, u32[]{:S(2)}, u32[]{:S(2)}) %collective-permute-start.72) | collective-permute-done | bytes 1310752 | tf_op jit(solution)/shard_map/ppermute | solution.py:31
  495.7 5.8 %collective-permute-start.91 = (f32[2,1536]{1,0:T(2,128)S(1)}, f32[2,1536]{1,0:T(2,128)S(1)}, u32[]{:S(2)}, u32[]{:S(2)}) collective-permute-start(f32[2,1536]{1,0:T(2,128)S(1)} %get-tuple-element.669), channel_id=1, source_target_pairs={{0,8},{4,12},{8,0},{12,4},{16,24},{20,28},{24,16},{28,20},{1,9},{5... | collective-permute-start | bytes 36872 | tf_op jit(solution)/shard_map/ppermute | solution.py:31
  508.8 4.8 finish.3
  517.1 7.8 %reduce-scatter.20.cloned.1.call-done.refs_0_ = bf16[128,1280]{1,0:T(8,128)(2,1)} async-done(((bf16[512,1280]{1,0:T(8,128)(2,1)}), bf16[128,1280]{1,0:T(8,128)(2,1)}) %reduce-scatter.20.cloned.1.call-update) | async-done | bytes 327696 | tf_op jit(solution)/shard_map/reduce_scatter | solution.py:179
  526.4 8.0 %collective-permute-done.95.refs_2_ = bf16[128,1280]{1,0:T(8,128)(2,1)S(1)} collective-permute-done((bf16[128,1280]{1,0:T(8,128)(2,1)}, bf16[128,1280]{1,0:T(8,128)(2,1)S(1)}, u32[]{:S(2)}, u32[]{:S(2)}) %collective-permute-start.95) | collective-permute-done | bytes 327712 | tf_op jit(solution)/shard_map/ppermute | solution.py:31
  (674 shorter events, 293.3 us)
Async XLA Ops:
  7.2 59.4 %all-gather.6.cloned.1.call-start = ((), (), s32[]{:S(2)}) async-start(), calls=%async_computation.7 | async-start | bytes 1966080 | tf_op jit(solution)/shard_map/all_gather | solution.py:171
  12.1 84.8 %all-gather.8.cloned.1.call-start = ((), (), s32[]{:S(2)}) async-start(), calls=%async_computation.8 | async-start | bytes 1310720 | tf_op jit(solution)/shard_map/all_gather | solution.py:171
  13.5 117.8 %all-gather.10.cloned.1.call-start = ((), (), s32[]{:S(2)}) async-start(), calls=%async_computation.9 | async-start | bytes 1638400 | tf_op jit(solution)/shard_map/all_gather | solution.py:171
  18.9 21.5 %collective-permute-start.7 = (bf16[144,768]{1,0:T(8,128)(2,1)S(1)}, bf16[144,768]{1,0:T(8,128)(2,1)S(1)}, u32[]{:S(2)}, u32[]{:S(2)}) collective-permute-start(bf16[144,768]{1,0:T(8,128)(2,1)S(1)} %pack.6), channel_id=1, source_target_pairs={{0,16},{4,20},{8,24},{12,28},{16,0},{20,4},{24,8},{28,12},{1,17},{... | collective-permute-start | bytes 663560 | tf_op jit(solution)/shard_map/ppermute | solution.py:31
  51.2 108.5 %all-gather.12.cloned.1.call-start = ((), (), s32[]{:S(2)}) async-start(), calls=%async_computation.10 | async-start | bytes 1310720 | tf_op jit(solution)/shard_map/all_gather | solution.py:171
  67.7 20.0 %collective-permute-start.10 = (bf16[512,512]{1,0:T(8,128)(2,1)S(1)}, bf16[512,512]{1,0:T(8,128)(2,1)S(1)}, u32[]{:S(2)}, u32[]{:S(2)}) collective-permute-start(bf16[512,512]{1,0:T(8,128)(2,1)S(1)} %slice.198.same), channel_id=1, source_target_pairs={{0,4},{4,0},{8,12},{12,8},{16,20},{20,16},{24,28},{28,24},{1,5},{5... | collective-permute-start | bytes 1572872 | tf_op jit(solution)/shard_map/ppermute | solution.py:31
  70.6 33.6 %collective-permute-start.14 = (bf16[512,1024]{1,0:T(8,128)(2,1)S(1)}, bf16[512,1024]{1,0:T(8,128)(2,1)S(1)}, u32[]{:S(2)}, u32[]{:S(2)}) collective-permute-start(bf16[512,1024]{1,0:T(8,128)(2,1)S(1)} %slice.199.refs_3_.refs_4_), channel_id=1, source_target_pairs={{0,4},{4,0},{8,12},{12,8},{16,20},{20,16},{24,28},{28,24},{1,5},{5... | collective-permute-start | bytes 3145736 | tf_op jit(solution)/shard_map/ppermute | solution.py:31
  104.1 27.1 %collective-permute-start.19 = (bf16[512,1024]{1,0:T(8,128)(2,1)}, bf16[512,1024]{1,0:T(8,128)(2,1)}, u32[]{:S(2)}, u32[]{:S(2)}) collective-permute-start(bf16[512,1024]{1,0:T(8,128)(2,1)} %all-gather.8.cloned.1.call-done.refs_6_), channel_id=1, source_target_pairs={{0,4},{4,0},{8,12},{12,8},{16,20},{20,16},{24,28},{28,24},{1,5},{5... | collective-permute-start | bytes 3145736 | tf_op jit(solution)/shard_map/ppermute | solution.py:31
  117.3 71.1 %all-gather.14.cloned.1.call-start = ((), (), s32[]{:S(2)}) async-start(), calls=%async_computation.11 | async-start | bytes 1310720 | tf_op jit(solution)/shard_map/all_gather | solution.py:171
  141.5 31.4 %collective-permute-start.24 = (bf16[512,1280]{1,0:T(8,128)(2,1)}, bf16[512,1280]{1,0:T(8,128)(2,1)}, u32[]{:S(2)}, u32[]{:S(2)}) collective-permute-start(bf16[512,1280]{1,0:T(8,128)(2,1)} %all-gather.10.cloned.1.call-done.refs_7_.same.refs_10_), channel_id=1, source_target_pairs={{0,4},{4,0},{8,12},{12,8},{16,20},{20,16},{24,28},{28,24},{1,5},{5... | collective-permute-start | bytes 3932168 | tf_op jit(solution)/shard_map/ppermute | solution.py:31
  156.5 235.3 %reduce-scatter.8.cloned.1.call-start = ((), (), s32[]{:S(2)}) async-start(), calls=%async_computation.12 | async-start | bytes 983040 | tf_op jit(solution)/shard_map/reduce_scatter | solution.py:179
  173.6 24.8 %collective-permute-start.27 = (bf16[512,1024]{1,0:T(8,128)(2,1)}, bf16[512,1024]{1,0:T(8,128)(2,1)S(1)}, u32[]{:S(2)}, u32[]{:S(2)}) collective-permute-start(bf16[512,1024]{1,0:T(8,128)(2,1)} %all-gather.12.cloned.1.call-done.refs_3_.refs_4_), channel_id=1, source_target_pairs={{0,4},{4,0},{8,12},{12,8},{16,20},{20,16},{24,28},{28,24},{1,5},{5... | collective-permute-start | bytes 3145736 | tf_op jit(solution)/shard_map/ppermute | solution.py:31
  184.2 34.3 %collective-permute-start.33 = (bf16[1024,512]{1,0:T(8,128)(2,1)S(1)}, bf16[1024,512]{1,0:T(8,128)(2,1)}, u32[]{:S(2)}, u32[]{:S(2)}) collective-permute-start(bf16[1024,512]{1,0:T(8,128)(2,1)S(1)} %assemble.3.refs_5_.refs_7_), channel_id=1, source_target_pairs={{0,1},{1,0},{2,3},{3,2},{4,5},{5,4},{6,7},{7,6},{8,9},{9,8},{10,11... | collective-permute-start | bytes 3145736 | tf_op jit(solution)/shard_map/ppermute | solution.py:31
  198.5 27.6 %collective-permute-start.36 = (bf16[512,1024]{1,0:T(8,128)(2,1)}, bf16[512,1024]{1,0:T(8,128)(2,1)S(1)}, u32[]{:S(2)}, u32[]{:S(2)}) collective-permute-start(bf16[512,1024]{1,0:T(8,128)(2,1)} %all-gather.14.cloned.1.call-done.refs_6_), channel_id=1, source_target_pairs={{0,4},{4,0},{8,12},{12,8},{16,20},{20,16},{24,28},{28,24},{1,5},{5... | collective-permute-start | bytes 3145736 | tf_op jit(solution)/shard_map/ppermute | solution.py:31
  280.0 22.2 %collective-permute-start.49 = (bf16[2,512,512]{2,1,0:T(8,128)(2,1)S(1)}, bf16[2,512,512]{2,1,0:T(8,128)(2,1)S(1)}, u32[]{:S(2)}, u32[]{:S(2)}) collective-permute-start(bf16[2,512,512]{2,1,0:T(8,128)(2,1)S(1)} %get-tuple-element.467), channel_id=1, source_target_pairs={{0,1},{1,0},{2,3},{3,2},{4,5},{5,4},{6,7},{7,6},{8,9},{9,8},{10,11... | collective-permute-start | bytes 3145736 | tf_op jit(solution)/shard_map/ppermute | solution.py:31
  280.6 20.7 %collective-permute-start.45 = (bf16[512,768]{1,0:T(8,128)(2,1)S(1)}, bf16[512,768]{1,0:T(8,128)(2,1)S(1)}, u32[]{:S(2)}, u32[]{:S(2)}) collective-permute-start(bf16[512,768]{1,0:T(8,128)(2,1)S(1)} %get-tuple-element.460), channel_id=1, source_target_pairs={{0,4},{4,0},{8,12},{12,8},{16,20},{20,16},{24,28},{28,24},{1,5},{5... | collective-permute-start | bytes 2359304 | tf_op jit(solution)/shard_map/ppermute | solution.py:31
  307.3 84.5 %reduce-scatter.10.cloned.1.call-start = ((), (), s32[]{:S(2)}) async-start(), calls=%async_computation.13 | async-start | bytes 819200 | tf_op jit(solution)/shard_map/reduce_scatter | solution.py:179
  310.3 29.4 %collective-permute-start.56 = (bf16[512,640]{1,0:T(8,128)(2,1)}, bf16[512,640]{1,0:T(8,128)(2,1)S(1)}, u32[]{:S(2)}, u32[]{:S(2)}) collective-permute-start(bf16[512,640]{1,0:T(8,128)(2,1)} %copy-done.142), channel_id=1, source_target_pairs={{0,4},{4,0},{8,12},{12,8},{16,20},{20,16},{24,28},{28,24},{1,5},{5... | collective-permute-start | bytes 1966088 | tf_op jit(solution)/shard_map/ppermute | solution.py:31
  344.3 110.4 %reduce-scatter.12.cloned.1.call-start = ((), (), s32[]{:S(2)}) async-start(), calls=%async_computation.14 | async-start | bytes 819200 | tf_op jit(solution)/shard_map/reduce_scatter | solution.py:179
  352.7 31.4 %collective-permute-start.65 = (bf16[512,1280]{1,0:T(8,128)(2,1)}, bf16[512,1280]{1,0:T(8,128)(2,1)}, u32[]{:S(2)}, u32[]{:S(2)}) collective-permute-start(bf16[512,1280]{1,0:T(8,128)(2,1)} %pad_maximum_fusion.1), channel_id=1, source_target_pairs={{0,4},{4,0},{8,12},{12,8},{16,20},{20,16},{24,28},{28,24},{1,5},{5... | collective-permute-start | bytes 3932168 | tf_op jit(solution)/shard_map/ppermute | solution.py:31
  356.9 97.8 %reduce-scatter.14.cloned.1.call-start = ((), (), s32[]{:S(2)}) async-start(), calls=%async_computation.15 | async-start | bytes 1638400 | tf_op jit(solution)/shard_map/reduce_scatter | solution.py:179
  391.8 73.6 %reduce-scatter.16.cloned.1.call-start = ((), (), s32[]{:S(2)}) async-start(), calls=%async_computation.16 | async-start | bytes 1310720 | tf_op jit(solution)/shard_map/reduce_scatter | solution.py:179
  391.9 27.3 %collective-permute-start.66 = (bf16[512,1024]{1,0:T(8,128)(2,1)}, bf16[512,1024]{1,0:T(8,128)(2,1)S(1)}, u32[]{:S(2)}, u32[]{:S(2)}) collective-permute-start(bf16[512,1024]{1,0:T(8,128)(2,1)} %copy-done.141), channel_id=1, source_target_pairs={{0,4},{4,0},{8,12},{12,8},{16,20},{20,16},{24,28},{28,24},{1,5},{5... | collective-permute-start | bytes 3145736 | tf_op jit(solution)/shard_map/ppermute | solution.py:31
  396.7 22.4 %collective-permute-start.67 = (bf16[2,512,512]{2,1,0:T(8,128)(2,1)S(1)}, bf16[2,512,512]{2,1,0:T(8,128)(2,1)S(1)}, u32[]{:S(2)}, u32[]{:S(2)}) collective-permute-start(bf16[2,512,512]{2,1,0:T(8,128)(2,1)S(1)} %get-tuple-element.559), channel_id=1, source_target_pairs={{0,1},{1,0},{2,3},{3,2},{4,5},{5,4},{6,7},{7,6},{8,9},{9,8},{10,11... | collective-permute-start | bytes 3145736 | tf_op jit(solution)/shard_map/ppermute | solution.py:31
  424.8 63.6 %reduce-scatter.18.cloned.1.call-start = ((), (), s32[]{:S(2)}) async-start(), calls=%async_computation.17 | async-start | bytes 1310720 | tf_op jit(solution)/shard_map/reduce_scatter | solution.py:179
  424.8 26.1 %collective-permute-start.71 = (bf16[512,1024]{1,0:T(8,128)(2,1)}, bf16[512,1024]{1,0:T(8,128)(2,1)S(1)}, u32[]{:S(2)}, u32[]{:S(2)}) collective-permute-start(bf16[512,1024]{1,0:T(8,128)(2,1)} %copy-done.140), channel_id=1, source_target_pairs={{0,4},{4,0},{8,12},{12,8},{16,20},{20,16},{24,28},{28,24},{1,5},{5... | collective-permute-start | bytes 3145736 | tf_op jit(solution)/shard_map/ppermute | solution.py:31
  431.2 38.6 %collective-permute-start.73 = (bf16[128,1024]{1,0:T(8,128)(2,1)S(1)}, bf16[128,1024]{1,0:T(8,128)(2,1)}, u32[]{:S(2)}, u32[]{:S(2)}) collective-permute-start(bf16[128,1024]{1,0:T(8,128)(2,1)S(1)} %pad_maximum_fusion.7.refs_0_), channel_id=1, source_target_pairs={{0,1},{1,0},{2,3},{3,2},{4,5},{5,4},{6,7},{7,6},{8,9},{9,8},{10,11... | collective-permute-start | bytes 786440 | tf_op jit(solution)/shard_map/ppermute | solution.py:31
  436.9 33.0 %collective-permute-start.75 = (bf16[128,1024]{1,0:T(8,128)(2,1)}, bf16[128,1024]{1,0:T(8,128)(2,1)}, u32[]{:S(2)}, u32[]{:S(2)}) collective-permute-start(bf16[128,1024]{1,0:T(8,128)(2,1)} %collective-permute-done.74.refs_2_), channel_id=1, source_target_pairs={{0,1},{1,0},{2,3},{3,2},{4,5},{5,4},{6,7},{7,6},{8,9},{9,8},{10,11... | collective-permute-start | bytes 786440 | tf_op jit(solution)/shard_map/ppermute | solution.py:31
  446.7 32.0 %collective-permute-start.72 = (bf16[512,1280]{1,0:T(8,128)(2,1)}, bf16[512,1280]{1,0:T(8,128)(2,1)}, u32[]{:S(2)}, u32[]{:S(2)}) collective-permute-start(bf16[512,1280]{1,0:T(8,128)(2,1)} %pad_maximum_fusion.3), channel_id=1, source_target_pairs={{0,4},{4,0},{8,12},{12,8},{16,20},{20,16},{24,28},{28,24},{1,5},{5... | collective-permute-start | bytes 3932168 | tf_op jit(solution)/shard_map/ppermute | solution.py:31
  452.4 72.5 %reduce-scatter.20.cloned.1.call-start = ((), (), s32[]{:S(2)}) async-start(), calls=%async_computation.18 | async-start | bytes 1638400 | tf_op jit(solution)/shard_map/reduce_scatter | solution.py:179
  455.8 24.0 %collective-permute-start.77 = (bf16[128,1024]{1,0:T(8,128)(2,1)S(1)}, bf16[128,1024]{1,0:T(8,128)(2,1)}, u32[]{:S(2)}, u32[]{:S(2)}) collective-permute-start(bf16[128,1024]{1,0:T(8,128)(2,1)S(1)} %pad_maximum_fusion.8.refs_4_), channel_id=1, source_target_pairs={{0,2},{1,3},{2,0},{3,1},{4,6},{5,7},{6,4},{7,5},{8,10},{9,11},{10,... | collective-permute-start | bytes 786440 | tf_op jit(solution)/shard_map/ppermute | solution.py:31
  456.3 24.0 %collective-permute-start.80 = (bf16[128,1280]{1,0:T(8,128)(2,1)}, bf16[128,1280]{1,0:T(8,128)(2,1)}, u32[]{:S(2)}, u32[]{:S(2)}) collective-permute-start(bf16[128,1280]{1,0:T(8,128)(2,1)} %reduce-scatter.14.cloned.1.call-done.refs_8_), channel_id=1, source_target_pairs={{0,2},{1,3},{2,0},{3,1},{4,6},{5,7},{6,4},{7,5},{8,10},{9,11},{10,... | collective-permute-start | bytes 983048 | tf_op jit(solution)/shard_map/ppermute | solution.py:31
  (235 other events, 1576.6 us)
Sparse Core Ops, SparseCore 0:
  12.2 54.3 all-gather.5
  68.7 28.0 all-gather.7
  99.0 32.1 all-gather.9
  132.6 26.9 all-gather.11
  161.0 27.4 all-gather.13
  307.5 27.0 reduce-scatter.7
  344.5 25.9 reduce-scatter.9
  372.7 21.0 reduce-scatter.11
  396.7 30.3 reduce-scatter.13
  429.3 26.9 reduce-scatter.15
  459.3 25.7 reduce-scatter.17
  488.5 36.3 reduce-scatter.19
